TPU v7x, 32 devices: a whole 2x2x4 slice. The times are simulated.
32 devices in a mesh: sec: 2 (over y), circ: 4 (over x, core), rad: 4 (over z).
Axes of the slice: x: 2, y: 2, z: 4, core: 2. Of those that a mesh axis runs over, the one named last changes fastest.
Arguments:
- adjoint: float32 [2, 5, 8, 64, 512], P('sec', None, None, 'rad', 'circ'), may hold values from -6 to 6
- source: float32 [2, 5, 8, 64, 512], P('sec', None, None, 'rad', 'circ'), may hold values from -6 to 6
- jacobian: float32 [2, 5, 5, 8, 64, 512], P('sec', None, None, None, 'rad', 'circ'), may hold values from -2 to 2
- couple: float32 [2, 12, 8, 64, 512], P('sec', None, None, 'rad', 'circ'), may hold values from 0.05 to 1
- donor_row: int32 [4, 4, 4, 6], P('rad'), may hold values from 0 to 15, as said below
- target_row: int32 [4, 4, 4, 6], P('rad'), may hold values from 0 to 15, as said below
- tile_count: int32 [4, 4, 4], P('rad'), may hold values from 0 to 6, as said below
- weights: float32 [4, 4, 4, 6, 128], P('rad', None, 'circ'), may hold values from 0.2 to 1
Outputs:
- swept: float32 [2, 5, 8, 64, 512], P('sec', None, None, 'rad', 'circ')
Inputs may be any that keep to these rules, and one draw needn't show every extreme that they name: `tile_count`: counts are ragged over all pairs of a radial index; in every draw some stator device receives 6 tiles from every rotor device of its radial index. `donor_row`: entries at slots at or past the pair's tile_count are not read. `target_row`: each target row lies within one row of its donor row. Entries at slots at or past the pair's tile_count are not read.
All inputs are finite; a program needn't handle non-finite values.
Results may differ from a plain program's by a relative error of at most 0.000075.
Values sent between devices are 32-bit elements; how exact they have to be, the bound alone decides.
No kernel may reach another device: no remote copies, remote signals or barrier semaphores. Data moves between devices by JAX's collectives and lax.ppermute only.
A program may use at most 64 MiB of HBM per device.

v0:
```python
import jax
import jax.numpy as jnp
from jax import lax
from jax.sharding import PartitionSpec as P

SWEEPS = 3


def passed_along(x, axis, by):
    peers = lax.axis_size(axis)
    pairs = [(i, i + by) for i in range(peers) if 0 <= i + by < peers]
    return lax.ppermute(x, axis, pairs)


def padded(x, sides, width, wrap):
    for axis, dim in sides:
        peers, length = (lax.axis_size(axis), x.shape[dim])
        up = [(i, (i + 1) % peers) for i in range(peers if wrap else peers - 1)]
        down = [(j, i) for i, j in up]
        last = lax.slice_in_dim(x, length - width, length, axis=dim)
        initial = lax.slice_in_dim(x, 0, width, axis=dim)
        before = lax.ppermute(last, axis, up)
        after = lax.ppermute(initial, axis, down)
        x = jnp.concatenate([before, x, after], axis=dim)
    return x


def pick_rows(face, rows):
    onehot = (rows[..., None] == jnp.arange(face.shape[2], dtype=jnp.int32)).astype(jnp.float32)
    return jnp.einsum("nkr,xyrc->nkxyc", onehot, face, precision=lax.Precision.HIGHEST)


def place_rows(tiles, targets, scale, rows_dev):
    onehot = (targets[..., None] == jnp.arange(rows_dev, dtype=jnp.int32)).astype(jnp.float32)
    weighted = tiles * scale[:, :, None, None, :]
    return jnp.einsum("dkr,dkxyc->xyrc", onehot, weighted, precision=lax.Precision.HIGHEST)


def sweep_once(lam_ext, couple, jacobian, rhs, pivot):
    na = lam_ext.shape[2]
    rows = lam_ext.shape[3] - 4
    cols = lam_ext.shape[4] - 4
    nvars = lam_ext.shape[1]
    center = lam_ext[:, :, :, 2 : 2 + rows, 2 : 2 + cols]
    axial_ext = jnp.pad(center, ((0, 0), (0, 0), (2, 2), (0, 0), (0, 0)))
    near = []
    for offset in (-2, -1, 1, 2):
        near.append(axial_ext[:, :, 2 + offset : 2 + offset + na])
    for offset in (-2, -1, 1, 2):
        near.append(lam_ext[:, :, :, 2 + offset : 2 + offset + rows, 2 : 2 + cols])
    for offset in (-2, -1, 1, 2):
        near.append(lam_ext[:, :, :, 2 : 2 + rows, 2 + offset : 2 + offset + cols])
    total = jnp.zeros_like(center)
    for index in range(12):
        total = total + couple[:, index][:, None] * near[index]
    turned = jnp.zeros_like(center)
    for column in range(nvars):
        turned = turned + jacobian[:, :, column] * total[:, column][:, None]
    return (rhs + turned) / pivot[:, None]


def per_device(adjoint, source, jacobian, couple, donor_row, target_row, tile_count, weights):
    section = lax.axis_index("sec")
    circ_at = lax.axis_index("circ")
    na = adjoint.shape[2]
    rows_dev = adjoint.shape[3]
    slots = donor_row.shape[-1]
    face = adjoint[0, :, na - 2 :]
    rows_all = donor_row[0]
    rows_out = lax.dynamic_index_in_dim(rows_all, circ_at, 0, keepdims=False)
    packed = pick_rows(face, rows_out)
    arrived = lax.all_to_all(packed, "circ", split_axis=0, concat_axis=0, tiled=True)
    received = passed_along(arrived, "sec", 1)
    counts_in = lax.dynamic_index_in_dim(tile_count[0], circ_at, 1, keepdims=False)
    targets_in = lax.dynamic_index_in_dim(target_row[0], circ_at, 1, keepdims=False)
    live = (jnp.arange(slots, dtype=jnp.int32)[None, :] < counts_in[:, None]).astype(jnp.float32)
    scale = weights[0, :, 0] * live[..., None]
    inflow = place_rows(received, targets_in, scale, rows_dev)
    stator_flag = (section == 1).astype(jnp.float32)
    rhs = source.at[0, :, 0:2].add(inflow * stator_flag)
    lam = adjoint
    pivot = 1.0 + jnp.sum(couple, axis=1)
    for sweep in range(SWEEPS):
        rad_ext = padded(lam, (("rad", 3),), 2, False)
        both_ext = padded(rad_ext, (("circ", 4),), 2, True)
        lam = sweep_once(both_ext, couple, jacobian, rhs, pivot)
    return lam


def solution(mesh):
    in_specs = (
        P("sec", None, None, "rad", "circ"),
        P("sec", None, None, "rad", "circ"),
        P("sec", None, None, None, "rad", "circ"),
        P("sec", None, None, "rad", "circ"),
        P("rad", None, None, None),
        P("rad", None, None, None),
        P("rad", None, None),
        P("rad", None, "circ", None, None),
    )
    out_specs = P("sec", None, None, "rad", "circ")
    return jax.shard_map(
        per_device, mesh=mesh, in_specs=in_specs, out_specs=out_specs, check_vma=False
    )
```

profile of v0, /device:TPU:0, one launch (start us, length us, event | category | flops | bytes accessed | tf_op | source)
XLA Modules:
  0.0 92.1 jit_solution(15936826394156775210)
XLA Ops:
  0.0 1.1 %fusion.104 = (f32[1,5,8,2,128]{4,3,2,1,0:T(2,128)S(1)}, f32[1,5,8,2,128]{4,3,2,1,0:T(2,128)S(1)}) fusion(f32[1,5,8,16,128]{4,3,2,1,0:T(8,128)} %param.10), kind=kLoop, calls=%fused_computation.212 | loop fusion | bytes 163840 | tf_op jit(solution)/shard_map/slice | solution.py:21
  1.1 1.3 %collective-permute-start.2 = (f32[1,5,8,2,128]{4,3,2,1,0:T(2,128)S(1)}, f32[1,5,8,2,128]{4,3,2,1,0:T(2,128)S(1)}, u32[]{:S(2)}, u32[]{:S(2)}) collective-permute-start(f32[1,5,8,2,128]{4,3,2,1,0:T(2,128)S(1)} %get-tuple-element.54), channel_id=1, source_target_pairs={{1,0},{2,1},{3,2},{5,4},{6,5},{7,6},{9,8},{10,9},{11,10},{13,12},{... | collective-permute-start | bytes 122888 | tf_op jit(solution)/shard_map/ppermute | solution.py:23
  2.4 5.6 %collective-permute-start.1 = (f32[1,5,8,2,128]{4,3,2,1,0:T(2,128)S(1)}, f32[1,5,8,2,128]{4,3,2,1,0:T(2,128)S(1)}, u32[]{:S(2)}, u32[]{:S(2)}) collective-permute-start(f32[1,5,8,2,128]{4,3,2,1,0:T(2,128)S(1)} %get-tuple-element.55), channel_id=1, source_target_pairs={{0,1},{1,2},{2,3},{4,5},{5,6},{6,7},{8,9},{9,10},{10,11},{12,13},{... | collective-permute-start | bytes 122888 | tf_op jit(solution)/shard_map/ppermute | solution.py:22
  8.0 1.2 %fusion.89 = f32[4,6,5,2,128]{4,1,3,2,0:T(8,128)S(1)} fusion(f32[1,5,8,16,128]{4,3,2,1,0:T(8,128)} %param.10, s32[4,6]{1,0:T(4,128)S(1)} %dynamic-slice_bitcast_fusion), kind=kOutput, calls=%fused_computation.161 | convolution fusion | flops 5898624 | bytes 204896 | tf_op jit(solution)/shard_map/nkr,xyrc->nkxyc/dot_general | solution.py:30
  9.2 0.7 copy.21
  9.9 3.9 %all-to-all-start = ((f32[4,6,5,2,128]{4,3,2,1,0:T(2,128)}), f32[4,6,5,2,128]{4,3,2,1,0:T(2,128)}, u32[]{:S(2)}, u32[]{:S(2)}) async-start(f32[4,6,5,2,128]{4,3,2,1,0:T(2,128)} %copy.21), calls=%async_computation | async-start | bytes 245760 | tf_op jit(solution)/shard_map/all_to_all | solution.py:72
  13.9 0.0 copy-done.3
  13.9 0.0 copy-start.13
  13.9 0.0 copy-done.14
  13.9 0.2 dynamic-slice_reduce_fusion
  14.1 0.8 slice_bitcast_fusion.26
  14.9 0.1 reduce_sum.9
  15.0 0.6 broadcast_add_fusion
  15.6 0.0 copy-done.13
  15.6 0.1 bitcast_multiply_fusion.15
  15.7 1.3 %constant_dynamic-slice_fusion = s32[1,4,1,6]{3,2,1,0:T(1,128)} fusion(s32[1,4,4,6]{3,2,1,0:T(4,128)} %param.15, s32[]{:T(128)S(6)} %select_n.8), kind=kLoop, calls=%fused_computation.206 | loop fusion | bytes 196 | tf_op jit(solution)/shard_map/jit(dynamic_index_in_dim)/dynamic_slice | solution.py:75
  17.0 0.6 copy.23
  17.6 0.0 collective-permute-done.2
  17.6 0.0 collective-permute-done.1
  17.6 0.1 pad_maximum_fusion
  17.7 0.2 fusion.101
  17.8 0.5 collective-permute-start.3
  18.3 1.3 %collective-permute-start.4 = (f32[1,5,8,20,2]{4,3,2,1,0:T(8,128)S(1)}, f32[1,5,8,20,2]{4,3,2,1,0:T(8,128)S(1)}, u32[]{:S(2)}, u32[]{:S(2)}) collective-permute-start(f32[1,5,8,20,2]{4,3,2,1,0:T(8,128)S(1)} %get-tuple-element.34), channel_id=1, source_target_pairs={{4,0},{8,4},{12,8},{0,12},{5,1},{9,5},{13,9},{1,13},{6,2},{10,6},{... | collective-permute-start | bytes 19208 | tf_op jit(solution)/shard_map/ppermute | solution.py:23
  19.7 9.4 %collective-permute-done.3 = f32[1,5,8,20,2]{4,3,2,1,0:T(8,128)S(1)} collective-permute-done((f32[1,5,8,20,2]{4,3,2,1,0:T(8,128)S(1)}, f32[1,5,8,20,2]{4,3,2,1,0:T(8,128)S(1)}, u32[]{:S(2)}, u32[]{:S(2)}) %collective-permute-start.3) | collective-permute-done | bytes 6432 | tf_op jit(solution)/shard_map/ppermute | solution.py:22
  29.1 1.8 %collective-permute-done.4 = f32[1,5,8,20,2]{4,3,2,1,0:T(8,128)S(1)} collective-permute-done((f32[1,5,8,20,2]{4,3,2,1,0:T(8,128)S(1)}, f32[1,5,8,20,2]{4,3,2,1,0:T(8,128)S(1)}, u32[]{:S(2)}, u32[]{:S(2)}) %collective-permute-start.4) | collective-permute-done | bytes 6432 | tf_op jit(solution)/shard_map/ppermute | solution.py:23
  30.9 2.1 %fusion.37 = f32[1,5,8,16,128]{4,3,2,1,0:T(8,128)S(1)} fusion(f32[1,5,8,2,128]{4,3,2,1,0:T(2,128)} %copy-done.12, f32[1,5,8,16,128]{4,3,2,1,0:T(8,128)S(1)} %copy-done.3, f32[1,5,8,20,2]{4,3,2,1,0:T(8,128)S(1)} %collective-permute-done.4, f32[1,5,8,2,128]{4,3,2,1,0:T(2,128)S(1)} %collective-permute-done.2, ...), kind=kLoop, calls=%fused_computation.63 | loop fusion | flops 3031040 | bytes 2191872 | tf_op jit(solution)/shard_map/add | solution.py:55
  33.0 0.0 all-to-all-done
  33.0 3.9 %collective-permute-start = (f32[4,6,5,2,128]{4,3,2,1,0:T(2,128)}, f32[4,6,5,2,128]{4,3,2,1,0:T(2,128)S(1)}, u32[]{:S(2)}, u32[]{:S(2)}) collective-permute-start(f32[4,6,5,2,128]{4,3,2,1,0:T(2,128)} %all-to-all-done), channel_id=1, source_target_pairs={{0,16},{1,17},{2,18},{3,19},{4,20},{5,21},{6,22},{7,23},{8,24},{9,... | collective-permute-start | bytes 368648 | tf_op jit(solution)/shard_map/ppermute | solution.py:12
  36.9 3.4 %collective-permute-done = f32[4,6,5,2,128]{4,3,2,1,0:T(2,128)S(1)} collective-permute-done((f32[4,6,5,2,128]{4,3,2,1,0:T(2,128)}, f32[4,6,5,2,128]{4,3,2,1,0:T(2,128)S(1)}, u32[]{:S(2)}, u32[]{:S(2)}) %collective-permute-start) | collective-permute-done | bytes 122912 | tf_op jit(solution)/shard_map/ppermute | solution.py:12
  40.3 0.8 broadcast_multiply_fusion
  41.1 1.0 %fusion.3 = f32[1,5,8,16,128]{4,3,2,1,0:T(8,128)S(1)} fusion(f32[1,5,8,16,128]{4,3,2,1,0:T(8,128)S(1)} %copy-done.2, f32[4,6,5,2,128]{4,3,2,1,0:T(2,128)S(1)} %broadcast_multiply_fusion, f32[]{:T(128)S(6)} %convert_element_type.17, s32[4,6]{1,0:T(4,128)} %bitcast.182), kind=kOutput, calls=%fused_computation.4 | convolution fusion | flops 5939584 | bytes 286820 | tf_op jit(solution)/shard_map/dkr,dkxyc->xyrc/dot_general | solution.py:36
  42.1 1.0 %fusion.72 = f32[1,5,8,16,128]{4,3,2,1,0:T(8,128)S(1)} fusion(f32[1,5,8,16,128]{4,3,2,1,0:T(8,128)S(1)} %fusion.3, f32[1,5,5,8,16,128]{5,4,3,2,1,0:T(8,128)S(1)} %copy-done.1, f32[8,16,128]{2,1,0:T(8,128)} %broadcast_add_fusion, f32[8,16,128]{2,1,0:T(8,128)S(1)} %get-tuple-element.50, f32[8,16,128]{2,1,0:T(8,128)S(1)} %get-tuple-element.51, ...), kind=kLoop, calls=%fused_computation.132 | loop fusion | flops 901120 | bytes 2686976 | tf_op jit(solution)/shard_map/div | solution.py:59
  43.1 0.0 copy-start.5
  43.1 0.0 copy-start.6
  43.2 0.0 copy-start.7
  43.2 0.0 copy-start.8
  43.2 0.0 copy-start.9
  43.2 0.0 copy-start.10
  43.2 3.6 %collective-permute-start.5 = (f32[1,5,8,2,128]{4,3,2,1,0:T(2,128)S(1)}, f32[1,5,8,2,128]{4,3,2,1,0:T(2,128)S(1)}, u32[]{:S(2)}, u32[]{:S(2)}) collective-permute-start(f32[1,5,8,2,128]{4,3,2,1,0:T(2,128)S(1)} %get-tuple-element.47), channel_id=1, source_target_pairs={{0,1},{1,2},{2,3},{4,5},{5,6},{6,7},{8,9},{9,10},{10,11},{12,13},{... | collective-permute-start | bytes 122888 | tf_op jit(solution)/shard_map/ppermute | solution.py:22
  46.9 1.3 %collective-permute-start.6 = (f32[1,5,8,2,128]{4,3,2,1,0:T(2,128)S(1)}, f32[1,5,8,2,128]{4,3,2,1,0:T(2,128)S(1)}, u32[]{:S(2)}, u32[]{:S(2)}) collective-permute-start(f32[1,5,8,2,128]{4,3,2,1,0:T(2,128)S(1)} %get-tuple-element.48), channel_id=1, source_target_pairs={{1,0},{2,1},{3,2},{5,4},{6,5},{7,6},{9,8},{10,9},{11,10},{13,12},{... | collective-permute-start | bytes 122888 | tf_op jit(solution)/shard_map/ppermute | solution.py:23
  48.2 0.4 collective-permute-done.5
  48.5 4.2 %collective-permute-done.6 = f32[1,5,8,2,128]{4,3,2,1,0:T(2,128)S(1)} collective-permute-done((f32[1,5,8,2,128]{4,3,2,1,0:T(2,128)S(1)}, f32[1,5,8,2,128]{4,3,2,1,0:T(2,128)S(1)}, u32[]{:S(2)}, u32[]{:S(2)}) %collective-permute-start.6) | collective-permute-done | bytes 40992 | tf_op jit(solution)/shard_map/ppermute | solution.py:23
  52.8 0.1 pad_maximum_fusion.1
  52.8 0.2 fusion.100
  53.0 0.1 collective-permute-start.7
  53.1 1.7 %collective-permute-start.8 = (f32[1,5,8,20,2]{4,3,2,1,0:T(8,128)S(1)}, f32[1,5,8,20,2]{4,3,2,1,0:T(8,128)S(1)}, u32[]{:S(2)}, u32[]{:S(2)}) collective-permute-start(f32[1,5,8,20,2]{4,3,2,1,0:T(8,128)S(1)} %get-tuple-element.32), channel_id=1, source_target_pairs={{4,0},{8,4},{12,8},{0,12},{5,1},{9,5},{13,9},{1,13},{6,2},{10,6},{... | collective-permute-start | bytes 19208 | tf_op jit(solution)/shard_map/ppermute | solution.py:23
  54.8 9.5 %collective-permute-done.7 = f32[1,5,8,20,2]{4,3,2,1,0:T(8,128)S(1)} collective-permute-done((f32[1,5,8,20,2]{4,3,2,1,0:T(8,128)S(1)}, f32[1,5,8,20,2]{4,3,2,1,0:T(8,128)S(1)}, u32[]{:S(2)}, u32[]{:S(2)}) %collective-permute-start.7) | collective-permute-done | bytes 6432 | tf_op jit(solution)/shard_map/ppermute | solution.py:22
  64.3 1.8 %collective-permute-done.8 = f32[1,5,8,20,2]{4,3,2,1,0:T(8,128)S(1)} collective-permute-done((f32[1,5,8,20,2]{4,3,2,1,0:T(8,128)S(1)}, f32[1,5,8,20,2]{4,3,2,1,0:T(8,128)S(1)}, u32[]{:S(2)}, u32[]{:S(2)}) %collective-permute-start.8) | collective-permute-done | bytes 6432 | tf_op jit(solution)/shard_map/ppermute | solution.py:23
  66.1 0.0 copy-done.8
  66.1 0.0 copy-done.9
  66.1 0.9 fusion.23
  67.1 0.2 fusion.75
  67.3 3.5 %collective-permute-start.9 = (f32[1,5,8,2,128]{4,3,2,1,0:T(2,128)S(1)}, f32[1,5,8,2,128]{4,3,2,1,0:T(2,128)S(1)}, u32[]{:S(2)}, u32[]{:S(2)}) collective-permute-start(f32[1,5,8,2,128]{4,3,2,1,0:T(2,128)S(1)} %get-tuple-element.40), channel_id=1, source_target_pairs={{0,1},{1,2},{2,3},{4,5},{5,6},{6,7},{8,9},{9,10},{10,11},{12,13},{... | collective-permute-start | bytes 122888 | tf_op jit(solution)/shard_map/ppermute | solution.py:22
  70.8 1.3 %collective-permute-start.10 = (f32[1,5,8,2,128]{4,3,2,1,0:T(2,128)S(1)}, f32[1,5,8,2,128]{4,3,2,1,0:T(2,128)S(1)}, u32[]{:S(2)}, u32[]{:S(2)}) collective-permute-start(f32[1,5,8,2,128]{4,3,2,1,0:T(2,128)S(1)} %get-tuple-element.41), channel_id=1, source_target_pairs={{1,0},{2,1},{3,2},{5,4},{6,5},{7,6},{9,8},{10,9},{11,10},{13,12},{... | collective-permute-start | bytes 122888 | tf_op jit(solution)/shard_map/ppermute | solution.py:23
  72.1 0.4 collective-permute-done.9
  72.4 4.2 %collective-permute-done.10 = f32[1,5,8,2,128]{4,3,2,1,0:T(2,128)S(1)} collective-permute-done((f32[1,5,8,2,128]{4,3,2,1,0:T(2,128)S(1)}, f32[1,5,8,2,128]{4,3,2,1,0:T(2,128)S(1)}, u32[]{:S(2)}, u32[]{:S(2)}) %collective-permute-start.10) | collective-permute-done | bytes 40992 | tf_op jit(solution)/shard_map/ppermute | solution.py:23
  76.7 0.1 pad_maximum_fusion.2
  76.7 0.2 fusion.99
  76.9 0.1 collective-permute-start.11
  77.0 1.7 %collective-permute-start.12 = (f32[1,5,8,20,2]{4,3,2,1,0:T(8,128)S(1)}, f32[1,5,8,20,2]{4,3,2,1,0:T(8,128)S(1)}, u32[]{:S(2)}, u32[]{:S(2)}) collective-permute-start(f32[1,5,8,20,2]{4,3,2,1,0:T(8,128)S(1)} %get-tuple-element.30), channel_id=1, source_target_pairs={{4,0},{8,4},{12,8},{0,12},{5,1},{9,5},{13,9},{1,13},{6,2},{10,6},{... | collective-permute-start | bytes 19208 | tf_op jit(solution)/shard_map/ppermute | solution.py:23
  78.7 9.2 %collective-permute-done.11 = f32[1,5,8,20,2]{4,3,2,1,0:T(8,128)S(1)} collective-permute-done((f32[1,5,8,20,2]{4,3,2,1,0:T(8,128)S(1)}, f32[1,5,8,20,2]{4,3,2,1,0:T(8,128)S(1)}, u32[]{:S(2)}, u32[]{:S(2)}) %collective-permute-start.11) | collective-permute-done | bytes 6432 | tf_op jit(solution)/shard_map/ppermute | solution.py:22
  87.9 2.3 %collective-permute-done.12 = f32[1,5,8,20,2]{4,3,2,1,0:T(8,128)S(1)} collective-permute-done((f32[1,5,8,20,2]{4,3,2,1,0:T(8,128)S(1)}, f32[1,5,8,20,2]{4,3,2,1,0:T(8,128)S(1)}, u32[]{:S(2)}, u32[]{:S(2)}) %collective-permute-start.12) | collective-permute-done | bytes 6432 | tf_op jit(solution)/shard_map/ppermute | solution.py:23
  90.2 0.9 fusion.11
  91.2 0.9 fusion.78
  (27 shorter events, 0.2 us)
Async XLA Ops:
  0.0 8.0 %copy-start = (s32[1,4,4,6]{3,2,1,0:T(4,128)S(1)}, s32[1,4,4,6]{3,2,1,0:T(4,128)}, u32[]{:S(2)}) copy-start(s32[1,4,4,6]{3,2,1,0:T(4,128)} %param.14) | copy-start | bytes 1156
  0.0 13.9 %copy-start.3 = (f32[1,5,8,16,128]{4,3,2,1,0:T(8,128)S(1)}, f32[1,5,8,16,128]{4,3,2,1,0:T(8,128)}, u32[]{:S(2)}) copy-start(f32[1,5,8,16,128]{4,3,2,1,0:T(8,128)} %param.10) | copy-start | bytes 983044
  0.0 14.1 %copy-start.4 = (f32[1,12,8,16,128]{4,3,2,1,0:T(8,128)S(1)}, f32[1,12,8,16,128]{4,3,2,1,0:T(8,128)}, u32[]{:S(2)}) copy-start(f32[1,12,8,16,128]{4,3,2,1,0:T(8,128)} %param.13) | copy-start | bytes 2359300
  0.0 13.9 %copy-start.14 = (s32[1,4,4]{2,1,0:T(4,128)S(1)}, s32[1,4,4]{2,1,0:T(4,128)}, u32[]{:S(2)}) copy-start(s32[1,4,4]{2,1,0:T(4,128)} %param.16) | copy-start | bytes 196
  1.1 16.4 %collective-permute-start.2 = (f32[1,5,8,2,128]{4,3,2,1,0:T(2,128)S(1)}, f32[1,5,8,2,128]{4,3,2,1,0:T(2,128)S(1)}, u32[]{:S(2)}, u32[]{:S(2)}) collective-permute-start(f32[1,5,8,2,128]{4,3,2,1,0:T(2,128)S(1)} %get-tuple-element.54), channel_id=1, source_target_pairs={{1,0},{2,1},{3,2},{5,4},{6,5},{7,6},{9,8},{10,9},{11,10},{13,12},{... | collective-permute-start | bytes 122888 | tf_op jit(solution)/shard_map/ppermute | solution.py:23
  2.4 15.1 %collective-permute-start.1 = (f32[1,5,8,2,128]{4,3,2,1,0:T(2,128)S(1)}, f32[1,5,8,2,128]{4,3,2,1,0:T(2,128)S(1)}, u32[]{:S(2)}, u32[]{:S(2)}) collective-permute-start(f32[1,5,8,2,128]{4,3,2,1,0:T(2,128)S(1)} %get-tuple-element.55), channel_id=1, source_target_pairs={{0,1},{1,2},{2,3},{4,5},{5,6},{6,7},{8,9},{9,10},{10,11},{12,13},{... | collective-permute-start | bytes 122888 | tf_op jit(solution)/shard_map/ppermute | solution.py:22
  9.9 23.1 %all-to-all-start = ((f32[4,6,5,2,128]{4,3,2,1,0:T(2,128)}), f32[4,6,5,2,128]{4,3,2,1,0:T(2,128)}, u32[]{:S(2)}, u32[]{:S(2)}) async-start(f32[4,6,5,2,128]{4,3,2,1,0:T(2,128)} %copy.21), calls=%async_computation | async-start | bytes 245760 | tf_op jit(solution)/shard_map/all_to_all | solution.py:72
  13.9 1.7 %copy-start.13 = (f32[1,4,1,6,128]{4,2,3,1,0:T(1,128)S(1)}, f32[1,4,1,6,128]{4,2,3,1,0:T(1,128)}, u32[]{:S(2)}) copy-start(f32[1,4,1,6,128]{4,2,3,1,0:T(1,128)} %param.17) | copy-start | bytes 36868
  17.6 13.3 %copy-start.12 = (f32[1,5,8,2,128]{4,3,2,1,0:T(2,128)}, f32[1,5,8,2,128]{4,3,2,1,0:T(2,128)S(1)}, u32[]{:S(2)}) copy-start(f32[1,5,8,2,128]{4,3,2,1,0:T(2,128)S(1)} %collective-permute-done.1) | copy-start | bytes 122884
  17.8 11.2 %collective-permute-start.3 = (f32[1,5,8,20,2]{4,3,2,1,0:T(8,128)S(1)}, f32[1,5,8,20,2]{4,3,2,1,0:T(8,128)S(1)}, u32[]{:S(2)}, u32[]{:S(2)}) collective-permute-start(f32[1,5,8,20,2]{4,3,2,1,0:T(8,128)S(1)} %get-tuple-element.33), channel_id=1, source_target_pairs={{0,4},{4,8},{8,12},{12,0},{1,5},{5,9},{9,13},{13,1},{2,6},{6,10},{... | collective-permute-start | bytes 19208 | tf_op jit(solution)/shard_map/ppermute | solution.py:22
  18.3 12.6 %collective-permute-start.4 = (f32[1,5,8,20,2]{4,3,2,1,0:T(8,128)S(1)}, f32[1,5,8,20,2]{4,3,2,1,0:T(8,128)S(1)}, u32[]{:S(2)}, u32[]{:S(2)}) collective-permute-start(f32[1,5,8,20,2]{4,3,2,1,0:T(8,128)S(1)} %get-tuple-element.34), channel_id=1, source_target_pairs={{4,0},{8,4},{12,8},{0,12},{5,1},{9,5},{13,9},{1,13},{6,2},{10,6},{... | collective-permute-start | bytes 19208 | tf_op jit(solution)/shard_map/ppermute | solution.py:23
  30.9 10.2 %copy-start.2 = (f32[1,5,8,16,128]{4,3,2,1,0:T(8,128)S(1)}, f32[1,5,8,16,128]{4,3,2,1,0:T(8,128)}, u32[]{:S(2)}) copy-start(f32[1,5,8,16,128]{4,3,2,1,0:T(8,128)} %param.11) | copy-start | bytes 983044
  30.9 11.2 %copy-start.1 = (f32[1,5,5,8,16,128]{5,4,3,2,1,0:T(8,128)S(1)}, f32[1,5,5,8,16,128]{5,4,3,2,1,0:T(8,128)}, u32[]{:S(2)}) copy-start(f32[1,5,5,8,16,128]{5,4,3,2,1,0:T(8,128)} %param.12) | copy-start | bytes 4915204
  33.0 7.3 %collective-permute-start = (f32[4,6,5,2,128]{4,3,2,1,0:T(2,128)}, f32[4,6,5,2,128]{4,3,2,1,0:T(2,128)S(1)}, u32[]{:S(2)}, u32[]{:S(2)}) collective-permute-start(f32[4,6,5,2,128]{4,3,2,1,0:T(2,128)} %all-to-all-done), channel_id=1, source_target_pairs={{0,16},{1,17},{2,18},{3,19},{4,20},{5,21},{6,22},{7,23},{8,24},{9,... | collective-permute-start | bytes 368648 | tf_op jit(solution)/shard_map/ppermute | solution.py:12
  43.1 23.0 %copy-start.5 = (f32[8,16,128]{2,1,0:T(8,128)S(1)}, f32[8,16,128]{2,1,0:T(8,128)}, u32[]{:S(2)}) copy-start(f32[8,16,128]{2,1,0:T(8,128)} %get-tuple-element.23) | copy-start | bytes 196612
  43.1 22.9 %copy-start.6 = (f32[8,16,128]{2,1,0:T(8,128)S(1)}, f32[8,16,128]{2,1,0:T(8,128)}, u32[]{:S(2)}) copy-start(f32[8,16,128]{2,1,0:T(8,128)} %get-tuple-element.24) | copy-start | bytes 196612
  43.2 22.9 %copy-start.7 = (f32[8,16,128]{2,1,0:T(8,128)S(1)}, f32[8,16,128]{2,1,0:T(8,128)}, u32[]{:S(2)}) copy-start(f32[8,16,128]{2,1,0:T(8,128)} %get-tuple-element.25) | copy-start | bytes 196612
  43.2 22.9 %copy-start.8 = (f32[8,16,128]{2,1,0:T(8,128)S(1)}, f32[8,16,128]{2,1,0:T(8,128)}, u32[]{:S(2)}) copy-start(f32[8,16,128]{2,1,0:T(8,128)} %get-tuple-element.26) | copy-start | bytes 196612
  43.2 22.9 %copy-start.9 = (f32[8,16,128]{2,1,0:T(8,128)S(1)}, f32[8,16,128]{2,1,0:T(8,128)}, u32[]{:S(2)}) copy-start(f32[8,16,128]{2,1,0:T(8,128)} %get-tuple-element.27) | copy-start | bytes 196612
  43.2 22.9 %copy-start.10 = (f32[8,16,128]{2,1,0:T(8,128)S(1)}, f32[8,16,128]{2,1,0:T(8,128)}, u32[]{:S(2)}) copy-start(f32[8,16,128]{2,1,0:T(8,128)} %get-tuple-element.28) | copy-start | bytes 196612
  43.2 5.3 %collective-permute-start.5 = (f32[1,5,8,2,128]{4,3,2,1,0:T(2,128)S(1)}, f32[1,5,8,2,128]{4,3,2,1,0:T(2,128)S(1)}, u32[]{:S(2)}, u32[]{:S(2)}) collective-permute-start(f32[1,5,8,2,128]{4,3,2,1,0:T(2,128)S(1)} %get-tuple-element.47), channel_id=1, source_target_pairs={{0,1},{1,2},{2,3},{4,5},{5,6},{6,7},{8,9},{9,10},{10,11},{12,13},{... | collective-permute-start | bytes 122888 | tf_op jit(solution)/shard_map/ppermute | solution.py:22
  46.9 5.9 %collective-permute-start.6 = (f32[1,5,8,2,128]{4,3,2,1,0:T(2,128)S(1)}, f32[1,5,8,2,128]{4,3,2,1,0:T(2,128)S(1)}, u32[]{:S(2)}, u32[]{:S(2)}) collective-permute-start(f32[1,5,8,2,128]{4,3,2,1,0:T(2,128)S(1)} %get-tuple-element.48), channel_id=1, source_target_pairs={{1,0},{2,1},{3,2},{5,4},{6,5},{7,6},{9,8},{10,9},{11,10},{13,12},{... | collective-permute-start | bytes 122888 | tf_op jit(solution)/shard_map/ppermute | solution.py:23
  53.0 14.0 %copy-start.11 = (f32[8,16,128]{2,1,0:T(8,128)S(1)}, f32[8,16,128]{2,1,0:T(8,128)}, u32[]{:S(2)}) copy-start(f32[8,16,128]{2,1,0:T(8,128)} %broadcast_add_fusion) | copy-start | bytes 196612
  53.0 11.3 %collective-permute-start.7 = (f32[1,5,8,20,2]{4,3,2,1,0:T(8,128)S(1)}, f32[1,5,8,20,2]{4,3,2,1,0:T(8,128)S(1)}, u32[]{:S(2)}, u32[]{:S(2)}) collective-permute-start(f32[1,5,8,20,2]{4,3,2,1,0:T(8,128)S(1)} %get-tuple-element.31), channel_id=1, source_target_pairs={{0,4},{4,8},{8,12},{12,0},{1,5},{5,9},{9,13},{13,1},{2,6},{6,10},{... | collective-permute-start | bytes 19208 | tf_op jit(solution)/shard_map/ppermute | solution.py:22
  53.1 13.0 %collective-permute-start.8 = (f32[1,5,8,20,2]{4,3,2,1,0:T(8,128)S(1)}, f32[1,5,8,20,2]{4,3,2,1,0:T(8,128)S(1)}, u32[]{:S(2)}, u32[]{:S(2)}) collective-permute-start(f32[1,5,8,20,2]{4,3,2,1,0:T(8,128)S(1)} %get-tuple-element.32), channel_id=1, source_target_pairs={{4,0},{8,4},{12,8},{0,12},{5,1},{9,5},{13,9},{1,13},{6,2},{10,6},{... | collective-permute-start | bytes 19208 | tf_op jit(solution)/shard_map/ppermute | solution.py:23
  67.3 5.1 %collective-permute-start.9 = (f32[1,5,8,2,128]{4,3,2,1,0:T(2,128)S(1)}, f32[1,5,8,2,128]{4,3,2,1,0:T(2,128)S(1)}, u32[]{:S(2)}, u32[]{:S(2)}) collective-permute-start(f32[1,5,8,2,128]{4,3,2,1,0:T(2,128)S(1)} %get-tuple-element.40), channel_id=1, source_target_pairs={{0,1},{1,2},{2,3},{4,5},{5,6},{6,7},{8,9},{9,10},{10,11},{12,13},{... | collective-permute-start | bytes 122888 | tf_op jit(solution)/shard_map/ppermute | solution.py:22
  70.8 5.9 %collective-permute-start.10 = (f32[1,5,8,2,128]{4,3,2,1,0:T(2,128)S(1)}, f32[1,5,8,2,128]{4,3,2,1,0:T(2,128)S(1)}, u32[]{:S(2)}, u32[]{:S(2)}) collective-permute-start(f32[1,5,8,2,128]{4,3,2,1,0:T(2,128)S(1)} %get-tuple-element.41), channel_id=1, source_target_pairs={{1,0},{2,1},{3,2},{5,4},{6,5},{7,6},{9,8},{10,9},{11,10},{13,12},{... | collective-permute-start | bytes 122888 | tf_op jit(solution)/shard_map/ppermute | solution.py:23
  76.9 11.0 %collective-permute-start.11 = (f32[1,5,8,20,2]{4,3,2,1,0:T(8,128)S(1)}, f32[1,5,8,20,2]{4,3,2,1,0:T(8,128)S(1)}, u32[]{:S(2)}, u32[]{:S(2)}) collective-permute-start(f32[1,5,8,20,2]{4,3,2,1,0:T(8,128)S(1)} %get-tuple-element.29), channel_id=1, source_target_pairs={{0,4},{4,8},{8,12},{12,0},{1,5},{5,9},{9,13},{13,1},{2,6},{6,10},{... | collective-permute-start | bytes 19208 | tf_op jit(solution)/shard_map/ppermute | solution.py:22
  77.0 13.3 %collective-permute-start.12 = (f32[1,5,8,20,2]{4,3,2,1,0:T(8,128)S(1)}, f32[1,5,8,20,2]{4,3,2,1,0:T(8,128)S(1)}, u32[]{:S(2)}, u32[]{:S(2)}) collective-permute-start(f32[1,5,8,20,2]{4,3,2,1,0:T(8,128)S(1)} %get-tuple-element.30), channel_id=1, source_target_pairs={{4,0},{8,4},{12,8},{0,12},{5,1},{9,5},{13,9},{1,13},{6,2},{10,6},{... | collective-permute-start | bytes 19208 | tf_op jit(solution)/shard_map/ppermute | solution.py:23
where the time goes:
time: 93.3 us; the launch traced here: 92.1 us
  waiting for transfers between devices  46.5 us (50%)
  starting transfers between devices  29.8 us (32%)
  other arithmetic  7.75 us (8%)
  local copies, waits for them, and re-layouts  5.52 us (6%)
  matrix products  2.15 us (2%)
    ppermute x6, waiting for transfers between devices, padded(): before = lax.ppermute(last, axis, up)  28.8 us
    ppermute x6, waiting for transfers between devices, padded(): after = lax.ppermute(initial, axis, down)  14.4 us
    ppermute x6, starting transfers between devices, padded(): before = lax.ppermute(last, axis, up)  13.3 us
    ppermute x6, starting transfers between devices, padded(): after = lax.ppermute(initial, axis, down)  8.68 us
    all_to_all x1, starting transfers between devices, per_device(): lax.all_to_all(packed, 'circ', split_axis=0, concat_axis=0, tiled=True)  3.95 us
    add x3, other arithmetic, sweep_once(): total = total + couple[:, index][:, None] * near[index]  3.9 us
    ppermute x1, starting transfers between devices, passed_along(): return lax.ppermute(x, axis, pairs)  3.87 us
    ppermute x1, waiting for transfers between devices, passed_along(): return lax.ppermute(x, axis, pairs)  3.35 us
  transfers between devices with their start and end apart: 14, of which 11 were waited for; matrix products, arithmetic and copies ran while one was open for 9% of the time, Pallas kernels for 0%

commit v1 on v0

v1 whole, which is shorter than its diff:
```python
import jax
import jax.numpy as jnp
from jax import lax
from jax.experimental import pallas as pl
from jax.experimental.pallas import tpu as pltpu
from jax.sharding import PartitionSpec as P

SWEEPS = 3
AXES = ("sec", "circ", "rad")
SUB, LANES = 8, 128
GROUP = 20
PARAMS = pltpu.CompilerParams(vmem_limit_bytes=16 * 1024 * 1024)


def routes(mesh):
    secs, circs, rads = (mesh.shape[a] for a in AXES)

    def pairs(target):
        flat = lambda s, c, r: (s * circs + c) * rads + r
        return [
            (flat(s, c, r), flat(*target(s, c, r)))
            for s in range(secs)
            for c in range(circs)
            for r in range(rads)
        ]

    def snake(s, c, r):
        if c % 2 == 0:
            return (s, c, r + 1) if r < rads - 1 else (s, c + 1, r)
        return (s, c, r - 1) if r > 0 else (s, c - 1, r)

    ahead = pairs(snake)
    return {
        "ahead": ahead,
        "back": [(b, a) for a, b in ahead],
        "mate": pairs(lambda s, c, r: (s, c ^ 1, r)),
        "across": pairs(lambda s, c, r: (s, (c - 1 if c % 2 == 0 else c + 1) % circs, r)),
        "faces": [
            pairs(lambda s, c, r: (1, (c + k) % circs, r) if s == 0 else (0, (c - k) % circs, r))
            for k in range(0, circs, 2)
        ],
    }


def iotas():
    sub = lax.broadcasted_iota(jnp.int32, (SUB, LANES), 0)
    lane = lax.broadcasted_iota(jnp.int32, (SUB, LANES), 1)
    return sub, lane


def down(x, by):
    return pltpu.roll(x, by % SUB, 0) if by % SUB else x


def along(x, by):
    return pltpu.roll(x, by % LANES, 1) if by % LANES else x


class Packer:
    def __init__(self, na, nv):
        self.sub, self.lane = iotas()
        self.na = na
        self.low, self.high, self.cols = {}, {}, {}

    def put(self, book, key, keep, x):
        book[key] = jnp.where(keep, x, book[key]) if key in book else x

    def add(self, v, a, half, x):
        k = v * self.na + a
        group, j = k // 4, k % 4
        inside = (self.sub >= 2 * j) & (self.sub < 2 * j + 2)
        if half == 0:
            self.put(self.low, group, inside, down(x, 2 * j))
        else:
            self.put(self.high, group, inside, down(x, 2 * j + 2))
        spot = 4 * (k % GROUP)
        inside = (self.lane >= spot) & (self.lane < spot + 4)
        self.put(self.cols, (k // GROUP, half), inside, along(x, spot + 2))

    def write(self, ahead_ref, back_ref, cols_ref):
        even = lax.axis_index("circ") % 2 == 0
        for g in range(len(self.low)):
            rows = slice(SUB * g, SUB * (g + 1))
            ahead_ref[rows, :] = jnp.where(even, self.high[g], self.low[g])
            back_ref[rows, :] = jnp.where(even, self.low[g], self.high[g])
        for (part, half), x in self.cols.items():
            at = SUB * (2 * part + half)
            cols_ref[at : at + SUB, :] = x


def pack_kernel(lam_ref, ahead_ref, back_ref, cols_ref, face_ref):
    nv, na = lam_ref.shape[:2]
    packer = Packer(na, nv)
    for v in range(nv):
        for a in range(na):
            for half in range(2):
                rows = slice(SUB * half, SUB * (half + 1))
                x = lam_ref[v, a, rows, :]
                packer.add(v, a, half, x)
                if a >= na - 2:
                    face_ref[v, a - (na - 2), rows, :] = x
    packer.write(ahead_ref, back_ref, cols_ref)


def taps_kernel(donors_ref, targets_ref, counts_ref, weights_ref, after_ref, taps_ref):
    me = lax.axis_index("circ")
    stator = lax.axis_index("sec") == 1
    sub, _ = iotas()
    slots = donors_ref.shape[-1]
    for d in range(donors_ref.shape[0]):
        acc = {(t, h): jnp.zeros((SUB, LANES), jnp.float32) for t in range(3) for h in range(2)}
        for k in range(slots):
            live = (k < counts_ref[d, me]) & stator
            target = targets_ref[d, me, k]
            step = target - donors_ref[d, me, k]
            w = jnp.broadcast_to(weights_ref[d * slots + k : d * slots + k + 1, :], (SUB, LANES))
            for t in range(3):
                row = jnp.where(live & (step == t - 1), target, -1)
                for h in range(2):
                    acc[t, h] += jnp.where(sub + SUB * h == row, w, 0.0)
        for (t, h), x in acc.items():
            taps_ref[d, t, SUB * h : SUB * (h + 1), :] = x


def local_kernel(first, *refs):
    lam_ref, couple_ref, _, near_ref = refs[:4]
    nv, na = lam_ref.shape[:2]
    sub, lane = iotas()
    for a in range(na):
        coef = []
        for half in range(2):
            rows = slice(SUB * half, SUB * (half + 1))
            c = [couple_ref[i, a, rows, :] for i in range(12)]
            if first:
                total = c[0]
                for i in range(1, 12):
                    total = total + c[i]
                refs[4][a, rows, :] = 1.0 / (1.0 + total)
            if half == 0:
                c[4] = jnp.where(sub >= 2, c[4], 0.0)
                c[5] = jnp.where(sub >= 1, c[5], 0.0)
            else:
                c[6] = jnp.where(sub < SUB - 1, c[6], 0.0)
                c[7] = jnp.where(sub < SUB - 2, c[7], 0.0)
            c[8] = jnp.where(lane >= 2, c[8], 0.0)
            c[9] = jnp.where(lane >= 1, c[9], 0.0)
            c[10] = jnp.where(lane < LANES - 1, c[10], 0.0)
            c[11] = jnp.where(lane < LANES - 2, c[11], 0.0)
            coef.append(c)
        for v in range(nv):
            x = [lam_ref[v, a, SUB * h : SUB * (h + 1), :] for h in range(2)]
            moved = {o: [down(x[h], -o) for h in range(2)] for o in (-2, -1, 1, 2)}
            for half in range(2):
                rows = slice(SUB * half, SUB * (half + 1))
                c = coef[half]
                total = None
                for i, o in enumerate((-2, -1, 1, 2)):
                    if 0 <= a + o < na:
                        term = c[i] * lam_ref[v, a + o, rows, :]
                        total = term if total is None else total + term
                for i, o in enumerate((-2, -1, 1, 2)):
                    m = moved[o]
                    if o < 0:
                        y = m[0] if half == 0 else jnp.where(sub >= -o, m[1], m[0])
                    else:
                        y = m[1] if half == 1 else jnp.where(sub < SUB - o, m[0], m[1])
                    total = total + c[4 + i] * y
                for i, o in enumerate((-2, -1, 1, 2)):
                    total = total + c[8 + i] * along(x[half], -o)
                near_ref[v, a, rows, :] = total


def finish_kernel(faces, last, *refs):
    near_ref, couple_ref, jac_ref, src_ref, inv_ref, ahead_ref, back_ref, mate_ref, across_ref = refs[:9]
    face_refs = refs[9 : 9 + faces]
    rest = refs[9 + faces :]
    if faces:
        taps_ref, out_ref, rhs_ref = rest[0], rest[1], rest[2]
        rest = rest[3:]
    else:
        out_ref, rhs_ref = rest[0], src_ref
        rest = rest[1:]
    nv, na = near_ref.shape[:2]
    sub, lane = iotas()
    circs, rads = lax.axis_size("circ"), lax.axis_size("rad")
    me, rad = lax.axis_index("circ"), lax.axis_index("rad")
    even = me % 2 == 0
    has_low = rad > 0
    has_high = rad < rads - 1

    low_rows, high_rows = [], []
    for g in range(nv * na // 4):
        rows = slice(SUB * g, SUB * (g + 1))
        x, y = ahead_ref[rows, :], back_ref[rows, :]
        low_rows.append(jnp.where(even, x, y))
        high_rows.append(jnp.where(even, y, x))

    wide, slim = {}, {}
    for part in range(nv * na // GROUP):
        for half in range(2):
            at = SUB * (2 * part + half)
            x, y = mate_ref[at : at + SUB, :], across_ref[at : at + SUB, :]
            right = along(jnp.where(even, x, y), -2)
            left = along(jnp.where(even, y, x), 2)
            wide[part, half] = jnp.where(lane % 4 < 2, right, left)
            slim[part, half] = jnp.where(lane % 4 < 2, along(right, 1), along(left, -1))

    packer = None if last else Packer(na, nv)
    for a in range(na):
        for half in range(2):
            rows = slice(SUB * half, SUB * (half + 1))
            c = [couple_ref[i, a, rows, :] for i in range(4, 12)]
            if half == 0:
                far = jnp.where((sub < 2) & has_low, c[0], 0.0)
                nigh = jnp.where((sub < 1) & has_low, c[1], 0.0)
            else:
                far = jnp.where((sub >= SUB - 2) & has_high, c[3], 0.0)
                nigh = jnp.where((sub >= SUB - 1) & has_high, c[2], 0.0)
            outer = jnp.where(lane < 2, c[4], jnp.where(lane >= LANES - 2, c[7], 0.0))
            inner = jnp.where(lane < 1, c[5], jnp.where(lane >= LANES - 1, c[6], 0.0))
            near = []
            for v in range(nv):
                k = v * na + a
                j = k % 4
                if half == 0:
                    m = low_rows[k // 4]
                    y2, y1 = down(m, -2 * j), down(m, -2 * j - 1)
                else:
                    m = high_rows[k // 4]
                    y2, y1 = down(m, 6 - 2 * j), down(m, 7 - 2 * j)
                spot = 4 * (k % GROUP)
                key = (k // GROUP, half)
                total = near_ref[v, a, rows, :] + (far * y2 + nigh * y1)
                total = total + outer * along(wide[key], LANES - 2 - spot)
                total = total + inner * along(slim[key], LANES - 2 - spot)
                near.append(total)
            inv = inv_ref[a, rows, :]
            for s in range(nv):
                acc = src_ref[s, a, rows, :]
                if faces and a < 2:
                    for n, face_ref in enumerate(face_refs):
                        donor = (me if n % 2 == 0 else me + 1 - 2 * (me % 2)) - (n // 2) * 2
                        donor = lax.rem(donor + circs, circs)
                        f = [face_ref[s, a, SUB * h : SUB * (h + 1), :] for h in range(2)]
                        before = down(f[half], 1)
                        after = down(f[half], -1)
                        if half == 1:
                            before = jnp.where(sub >= 1, before, down(f[0], 1))
                        else:
                            after = jnp.where(sub < SUB - 1, after, down(f[1], -1))
                        acc = acc + taps_ref[donor, 0, rows, :] * after
                        acc = acc + taps_ref[donor, 1, rows, :] * f[half]
                        acc = acc + taps_ref[donor, 2, rows, :] * before
                if faces:
                    rhs_ref[s, a, rows, :] = acc
                for b in range(nv):
                    acc = acc + jac_ref[s, b, a, rows, :] * near[b]
                x = acc * inv
                out_ref[s, a, rows, :] = x
                if packer is not None:
                    packer.add(s, a, half, x)
    if packer is not None:
        packer.write(*rest)


def whole(count):
    return [pl.BlockSpec(memory_space=pltpu.VMEM)] * count


def call(kernel, outs, args, specs, name):
    specs = [pl.BlockSpec(memory_space=pltpu.VMEM)] * len(args) if specs is None else specs
    return pl.pallas_call(
        kernel,
        out_shape=outs,
        in_specs=specs,
        out_specs=whole(len(outs)),
        compiler_params=PARAMS,
        name=name,
    )(*args)


def solution(mesh):
    route = routes(mesh)
    vmem = lambda *shape: pltpu.VMEM(shape, jnp.float32)

    def sent(x, pairs):
        return lax.ppermute(x, AXES, pairs)

    def per_device(adjoint, source, jacobian, couple, donor_row, target_row, tile_count, weights):
        lam, src, jac, cpl = adjoint[0], source[0], jacobian[0], couple[0]
        nv, na, nr, nc = lam.shape
        slots = donor_row.shape[-1]
        edges = [vmem(2 * nv * na, nc), vmem(2 * nv * na, nc), vmem(4 * SUB, nc)]
        anyspec = pl.BlockSpec(memory_space=pl.ANY)
        vspec = pl.BlockSpec(memory_space=pltpu.VMEM)
        sspec = pl.BlockSpec(memory_space=pltpu.SMEM)

        *msgs, face = call(pack_kernel, edges + [vmem(nv, 2, nr, nc)], [lam], None, "pack")
        rhs, inv, faces, taps = src, None, [], None
        for sweep in range(SWEEPS):
            if sweep == 0:
                direct = [sent(face, pairs) for pairs in route["faces"]]
            ahead = sent(msgs[0], route["ahead"])
            back = sent(msgs[1], route["back"])
            across = sent(msgs[2], route["across"])
            mate = sent(msgs[2], route["mate"])
            first, last = sweep == 0, sweep == SWEEPS - 1
            outs = [vmem(nv, na, nr, nc)] + ([vmem(na, nr, nc)] if first else [])
            near, *more = call(
                lambda *refs, first=first: local_kernel(first, *refs),
                outs, [lam, cpl, mate], [vspec, vspec, anyspec], f"local{sweep}",
            )
            if first:
                inv = more[0]
                for x in direct:
                    faces += [x, sent(x, route["mate"])]
                taps = call(
                    taps_kernel,
                    [vmem(donor_row.shape[1], 3, nr, nc)],
                    [donor_row[0], target_row[0], tile_count[0],
                     weights.reshape(-1, nc), mate],
                    [sspec, sspec, sspec, vspec, anyspec], "taps",
                )[0]
            extra = faces + [taps] if first else []
            if last:
                outs = [jax.ShapeDtypeStruct((nv, na, nr, nc), jnp.float32)]
            else:
                outs = [vmem(nv, na, nr, nc)] + ([vmem(nv, na, nr, nc)] if first else []) + edges
            res = call(
                lambda *refs, n=len(faces) if first else 0, last=last: finish_kernel(n, last, *refs),
                outs, [near, cpl, jac, rhs, inv, ahead, back, mate, across] + extra, None, f"finish{sweep}",
            )
            lam = res[0]
            if first:
                rhs = res[1]
            msgs = res[2:] if first else res[1:]
        return lam[None]

    in_specs = (
        P("sec", None, None, "rad", "circ"),
        P("sec", None, None, "rad", "circ"),
        P("sec", None, None, None, "rad", "circ"),
        P("sec", None, None, "rad", "circ"),
        P("rad", None, None, None),
        P("rad", None, None, None),
        P("rad", None, None),
        P("rad", None, "circ", None, None),
    )
    out_specs = P("sec", None, None, "rad", "circ")
    return jax.shard_map(
        per_device, mesh=mesh, in_specs=in_specs, out_specs=out_specs, check_vma=False
    )
```

time: 93.3 us -> 34.7 us (0.37)
  waiting for transfers between devices: 46.5 us -> 10.2 us
  starting transfers between devices: 29.8 us -> 13 us
  other arithmetic: 7.75 us -> 0 us
  Pallas kernels: 0 us -> 4.63 us
  matrix products: 2.15 us -> 0 us
    ppermute x13 -> x16, waiting for transfers between devices: 46.5 us -> 10.2 us  [sent(): return lax.ppermute(x, AXES, pairs)]
    ppermute x13 -> x16, starting transfers between devices: 25.8 us -> 13 us  [sent(): return lax.ppermute(x, AXES, pairs)]
    unnamed x31 -> x20, local copies, waits for them, and re-layouts: 0.08 us -> 6.32 us
    pallas_call x0 -> x8, Pallas kernels: none -> 4.63 us  [call(): pl.pallas_call(kernel, out_shape=outs, in_specs=specs, out_specs=whole(le...]
    add x4 -> x0, other arithmetic: 4.53 us -> none  [the longest x3 3.9 us: sweep_once(): total = total + couple[:, index][:, None] * near[index]]
    all_to_all x1 -> x0, starting transfers between devices: 3.95 us -> none  [per_device(): lax.all_to_all(packed, 'circ', split_axis=0, concat_axis=0, tiled=True)]
    dot_general x2 -> x0, matrix products: 2.15 us -> none  [the longest x1 1.15 us: pick_rows(): jnp.einsum('nkr,xyrc->nkxyc', onehot, face, precision=lax.Precision.HIGHEST)]
    div x3 -> x0, other arithmetic: 2.09 us -> none  [sweep_once(): return (rhs + turned) / pivot[:, None]]
  transfers between devices with their start and end apart: 14 -> 16, of which waited for: 11 -> 9; matrix products, arithmetic and copies ran while one was open for 9% -> 0% of each run, Pallas kernels for 0% -> 6%
where the time goes in v1:
time: 34.7 us; the launch traced here: 34.3 us
  starting transfers between devices  13 us (37%)
  waiting for transfers between devices  10.2 us (29%)
  local copies, waits for them, and re-layouts  6.32 us (18%)
  Pallas kernels  4.63 us (13%)
    ppermute x16, starting transfers between devices, sent(): return lax.ppermute(x, AXES, pairs)  13 us
    ppermute x16, waiting for transfers between devices, sent(): return lax.ppermute(x, AXES, pairs)  10.2 us
    unnamed x20, local copies, waits for them, and re-layouts  6.32 us
    pallas_call x8, Pallas kernels, call(): pl.pallas_call(kernel, out_shape=outs, in_specs=specs, out_specs=whole(le...  4.63 us
  transfers between devices with their start and end apart: 16, of which 9 were waited for; matrix products, arithmetic and copies ran while one was open for 0% of the time, Pallas kernels for 6%

profile of v1, /device:TPU:0, one launch (start us, length us, event | category | flops | bytes accessed | tf_op | source)
XLA Modules:
  0.0 34.3 jit_solution(16007107229414263293)
XLA Ops:
  0.0 0.0 copy-start.4
  0.0 1.0 %copy-done.4 = f32[1,5,8,16,128]{4,3,2,1,0:T(8,128)S(1)} copy-done((f32[1,5,8,16,128]{4,3,2,1,0:T(8,128)S(1)}, f32[1,5,8,16,128]{4,3,2,1,0:T(8,128)}, u32[]{:S(2)}) %copy-start.4) | copy-done | bytes 327704
  1.0 0.0 copy-start.5
  1.0 0.1 pack.1
  1.1 4.0 %collective-permute-start.6 = (f32[5,2,16,128]{3,2,1,0:T(8,128)S(1)}, f32[5,2,16,128]{3,2,1,0:T(8,128)S(1)}, u32[]{:S(2)}, u32[]{:S(2)}) collective-permute-start(f32[5,2,16,128]{3,2,1,0:T(8,128)S(1)} %get-tuple-element.25), channel_id=1, source_target_pairs={{0,24},{1,25},{2,26},{3,27},{4,28},{5,29},{6,30},{7,31},{8,16},{9,... | collective-permute-start | bytes 245768 | tf_op jit(solution)/shard_map/ppermute | solution.py:287
  5.1 0.5 %collective-permute-start.4 = (f32[5,2,16,128]{3,2,1,0:T(8,128)S(1)}, f32[5,2,16,128]{3,2,1,0:T(8,128)S(1)}, u32[]{:S(2)}, u32[]{:S(2)}) collective-permute-start(f32[5,2,16,128]{3,2,1,0:T(8,128)S(1)} %get-tuple-element.25), channel_id=1, source_target_pairs={{0,16},{1,17},{2,18},{3,19},{4,20},{5,21},{6,22},{7,23},{8,24},{9,... | collective-permute-start | bytes 245768 | tf_op jit(solution)/shard_map/ppermute | solution.py:287
  5.6 2.0 %collective-permute-done.6.refs_11_ = f32[5,2,16,128]{3,2,1,0:T(8,128)S(1)} collective-permute-done((f32[5,2,16,128]{3,2,1,0:T(8,128)S(1)}, f32[5,2,16,128]{3,2,1,0:T(8,128)S(1)}, u32[]{:S(2)}, u32[]{:S(2)}) %collective-permute-start.6) | collective-permute-done | bytes 81952 | tf_op jit(solution)/shard_map/ppermute | solution.py:287
  7.6 0.0 collective-permute-start.7
  7.6 2.0 %collective-permute-done.4.refs_9_ = f32[5,2,16,128]{3,2,1,0:T(8,128)S(1)} collective-permute-done((f32[5,2,16,128]{3,2,1,0:T(8,128)S(1)}, f32[5,2,16,128]{3,2,1,0:T(8,128)S(1)}, u32[]{:S(2)}, u32[]{:S(2)}) %collective-permute-start.4) | collective-permute-done | bytes 81952 | tf_op jit(solution)/shard_map/ppermute | solution.py:287
  9.5 0.0 collective-permute-start.5
  9.5 1.8 %collective-permute-start.1 = (f32[80,128]{1,0:T(8,128)S(1)}, f32[80,128]{1,0:T(8,128)S(1)}, u32[]{:S(2)}, u32[]{:S(2)}) collective-permute-start(f32[80,128]{1,0:T(8,128)S(1)} %get-tuple-element.23), channel_id=1, source_target_pairs={{0,1},{1,2},{2,3},{3,7},{4,0},{5,4},{6,5},{7,6},{8,9},{9,10},{10,1... | collective-permute-start | bytes 122888 | tf_op jit(solution)/shard_map/ppermute | solution.py:287
  11.3 0.0 collective-permute-start.2
  11.3 0.2 collective-permute-start
  11.6 1.0 %collective-permute-done.refs_2_.after_ref.refs_7_ = f32[32,128]{1,0:T(8,128)S(1)} collective-permute-done((f32[32,128]{1,0:T(8,128)S(1)}, f32[32,128]{1,0:T(8,128)S(1)}, u32[]{:S(2)}, u32[]{:S(2)}) %collective-permute-start) | collective-permute-done | bytes 16416 | tf_op jit(solution)/shard_map/ppermute | solution.py:287
  12.5 1.2 %collective-permute-start.3 = (f32[32,128]{1,0:T(8,128)S(1)}, f32[32,128]{1,0:T(8,128)S(1)}, u32[]{:S(2)}, u32[]{:S(2)}) collective-permute-start(f32[32,128]{1,0:T(8,128)S(1)} %get-tuple-element.20), channel_id=1, source_target_pairs={{0,12},{1,13},{2,14},{3,15},{4,8},{5,9},{6,10},{7,11},{8,4},{9,5},... | collective-permute-start | bytes 49160 | tf_op jit(solution)/shard_map/ppermute | solution.py:287
  13.7 0.0 copy-start
  13.7 1.1 %copy-done = f32[1,12,8,16,128]{4,3,2,1,0:T(8,128)S(1)} copy-done((f32[1,12,8,16,128]{4,3,2,1,0:T(8,128)S(1)}, f32[1,12,8,16,128]{4,3,2,1,0:T(8,128)}, u32[]{:S(2)}) %copy-start) | copy-done | bytes 786456
  14.9 0.0 copy-start.1
  14.9 0.4 %local0.1 = (f32[5,8,16,128]{3,2,1,0:T(8,128)S(1)}, f32[8,16,128]{2,1,0:T(8,128)S(1)}) custom-call(f32[5,8,16,128]{3,2,1,0:T(8,128)S(1)} %bitcast.19, f32[12,8,16,128]{3,2,1,0:T(8,128)S(1)} %bitcast.9, f32[32,128]{1,0:T(8,128)S(1)} %collective-permute-done.refs_2_.after_ref.refs_7_), custom_call_target="tpu_custom_call" | custom-call | tf_op jit(solution)/shard_map/local0/pallas_call | solution.py:272
  15.3 0.0 copy-start.6
  15.3 0.7 %copy-done.6 = f32[1,4,1,6,128]{4,2,3,1,0:T(1,128)S(1)} copy-done((f32[1,4,1,6,128]{4,2,3,1,0:T(1,128)S(1)}, f32[1,4,1,6,128]{4,2,3,1,0:T(1,128)}, u32[]{:S(2)}) %copy-start.6) | copy-done | bytes 12312
  16.0 0.0 copy-start.7
  16.0 0.7 %copy-done.7 = s32[1,4,4,6]{3,2,1,0:T(4,128)S(1)} copy-done((s32[1,4,4,6]{3,2,1,0:T(4,128)S(1)}, s32[1,4,4,6]{3,2,1,0:T(4,128)}, u32[]{:S(2)}) %copy-start.7) | copy-done | bytes 408
  16.7 0.0 copy-start.8
  16.7 0.7 %copy-done.8 = s32[1,4,4,6]{3,2,1,0:T(4,128)S(1)} copy-done((s32[1,4,4,6]{3,2,1,0:T(4,128)S(1)}, s32[1,4,4,6]{3,2,1,0:T(4,128)}, u32[]{:S(2)}) %copy-start.8) | copy-done | bytes 408
  17.4 0.0 copy-start.9
  17.4 0.7 %copy-done.9 = s32[1,4,4]{2,1,0:T(4,128)S(1)} copy-done((s32[1,4,4]{2,1,0:T(4,128)S(1)}, s32[1,4,4]{2,1,0:T(4,128)}, u32[]{:S(2)}) %copy-start.9) | copy-done | bytes 88
  18.1 1.0 %taps.1.refs_13_ = f32[4,3,16,128]{3,2,1,0:T(8,128)S(1)} custom-call(s32[4,4,6]{2,1,0:T(4,128)S(1)} %bitcast.22, s32[4,4,6]{2,1,0:T(4,128)S(1)} %bitcast.23, s32[4,4]{1,0:T(4,128)S(1)} %bitcast.24, f32[24,128]{1,0:T(8,128)S(1)} %bitcast.21, f32[32,128]{1,0:T(8,128)S(1)} %collective-permute-done.refs_2_.after_ref.refs_7_), custom_call_target="tpu_custom_call" | custom-call | tf_op jit(solution)/shard_map/taps/pallas_call | solution.py:272
  19.1 0.0 collective-permute-done.3.refs_8_
  19.1 0.0 collective-permute-done.1.refs_5_
  19.1 0.0 collective-permute-done.2.refs_6_
  19.1 0.0 collective-permute-done.7.refs_12_
  19.1 0.0 collective-permute-done.5.refs_10_
  19.1 0.0 copy-done.5
  19.1 0.0 copy-done.1
  19.1 0.0 copy-start.2
  19.2 1.4 %copy-done.2 = f32[1,5,5,8,16,128]{5,4,3,2,1,0:T(8,128)S(1)} copy-done((f32[1,5,5,8,16,128]{5,4,3,2,1,0:T(8,128)S(1)}, f32[1,5,5,8,16,128]{5,4,3,2,1,0:T(8,128)}, u32[]{:S(2)}) %copy-start.2) | copy-done | bytes 1638424
  20.6 0.0 copy-start.3
  20.6 0.6 %finish0.1 = (f32[5,8,16,128]{3,2,1,0:T(8,128)S(1)}, f32[5,8,16,128]{3,2,1,0:T(8,128)S(1)}, f32[80,128]{1,0:T(8,128)S(1)}, f32[80,128]{1,0:T(8,128)S(1)}, f32[32,128]{1,0:T(8,128)S(1)}) custom-call(f32[5,8,16,128]{3,2,1,0:T(8,128)S(1)} %get-tuple-element.21.refs_0_, f32[12,8,16,128]{3,2,1,0:T(8,128)S(1)} %bitcast.10, f32[5,5,8,16,128]{4,3,2,1,0:T(8,128)S(1)} %bitcast.15, ...), custom_call_target="tpu_custom_call" | custom-call | tf_op jit(solution)/shard_map/finish0/pallas_call | solution.py:272
  21.2 1.8 %collective-permute-start.9 = (f32[80,128]{1,0:T(8,128)S(1)}, f32[80,128]{1,0:T(8,128)S(1)}, u32[]{:S(2)}, u32[]{:S(2)}) collective-permute-start(f32[80,128]{1,0:T(8,128)S(1)} %get-tuple-element.29), channel_id=1, source_target_pairs={{0,1},{1,2},{2,3},{3,7},{4,0},{5,4},{6,5},{7,6},{8,9},{9,10},{10,1... | collective-permute-start | bytes 122888 | tf_op jit(solution)/shard_map/ppermute | solution.py:287
  23.0 0.0 collective-permute-start.10
  23.0 0.1 collective-permute-start.8
  23.1 0.8 %collective-permute-start.11 = (f32[32,128]{1,0:T(8,128)S(1)}, f32[32,128]{1,0:T(8,128)S(1)}, u32[]{:S(2)}, u32[]{:S(2)}) collective-permute-start(f32[32,128]{1,0:T(8,128)S(1)} %get-tuple-element.27), channel_id=1, source_target_pairs={{0,12},{1,13},{2,14},{3,15},{4,8},{5,9},{6,10},{7,11},{8,4},{9,5},... | collective-permute-start | bytes 49160 | tf_op jit(solution)/shard_map/ppermute | solution.py:287
  23.9 0.3 collective-permute-done.8.refs_2_.refs_7_
  24.2 0.4 %local1.1.refs_0_ = f32[5,8,16,128]{3,2,1,0:T(8,128)S(1)} custom-call(f32[5,8,16,128]{3,2,1,0:T(8,128)S(1)} %get-tuple-element.26.refs_0_, f32[12,8,16,128]{3,2,1,0:T(8,128)S(1)} %bitcast.11, f32[32,128]{1,0:T(8,128)S(1)} %collective-permute-done.8.refs_2_.refs_7_), custom_call_target="tpu_custom_call" | custom-call | tf_op jit(solution)/shard_map/local1/pallas_call | solution.py:272
  24.6 1.6 %collective-permute-done.11.refs_8_ = f32[32,128]{1,0:T(8,128)S(1)} collective-permute-done((f32[32,128]{1,0:T(8,128)S(1)}, f32[32,128]{1,0:T(8,128)S(1)}, u32[]{:S(2)}, u32[]{:S(2)}) %collective-permute-start.11) | collective-permute-done | bytes 16416 | tf_op jit(solution)/shard_map/ppermute | solution.py:287
  26.2 0.0 collective-permute-done.9.refs_5_
  26.2 0.8 %collective-permute-done.10.refs_6_ = f32[80,128]{1,0:T(8,128)S(1)} collective-permute-done((f32[80,128]{1,0:T(8,128)S(1)}, f32[80,128]{1,0:T(8,128)S(1)}, u32[]{:S(2)}, u32[]{:S(2)}) %collective-permute-start.10) | collective-permute-done | bytes 40992 | tf_op jit(solution)/shard_map/ppermute | solution.py:287
  27.0 0.0 copy-done.3
  27.0 0.5 %finish1.1 = (f32[5,8,16,128]{3,2,1,0:T(8,128)S(1)}, f32[80,128]{1,0:T(8,128)S(1)}, f32[80,128]{1,0:T(8,128)S(1)}, f32[32,128]{1,0:T(8,128)S(1)}) custom-call(f32[5,8,16,128]{3,2,1,0:T(8,128)S(1)} %local1.1.refs_0_, f32[12,8,16,128]{3,2,1,0:T(8,128)S(1)} %bitcast.12, f32[5,5,8,16,128]{4,3,2,1,0:T(8,128)S(1)} %bitcast.16, ...), custom_call_target="tpu_custom_call" | custom-call | tf_op jit(solution)/shard_map/finish1/pallas_call | solution.py:272
  27.5 1.6 %collective-permute-start.13 = (f32[80,128]{1,0:T(8,128)S(1)}, f32[80,128]{1,0:T(8,128)S(1)}, u32[]{:S(2)}, u32[]{:S(2)}) collective-permute-start(f32[80,128]{1,0:T(8,128)S(1)} %get-tuple-element.33), channel_id=1, source_target_pairs={{0,1},{1,2},{2,3},{3,7},{4,0},{5,4},{6,5},{7,6},{8,9},{9,10},{10,1... | collective-permute-start | bytes 122888 | tf_op jit(solution)/shard_map/ppermute | solution.py:287
  29.1 0.0 collective-permute-start.14
  29.1 0.0 collective-permute-start.12
  29.1 0.9 %collective-permute-start.15 = (f32[32,128]{1,0:T(8,128)S(1)}, f32[32,128]{1,0:T(8,128)S(1)}, u32[]{:S(2)}, u32[]{:S(2)}) collective-permute-start(f32[32,128]{1,0:T(8,128)S(1)} %get-tuple-element.32), channel_id=1, source_target_pairs={{0,12},{1,13},{2,14},{3,15},{4,8},{5,9},{6,10},{7,11},{8,4},{9,5},... | collective-permute-start | bytes 49160 | tf_op jit(solution)/shard_map/ppermute | solution.py:287
  30.0 0.3 collective-permute-done.12.refs_2_.refs_7_
  30.3 0.4 %local2.1.refs_0_ = f32[5,8,16,128]{3,2,1,0:T(8,128)S(1)} custom-call(f32[5,8,16,128]{3,2,1,0:T(8,128)S(1)} %get-tuple-element.31.refs_0_, f32[12,8,16,128]{3,2,1,0:T(8,128)S(1)} %bitcast.13, f32[32,128]{1,0:T(8,128)S(1)} %collective-permute-done.12.refs_2_.refs_7_), custom_call_target="tpu_custom_call" | custom-call | tf_op jit(solution)/shard_map/local2/pallas_call | solution.py:272
  30.7 1.6 %collective-permute-done.15.refs_8_ = f32[32,128]{1,0:T(8,128)S(1)} collective-permute-done((f32[32,128]{1,0:T(8,128)S(1)}, f32[32,128]{1,0:T(8,128)S(1)}, u32[]{:S(2)}, u32[]{:S(2)}) %collective-permute-start.15) | collective-permute-done | bytes 16416 | tf_op jit(solution)/shard_map/ppermute | solution.py:287
  32.3 0.0 collective-permute-done.13.refs_5_
  32.3 0.8 %collective-permute-done.14.refs_6_ = f32[80,128]{1,0:T(8,128)S(1)} collective-permute-done((f32[80,128]{1,0:T(8,128)S(1)}, f32[80,128]{1,0:T(8,128)S(1)}, u32[]{:S(2)}, u32[]{:S(2)}) %collective-permute-start.14) | collective-permute-done | bytes 40992 | tf_op jit(solution)/shard_map/ppermute | solution.py:287
  33.1 1.2 %finish2.1 = f32[5,8,16,128]{3,2,1,0:T(8,128)} custom-call(f32[5,8,16,128]{3,2,1,0:T(8,128)S(1)} %local2.1.refs_0_, f32[12,8,16,128]{3,2,1,0:T(8,128)S(1)} %bitcast.14, f32[5,5,8,16,128]{4,3,2,1,0:T(8,128)S(1)} %bitcast.17, f32[5,8,16,128]{3,2,1,0:T(8,128)S(1)} %get-tuple-element.28.refs_3_, f32[8,16,128]{2,1,0:T(8,128)S(1)} %get-tuple-element.22.refs_4_, ...), custom_call_target="tpu_custom_call" | custom-call | tf_op jit(solution)/shard_map/finish2/pallas_call | solution.py:272
Async XLA Ops:
  0.0 1.0 %copy-start.4 = (f32[1,5,8,16,128]{4,3,2,1,0:T(8,128)S(1)}, f32[1,5,8,16,128]{4,3,2,1,0:T(8,128)}, u32[]{:S(2)}) copy-start(f32[1,5,8,16,128]{4,3,2,1,0:T(8,128)} %param.8) | copy-start | bytes 983044
  1.0 18.1 %copy-start.5 = (f32[1,5,8,16,128]{4,3,2,1,0:T(8,128)S(1)}, f32[1,5,8,16,128]{4,3,2,1,0:T(8,128)}, u32[]{:S(2)}) copy-start(f32[1,5,8,16,128]{4,3,2,1,0:T(8,128)} %param.9) | copy-start | bytes 983044
  1.1 6.4 %collective-permute-start.6 = (f32[5,2,16,128]{3,2,1,0:T(8,128)S(1)}, f32[5,2,16,128]{3,2,1,0:T(8,128)S(1)}, u32[]{:S(2)}, u32[]{:S(2)}) collective-permute-start(f32[5,2,16,128]{3,2,1,0:T(8,128)S(1)} %get-tuple-element.25), channel_id=1, source_target_pairs={{0,24},{1,25},{2,26},{3,27},{4,28},{5,29},{6,30},{7,31},{8,16},{9,... | collective-permute-start | bytes 245768 | tf_op jit(solution)/shard_map/ppermute | solution.py:287
  5.1 4.4 %collective-permute-start.4 = (f32[5,2,16,128]{3,2,1,0:T(8,128)S(1)}, f32[5,2,16,128]{3,2,1,0:T(8,128)S(1)}, u32[]{:S(2)}, u32[]{:S(2)}) collective-permute-start(f32[5,2,16,128]{3,2,1,0:T(8,128)S(1)} %get-tuple-element.25), channel_id=1, source_target_pairs={{0,16},{1,17},{2,18},{3,19},{4,20},{5,21},{6,22},{7,23},{8,24},{9,... | collective-permute-start | bytes 245768 | tf_op jit(solution)/shard_map/ppermute | solution.py:287
  7.6 11.5 %collective-permute-start.7 = (f32[5,2,16,128]{3,2,1,0:T(8,128)S(1)}, f32[5,2,16,128]{3,2,1,0:T(8,128)S(1)}, u32[]{:S(2)}, u32[]{:S(2)}) collective-permute-start(f32[5,2,16,128]{3,2,1,0:T(8,128)S(1)} %collective-permute-done.6.refs_11_), channel_id=1, source_target_pairs={{0,4},{1,5},{2,6},{3,7},{4,0},{5,1},{6,2},{7,3},{8,12},{9,13},{10,... | collective-permute-start | bytes 245768 | tf_op jit(solution)/shard_map/ppermute | solution.py:287
  9.5 9.6 %collective-permute-start.5 = (f32[5,2,16,128]{3,2,1,0:T(8,128)S(1)}, f32[5,2,16,128]{3,2,1,0:T(8,128)S(1)}, u32[]{:S(2)}, u32[]{:S(2)}) collective-permute-start(f32[5,2,16,128]{3,2,1,0:T(8,128)S(1)} %collective-permute-done.4.refs_9_), channel_id=1, source_target_pairs={{0,4},{1,5},{2,6},{3,7},{4,0},{5,1},{6,2},{7,3},{8,12},{9,13},{10,... | collective-permute-start | bytes 245768 | tf_op jit(solution)/shard_map/ppermute | solution.py:287
  9.5 9.5 %collective-permute-start.1 = (f32[80,128]{1,0:T(8,128)S(1)}, f32[80,128]{1,0:T(8,128)S(1)}, u32[]{:S(2)}, u32[]{:S(2)}) collective-permute-start(f32[80,128]{1,0:T(8,128)S(1)} %get-tuple-element.23), channel_id=1, source_target_pairs={{0,1},{1,2},{2,3},{3,7},{4,0},{5,4},{6,5},{7,6},{8,9},{9,10},{10,1... | collective-permute-start | bytes 122888 | tf_op jit(solution)/shard_map/ppermute | solution.py:287
  11.3 7.8 %collective-permute-start.2 = (f32[80,128]{1,0:T(8,128)S(1)}, f32[80,128]{1,0:T(8,128)S(1)}, u32[]{:S(2)}, u32[]{:S(2)}) collective-permute-start(f32[80,128]{1,0:T(8,128)S(1)} %get-tuple-element.24), channel_id=1, source_target_pairs={{1,0},{2,1},{3,2},{7,3},{0,4},{4,5},{5,6},{6,7},{9,8},{10,9},{11,1... | collective-permute-start | bytes 122888 | tf_op jit(solution)/shard_map/ppermute | solution.py:287
  11.3 1.2 %collective-permute-start = (f32[32,128]{1,0:T(8,128)S(1)}, f32[32,128]{1,0:T(8,128)S(1)}, u32[]{:S(2)}, u32[]{:S(2)}) collective-permute-start(f32[32,128]{1,0:T(8,128)S(1)} %get-tuple-element.20), channel_id=1, source_target_pairs={{0,4},{1,5},{2,6},{3,7},{4,0},{5,1},{6,2},{7,3},{8,12},{9,13},{10,... | collective-permute-start | bytes 49160 | tf_op jit(solution)/shard_map/ppermute | solution.py:287
  12.5 6.6 %collective-permute-start.3 = (f32[32,128]{1,0:T(8,128)S(1)}, f32[32,128]{1,0:T(8,128)S(1)}, u32[]{:S(2)}, u32[]{:S(2)}) collective-permute-start(f32[32,128]{1,0:T(8,128)S(1)} %get-tuple-element.20), channel_id=1, source_target_pairs={{0,12},{1,13},{2,14},{3,15},{4,8},{5,9},{6,10},{7,11},{8,4},{9,5},... | collective-permute-start | bytes 49160 | tf_op jit(solution)/shard_map/ppermute | solution.py:287
  13.7 1.1 %copy-start = (f32[1,12,8,16,128]{4,3,2,1,0:T(8,128)S(1)}, f32[1,12,8,16,128]{4,3,2,1,0:T(8,128)}, u32[]{:S(2)}) copy-start(f32[1,12,8,16,128]{4,3,2,1,0:T(8,128)} %param.11) | copy-start | bytes 2359300
  14.9 4.3 %copy-start.1 = (f32[1,12,8,16,128]{4,3,2,1,0:T(8,128)S(1)}, f32[1,12,8,16,128]{4,3,2,1,0:T(8,128)}, u32[]{:S(2)}) copy-start(f32[1,12,8,16,128]{4,3,2,1,0:T(8,128)} %param.11) | copy-start | bytes 2359300
  15.3 0.7 %copy-start.6 = (f32[1,4,1,6,128]{4,2,3,1,0:T(1,128)S(1)}, f32[1,4,1,6,128]{4,2,3,1,0:T(1,128)}, u32[]{:S(2)}) copy-start(f32[1,4,1,6,128]{4,2,3,1,0:T(1,128)} %param.15) | copy-start | bytes 36868
  16.0 0.7 %copy-start.7 = (s32[1,4,4,6]{3,2,1,0:T(4,128)S(1)}, s32[1,4,4,6]{3,2,1,0:T(4,128)}, u32[]{:S(2)}) copy-start(s32[1,4,4,6]{3,2,1,0:T(4,128)} %param.12) | copy-start | bytes 1156
  16.7 0.7 %copy-start.8 = (s32[1,4,4,6]{3,2,1,0:T(4,128)S(1)}, s32[1,4,4,6]{3,2,1,0:T(4,128)}, u32[]{:S(2)}) copy-start(s32[1,4,4,6]{3,2,1,0:T(4,128)} %param.13) | copy-start | bytes 1156
  17.4 0.7 %copy-start.9 = (s32[1,4,4]{2,1,0:T(4,128)S(1)}, s32[1,4,4]{2,1,0:T(4,128)}, u32[]{:S(2)}) copy-start(s32[1,4,4]{2,1,0:T(4,128)} %param.14) | copy-start | bytes 196
  19.1 1.4 %copy-start.2 = (f32[1,5,5,8,16,128]{5,4,3,2,1,0:T(8,128)S(1)}, f32[1,5,5,8,16,128]{5,4,3,2,1,0:T(8,128)}, u32[]{:S(2)}) copy-start(f32[1,5,5,8,16,128]{5,4,3,2,1,0:T(8,128)} %param.10) | copy-start | bytes 4915204
  20.6 6.4 %copy-start.3 = (f32[1,5,5,8,16,128]{5,4,3,2,1,0:T(8,128)S(1)}, f32[1,5,5,8,16,128]{5,4,3,2,1,0:T(8,128)}, u32[]{:S(2)}) copy-start(f32[1,5,5,8,16,128]{5,4,3,2,1,0:T(8,128)} %param.10) | copy-start | bytes 4915204
  21.2 5.1 %collective-permute-start.9 = (f32[80,128]{1,0:T(8,128)S(1)}, f32[80,128]{1,0:T(8,128)S(1)}, u32[]{:S(2)}, u32[]{:S(2)}) collective-permute-start(f32[80,128]{1,0:T(8,128)S(1)} %get-tuple-element.29), channel_id=1, source_target_pairs={{0,1},{1,2},{2,3},{3,7},{4,0},{5,4},{6,5},{7,6},{8,9},{9,10},{10,1... | collective-permute-start | bytes 122888 | tf_op jit(solution)/shard_map/ppermute | solution.py:287
  23.0 4.0 %collective-permute-start.10 = (f32[80,128]{1,0:T(8,128)S(1)}, f32[80,128]{1,0:T(8,128)S(1)}, u32[]{:S(2)}, u32[]{:S(2)}) collective-permute-start(f32[80,128]{1,0:T(8,128)S(1)} %get-tuple-element.30), channel_id=1, source_target_pairs={{1,0},{2,1},{3,2},{7,3},{0,4},{4,5},{5,6},{6,7},{9,8},{10,9},{11,1... | collective-permute-start | bytes 122888 | tf_op jit(solution)/shard_map/ppermute | solution.py:287
  23.0 1.2 %collective-permute-start.8 = (f32[32,128]{1,0:T(8,128)S(1)}, f32[32,128]{1,0:T(8,128)S(1)}, u32[]{:S(2)}, u32[]{:S(2)}) collective-permute-start(f32[32,128]{1,0:T(8,128)S(1)} %get-tuple-element.27), channel_id=1, source_target_pairs={{0,4},{1,5},{2,6},{3,7},{4,0},{5,1},{6,2},{7,3},{8,12},{9,13},{10,... | collective-permute-start | bytes 49160 | tf_op jit(solution)/shard_map/ppermute | solution.py:287
  23.1 3.2 %collective-permute-start.11 = (f32[32,128]{1,0:T(8,128)S(1)}, f32[32,128]{1,0:T(8,128)S(1)}, u32[]{:S(2)}, u32[]{:S(2)}) collective-permute-start(f32[32,128]{1,0:T(8,128)S(1)} %get-tuple-element.27), channel_id=1, source_target_pairs={{0,12},{1,13},{2,14},{3,15},{4,8},{5,9},{6,10},{7,11},{8,4},{9,5},... | collective-permute-start | bytes 49160 | tf_op jit(solution)/shard_map/ppermute | solution.py:287
  27.5 4.8 %collective-permute-start.13 = (f32[80,128]{1,0:T(8,128)S(1)}, f32[80,128]{1,0:T(8,128)S(1)}, u32[]{:S(2)}, u32[]{:S(2)}) collective-permute-start(f32[80,128]{1,0:T(8,128)S(1)} %get-tuple-element.33), channel_id=1, source_target_pairs={{0,1},{1,2},{2,3},{3,7},{4,0},{5,4},{6,5},{7,6},{8,9},{9,10},{10,1... | collective-permute-start | bytes 122888 | tf_op jit(solution)/shard_map/ppermute | solution.py:287
  29.1 4.0 %collective-permute-start.14 = (f32[80,128]{1,0:T(8,128)S(1)}, f32[80,128]{1,0:T(8,128)S(1)}, u32[]{:S(2)}, u32[]{:S(2)}) collective-permute-start(f32[80,128]{1,0:T(8,128)S(1)} %get-tuple-element.34), channel_id=1, source_target_pairs={{1,0},{2,1},{3,2},{7,3},{0,4},{4,5},{5,6},{6,7},{9,8},{10,9},{11,1... | collective-permute-start | bytes 122888 | tf_op jit(solution)/shard_map/ppermute | solution.py:287
  29.1 1.2 %collective-permute-start.12 = (f32[32,128]{1,0:T(8,128)S(1)}, f32[32,128]{1,0:T(8,128)S(1)}, u32[]{:S(2)}, u32[]{:S(2)}) collective-permute-start(f32[32,128]{1,0:T(8,128)S(1)} %get-tuple-element.32), channel_id=1, source_target_pairs={{0,4},{1,5},{2,6},{3,7},{4,0},{5,1},{6,2},{7,3},{8,12},{9,13},{10,... | collective-permute-start | bytes 49160 | tf_op jit(solution)/shard_map/ppermute | solution.py:287
  29.1 3.2 %collective-permute-start.15 = (f32[32,128]{1,0:T(8,128)S(1)}, f32[32,128]{1,0:T(8,128)S(1)}, u32[]{:S(2)}, u32[]{:S(2)}) collective-permute-start(f32[32,128]{1,0:T(8,128)S(1)} %get-tuple-element.32), channel_id=1, source_target_pairs={{0,12},{1,13},{2,14},{3,15},{4,8},{5,9},{6,10},{7,11},{8,4},{9,5},... | collective-permute-start | bytes 49160 | tf_op jit(solution)/shard_map/ppermute | solution.py:287

commit v2 on v1

--- a/solution.py
+++ b/solution.py
@@ -88,42 +88,49 @@
             cols_ref[at : at + SUB, :] = x
 
 
-def pack_kernel(lam_ref, ahead_ref, back_ref, cols_ref, face_ref):
-    nv, na = lam_ref.shape[:2]
+def pack_kernel(adjoint_ref, donors_in, ahead_ref, back_ref, cols_ref, *refs):
+    *tile_refs, lam_ref, donors_ref, sems = refs
+    nv, na, nr, _ = lam_ref.shape
+    listed = pltpu.make_async_copy(donors_in, donors_ref, sems.at[nv])
+    listed.start()
+    copies = [pltpu.make_async_copy(adjoint_ref.at[v], lam_ref.at[v], sems.at[v]) for v in range(nv)]
+    for copy in copies:
+        copy.start()
     packer = Packer(na, nv)
     for v in range(nv):
+        copies[v].wait()
         for a in range(na):
             for half in range(2):
-                rows = slice(SUB * half, SUB * (half + 1))
-                x = lam_ref[v, a, rows, :]
-                packer.add(v, a, half, x)
-                if a >= na - 2:
-                    face_ref[v, a - (na - 2), rows, :] = x
+                packer.add(v, a, half, lam_ref[v, a, SUB * half : SUB * (half + 1), :])
     packer.write(ahead_ref, back_ref, cols_ref)
-
-
-def taps_kernel(donors_ref, targets_ref, counts_ref, weights_ref, after_ref, taps_ref):
+    listed.wait()
+    me, circs, slots = lax.axis_index("circ"), donors_ref.shape[1], donors_ref.shape[2]
+    for n, tile_ref in enumerate(tile_refs):
+        reader = lax.rem(me + 2 * n, circs)
+        for part, to in enumerate((reader, reader + 1 - 2 * (reader % 2))):
+            for k in range(slots):
+                row = jnp.clip(donors_ref[me, to, k], 0, nr - 1)
+                for v in range(nv):
+                    for a in range(2):
+                        at = ((part * slots + k) * nv + v) * 2 + a
+                        tile_ref[at : at + 1, :] = lam_ref[v, na - 2 + a, pl.ds(row, 1), :]
+
+
+def place_weights(targets_ref, counts_ref, weights_ref, placed_ref):
     me = lax.axis_index("circ")
     stator = lax.axis_index("sec") == 1
     sub, _ = iotas()
-    slots = donors_ref.shape[-1]
-    for d in range(donors_ref.shape[0]):
-        acc = {(t, h): jnp.zeros((SUB, LANES), jnp.float32) for t in range(3) for h in range(2)}
+    slots = targets_ref.shape[-1]
+    for d in range(targets_ref.shape[0]):
         for k in range(slots):
             live = (k < counts_ref[d, me]) & stator
-            target = targets_ref[d, me, k]
-            step = target - donors_ref[d, me, k]
+            row = jnp.where(live, targets_ref[d, me, k], -1)
             w = jnp.broadcast_to(weights_ref[d * slots + k : d * slots + k + 1, :], (SUB, LANES))
-            for t in range(3):
-                row = jnp.where(live & (step == t - 1), target, -1)
-                for h in range(2):
-                    acc[t, h] += jnp.where(sub + SUB * h == row, w, 0.0)
-        for (t, h), x in acc.items():
-            taps_ref[d, t, SUB * h : SUB * (h + 1), :] = x
-
-
-def local_kernel(first, *refs):
-    lam_ref, couple_ref, _, near_ref = refs[:4]
+            for h in range(2):
+                placed_ref[d, k, SUB * h : SUB * (h + 1), :] = jnp.where(sub + SUB * h == row, w, 0.0)
+
+
+def local_sums(lam_ref, couple_ref, near_ref, inv_ref=None):
     nv, na = lam_ref.shape[:2]
     sub, lane = iotas()
     for a in range(na):
@@ -131,11 +138,11 @@
         for half in range(2):
             rows = slice(SUB * half, SUB * (half + 1))
             c = [couple_ref[i, a, rows, :] for i in range(12)]
-            if first:
+            if inv_ref is not None:
                 total = c[0]
                 for i in range(1, 12):
                     total = total + c[i]
-                refs[4][a, rows, :] = 1.0 / (1.0 + total)
+                inv_ref[a, rows, :] = 1.0 / (1.0 + total)
             if half == 0:
                 c[4] = jnp.where(sub >= 2, c[4], 0.0)
                 c[5] = jnp.where(sub >= 1, c[5], 0.0)
@@ -170,16 +177,62 @@
                 near_ref[v, a, rows, :] = total
 
 
+def work_kernel(*refs):
+    lam_ref, couple_in, jac_in, src_in, weights_in, targets_in, counts_in = refs[:7]
+    couple_ref, jac_ref, src_ref, near_ref, inv_ref, placed_ref = refs[7:13]
+    weights_ref, targets_ref, counts_ref, big, small = refs[13:]
+    wide = [
+        pltpu.make_async_copy(couple_in, couple_ref, big.at[0]),
+        pltpu.make_async_copy(src_in, src_ref, big.at[1]),
+    ] + [
+        pltpu.make_async_copy(jac_in.at[s], jac_ref.at[s], big.at[2 + s])
+        for s in range(jac_ref.shape[0])
+    ]
+    slim = [
+        pltpu.make_async_copy(weights_in, weights_ref, small.at[0]),
+        pltpu.make_async_copy(targets_in, targets_ref, small.at[1]),
+        pltpu.make_async_copy(counts_in, counts_ref, small.at[2]),
+    ]
+    for copy in slim + wide:
+        copy.start()
+    for copy in slim:
+        copy.wait()
+    place_weights(targets_ref, counts_ref, weights_ref, placed_ref)
+    wide[0].wait()
+    local_sums(lam_ref, couple_ref, near_ref, inv_ref)
+    for copy in wide[1:]:
+        copy.wait()
+
+
+def local_kernel(lam_ref, couple_ref, _, near_ref):
+    local_sums(lam_ref, couple_ref, near_ref)
+
+
+def relay_kernel(*refs):
+    cols_ref, *refs = refs
+    routes = len(refs) // 2
+    share = shares(routes)
+    for n, (tile_ref, out_ref) in enumerate(zip(refs[:routes], refs[routes:])):
+        half = tile_ref.shape[0] // 2
+        out_ref[share : share + half, :] = tile_ref[half:, :]
+        if share * n < cols_ref.shape[0]:
+            out_ref[:share, :] = cols_ref[share * n : share * (n + 1), :]
+
+
+def shares(routes):
+    return SUB * max(1, 4 // routes)
+
+
 def finish_kernel(faces, last, *refs):
-    near_ref, couple_ref, jac_ref, src_ref, inv_ref, ahead_ref, back_ref, mate_ref, across_ref = refs[:9]
-    face_refs = refs[9 : 9 + faces]
-    rest = refs[9 + faces :]
+    near_ref, couple_ref, jac_ref, src_ref, inv_ref, ahead_ref, back_ref, across_ref = refs[:8]
     if faces:
-        taps_ref, out_ref, rhs_ref = rest[0], rest[1], rest[2]
-        rest = rest[3:]
+        relayed, direct = refs[8 : 8 + faces], refs[8 + faces : 8 + 2 * faces]
+        placed_ref, out_ref, rhs_ref, *rest = refs[8 + 2 * faces :]
+        share = shares(faces)
+        mate_at = lambda at: relayed[at // share][at % share : at % share + SUB, :]
     else:
-        out_ref, rhs_ref = rest[0], src_ref
-        rest = rest[1:]
+        mate_ref, out_ref, *rest = refs[8:]
+        mate_at = lambda at: mate_ref[at : at + SUB, :]
     nv, na = near_ref.shape[:2]
     sub, lane = iotas()
     circs, rads = lax.axis_size("circ"), lax.axis_size("rad")
@@ -199,7 +252,7 @@
     for part in range(nv * na // GROUP):
         for half in range(2):
             at = SUB * (2 * part + half)
-            x, y = mate_ref[at : at + SUB, :], across_ref[at : at + SUB, :]
+            x, y = mate_at(at), across_ref[at : at + SUB, :]
             right = along(jnp.where(even, x, y), -2)
             left = along(jnp.where(even, y, x), 2)
             wide[part, half] = jnp.where(lane % 4 < 2, right, left)
@@ -238,19 +291,14 @@
             for s in range(nv):
                 acc = src_ref[s, a, rows, :]
                 if faces and a < 2:
-                    for n, face_ref in enumerate(face_refs):
-                        donor = (me if n % 2 == 0 else me + 1 - 2 * (me % 2)) - (n // 2) * 2
+                    sources = [(ref, 0, me - 2 * n) for n, ref in enumerate(direct)]
+                    sources += [(ref, share, me + 1 - 2 * (me % 2) - 2 * n) for n, ref in enumerate(relayed)]
+                    for tile_ref, start, donor in sources:
                         donor = lax.rem(donor + circs, circs)
-                        f = [face_ref[s, a, SUB * h : SUB * (h + 1), :] for h in range(2)]
-                        before = down(f[half], 1)
-                        after = down(f[half], -1)
-                        if half == 1:
-                            before = jnp.where(sub >= 1, before, down(f[0], 1))
-                        else:
-                            after = jnp.where(sub < SUB - 1, after, down(f[1], -1))
-                        acc = acc + taps_ref[donor, 0, rows, :] * after
-                        acc = acc + taps_ref[donor, 1, rows, :] * f[half]
-                        acc = acc + taps_ref[donor, 2, rows, :] * before
+                        for t in range(placed_ref.shape[1]):
+                            at = start + (t * nv + s) * 2 + a
+                            tile = jnp.broadcast_to(tile_ref[at : at + 1, :], (SUB, LANES))
+                            acc = acc + placed_ref[donor, t, rows, :] * tile
                 if faces:
                     rhs_ref[s, a, rows, :] = acc
                 for b in range(nv):
@@ -263,18 +311,18 @@
         packer.write(*rest)
 
 
-def whole(count):
-    return [pl.BlockSpec(memory_space=pltpu.VMEM)] * count
-
-
-def call(kernel, outs, args, specs, name):
-    specs = [pl.BlockSpec(memory_space=pltpu.VMEM)] * len(args) if specs is None else specs
+def call(kernel, name, outs, args, specs=None, scratch=(), us=1):
+    vmem = pl.BlockSpec(memory_space=pltpu.VMEM)
     return pl.pallas_call(
         kernel,
         out_shape=outs,
-        in_specs=specs,
-        out_specs=whole(len(outs)),
+        in_specs=[vmem] * len(args) if specs is None else specs,
+        out_specs=[vmem] * len(outs),
+        scratch_shapes=list(scratch),
         compiler_params=PARAMS,
+        cost_estimate=pl.CostEstimate(
+            flops=us * 1_000_000, bytes_accessed=us * 3_000_000, transcendentals=0
+        ),
         name=name,
     )(*args)
 
@@ -282,58 +330,69 @@
 def solution(mesh):
     route = routes(mesh)
     vmem = lambda *shape: pltpu.VMEM(shape, jnp.float32)
+    inside = pl.BlockSpec(memory_space=pltpu.VMEM)
+    outside = pl.BlockSpec(memory_space=pltpu.HBM)
+    far = lambda x: pltpu.with_memory_space_constraint(x, pltpu.HBM)
+    unread = pl.BlockSpec(memory_space=pl.ANY)
 
     def sent(x, pairs):
         return lax.ppermute(x, AXES, pairs)
 
     def per_device(adjoint, source, jacobian, couple, donor_row, target_row, tile_count, weights):
-        lam, src, jac, cpl = adjoint[0], source[0], jacobian[0], couple[0]
-        nv, na, nr, nc = lam.shape
-        slots = donor_row.shape[-1]
+        nv, na, nr, nc = adjoint.shape[1:]
+        donors, slots = donor_row.shape[2:]
         edges = [vmem(2 * nv * na, nc), vmem(2 * nv * na, nc), vmem(4 * SUB, nc)]
-        anyspec = pl.BlockSpec(memory_space=pl.ANY)
-        vspec = pl.BlockSpec(memory_space=pltpu.VMEM)
-        sspec = pl.BlockSpec(memory_space=pltpu.SMEM)
-
-        *msgs, face = call(pack_kernel, edges + [vmem(nv, 2, nr, nc)], [lam], None, "pack")
-        rhs, inv, faces, taps = src, None, [], None
+        count = len(route["faces"])
+        ahead, back, cols, *tiles, lam = call(
+            pack_kernel, "pack",
+            edges + [vmem(4 * slots * nv, nc)] * count + [vmem(nv, na, nr, nc)],
+            [far(adjoint[0]), far(donor_row[0])], [outside] * 2,
+            [pltpu.SMEM(donor_row.shape[1:], jnp.int32), pltpu.SemaphoreType.DMA((nv + 1,))],
+        )
+        rhs = None
         for sweep in range(SWEEPS):
-            if sweep == 0:
-                direct = [sent(face, pairs) for pairs in route["faces"]]
-            ahead = sent(msgs[0], route["ahead"])
-            back = sent(msgs[1], route["back"])
-            across = sent(msgs[2], route["across"])
-            mate = sent(msgs[2], route["mate"])
             first, last = sweep == 0, sweep == SWEEPS - 1
-            outs = [vmem(nv, na, nr, nc)] + ([vmem(na, nr, nc)] if first else [])
-            near, *more = call(
-                lambda *refs, first=first: local_kernel(first, *refs),
-                outs, [lam, cpl, mate], [vspec, vspec, anyspec], f"local{sweep}",
-            )
             if first:
-                inv = more[0]
-                for x in direct:
-                    faces += [x, sent(x, route["mate"])]
-                taps = call(
-                    taps_kernel,
-                    [vmem(donor_row.shape[1], 3, nr, nc)],
-                    [donor_row[0], target_row[0], tile_count[0],
-                     weights.reshape(-1, nc), mate],
-                    [sspec, sspec, sspec, vspec, anyspec], "taps",
+                tiles = [sent(x, pairs) for x, pairs in zip(tiles, route["faces"])]
+            ahead = sent(ahead, route["ahead"])
+            back = sent(back, route["back"])
+            across = sent(cols, route["across"])
+            if first:
+                relayed = call(
+                    relay_kernel, "relay", [vmem(shares(count) + 2 * slots * nv, nc)] * count, [cols, *tiles]
+                )
+                relayed = [sent(x, route["mate"]) for x in relayed]
+                cpl, jac, rhs, near, inv, placed = call(
+                    work_kernel, "work",
+                    [vmem(12, na, nr, nc), vmem(nv, nv, na, nr, nc), vmem(nv, na, nr, nc),
+                     vmem(nv, na, nr, nc), vmem(na, nr, nc), vmem(donors, slots, nr, nc)],
+                    [lam, *map(far, (couple[0], jacobian[0], source[0], weights.reshape(-1, nc),
+                                     target_row[0], tile_count[0]))],
+                    [inside] + [outside] * 6,
+                    [pltpu.VMEM((donors * slots, nc), jnp.float32),
+                     pltpu.SMEM(target_row.shape[1:], jnp.int32), pltpu.SMEM(tile_count.shape[1:], jnp.int32),
+                     pltpu.SemaphoreType.DMA((2 + nv,)), pltpu.SemaphoreType.DMA((3,))],
+                )
+                extra = relayed + tiles + [placed]
+            else:
+                mate = sent(cols, route["mate"])
+                extra = [mate]
+                near = call(
+                    local_kernel, f"local{sweep}", [vmem(nv, na, nr, nc)],
+                    [lam, cpl, mate], [inside, inside, unread],
                 )[0]
-            extra = faces + [taps] if first else []
             if last:
                 outs = [jax.ShapeDtypeStruct((nv, na, nr, nc), jnp.float32)]
             else:
-                outs = [vmem(nv, na, nr, nc)] + ([vmem(nv, na, nr, nc)] if first else []) + edges
-            res = call(
-                lambda *refs, n=len(faces) if first else 0, last=last: finish_kernel(n, last, *refs),
-                outs, [near, cpl, jac, rhs, inv, ahead, back, mate, across] + extra, None, f"finish{sweep}",
+                outs = [vmem(nv, na, nr, nc)] * (2 if first else 1) + edges
+            lam, *more = call(
+                lambda *refs, n=count if first else 0, last=last: finish_kernel(n, last, *refs),
+                f"finish{sweep}", outs, [near, cpl, jac, rhs, inv, ahead, back, across] + extra,
             )
-            lam = res[0]
             if first:
-                rhs = res[1]
-            msgs = res[2:] if first else res[1:]
+                rhs, *more = more
+            if not last:
+                ahead, back, cols = more
         return lam[None]
 
     in_specs = (

time: 34.7 us -> 27.3 us (0.79)
  local copies, waits for them, and re-layouts: 6.32 us -> 0 us
  waiting for transfers between devices: 10.2 us -> 6.1 us
  Pallas kernels: 4.63 us -> 6.77 us
  starting transfers between devices: 13 us -> 14.1 us
    unnamed x20 -> x0, local copies, waits for them, and re-layouts: 6.32 us -> none
    ppermute x16 -> x15, waiting for transfers between devices: 10.2 us -> 6.1 us  [sent(): return lax.ppermute(x, AXES, pairs)]
    pallas_call x8, Pallas kernels: 4.63 us -> 6.77 us  [call(): pl.pallas_call(kernel, out_shape=outs, in_specs=[vmem] * len(args) if spe...]
    ppermute x16 -> x15, starting transfers between devices: 13 us -> 14.1 us  [sent(): return lax.ppermute(x, AXES, pairs)]
  transfers between devices with their start and end apart: 16 -> 15, of which waited for: 9 -> 6; matrix products, arithmetic and copies ran while one was open for 0% -> 0% of each run, Pallas kernels for 6% -> 10%
where the time goes in v2:
time: 27.3 us; the launch traced here: 27.1 us
  starting transfers between devices  14.1 us (52%)
  Pallas kernels  6.77 us (25%)
  waiting for transfers between devices  6.1 us (22%)
    ppermute x15, starting transfers between devices, sent(): return lax.ppermute(x, AXES, pairs)  14.1 us
    pallas_call x8, Pallas kernels, call(): pl.pallas_call(kernel, out_shape=outs, in_specs=[vmem] * len(args) if spe...  6.77 us
    ppermute x15, waiting for transfers between devices, sent(): return lax.ppermute(x, AXES, pairs)  6.1 us
  transfers between devices with their start and end apart: 15, of which 6 were waited for; matrix products, arithmetic and copies ran while one was open for 0% of the time, Pallas kernels for 10%

profile of v2, /device:TPU:0, one launch (start us, length us, event | category | flops | bytes accessed | tf_op | source)
XLA Modules:
  0.0 27.1 jit_solution(6384756661084730511)
XLA Ops:
  0.0 1.5 %pack.1 = (f32[80,128]{1,0:T(8,128)S(1)}, f32[80,128]{1,0:T(8,128)S(1)}, f32[32,128]{1,0:T(8,128)S(1)}, f32[120,128]{1,0:T(8,128)S(1)}, f32[120,128]{1,0:T(8,128)S(1)}, /*index=5*/f32[5,8,16,128]{3,2,1,0:T(8,128)S(1)}) custom-call(f32[5,8,16,128]{3,2,1,0:T(8,128)} %bitcast.11, s32[4,4,6]{2,1,0:T(4,128)} %bitcast.15), custom_call_target="tpu_custom_call" | custom-call | flops 1000000 | bytes 3000000 | tf_op jit(solution)/shard_map/pack/pallas_call | solution.py:316
  1.5 3.0 %collective-permute-start.3 = (f32[120,128]{1,0:T(8,128)S(1)}, f32[120,128]{1,0:T(8,128)S(1)}, u32[]{:S(2)}, u32[]{:S(2)}) collective-permute-start(f32[120,128]{1,0:T(8,128)S(1)} %get-tuple-element.37), channel_id=1, source_target_pairs={{0,16},{1,17},{2,18},{3,19},{4,20},{5,21},{6,22},{7,23},{8,24},{9,... | collective-permute-start | bytes 184328 | tf_op jit(solution)/shard_map/ppermute | solution.py:339
  4.5 1.4 %collective-permute-start.4 = (f32[120,128]{1,0:T(8,128)S(1)}, f32[120,128]{1,0:T(8,128)S(1)}, u32[]{:S(2)}, u32[]{:S(2)}) collective-permute-start(f32[120,128]{1,0:T(8,128)S(1)} %get-tuple-element.38), channel_id=1, source_target_pairs={{0,24},{1,25},{2,26},{3,27},{4,28},{5,29},{6,30},{7,31},{8,16},{9,... | collective-permute-start | bytes 184328 | tf_op jit(solution)/shard_map/ppermute | solution.py:339
  5.9 1.6 %collective-permute-start = (f32[80,128]{1,0:T(8,128)S(1)}, f32[80,128]{1,0:T(8,128)S(1)}, u32[]{:S(2)}, u32[]{:S(2)}) collective-permute-start(f32[80,128]{1,0:T(8,128)S(1)} %get-tuple-element.34), channel_id=1, source_target_pairs={{0,1},{1,2},{2,3},{3,7},{4,0},{5,4},{6,5},{7,6},{8,9},{9,10},{10,1... | collective-permute-start | bytes 122888 | tf_op jit(solution)/shard_map/ppermute | solution.py:339
  7.5 0.0 collective-permute-start.1
  7.5 0.0 collective-permute-done.3.refs_1_.refs_10_
  7.5 2.1 %collective-permute-done.4.refs_2_.refs_11_ = f32[120,128]{1,0:T(8,128)S(1)} collective-permute-done((f32[120,128]{1,0:T(8,128)S(1)}, f32[120,128]{1,0:T(8,128)S(1)}, u32[]{:S(2)}, u32[]{:S(2)}) %collective-permute-start.4) | collective-permute-done | bytes 61472 | tf_op jit(solution)/shard_map/ppermute | solution.py:339
  9.6 0.0 collective-permute-start.5
  9.6 0.5 %collective-permute-start.6 = (f32[76,128]{1,0:T(8,128)S(1)}, f32[76,128]{1,0:T(8,128)S(1)}, u32[]{:S(2)}, u32[]{:S(2)}) collective-permute-start(f32[76,128]{1,0:T(8,128)S(1)} %get-tuple-element.40), channel_id=1, source_target_pairs={{0,4},{1,5},{2,6},{3,7},{4,0},{5,1},{6,2},{7,3},{8,12},{9,13},{10,... | collective-permute-start | bytes 116744 | tf_op jit(solution)/shard_map/ppermute | solution.py:339
  10.1 1.2 %collective-permute-start.2 = (f32[32,128]{1,0:T(8,128)S(1)}, f32[32,128]{1,0:T(8,128)S(1)}, u32[]{:S(2)}, u32[]{:S(2)}) collective-permute-start(f32[32,128]{1,0:T(8,128)S(1)} %get-tuple-element.36.refs_0_), channel_id=1, source_target_pairs={{0,12},{1,13},{2,14},{3,15},{4,8},{5,9},{6,10},{7,11},{8,4},{9,5},... | collective-permute-start | bytes 49160 | tf_op jit(solution)/shard_map/ppermute | solution.py:339
  11.3 1.9 %work.1 = (f32[12,8,16,128]{3,2,1,0:T(8,128)S(1)}, f32[5,5,8,16,128]{4,3,2,1,0:T(8,128)S(1)}, f32[5,8,16,128]{3,2,1,0:T(8,128)S(1)}, f32[5,8,16,128]{3,2,1,0:T(8...) custom-call(f32[5,8,16,128]{3,2,1,0:T(8,128)S(1)} %get-tuple-element.28.refs_0_, ...), custom_call_target="tpu_custom_call" | custom-call | flops 1000000 | bytes 3000000 | tf_op jit(solution)/shard_map/work/pallas_call | solution.py:316
  13.2 0.1 collective-permute-done.2.refs_7_
  13.3 0.0 collective-permute-done.refs_5_
  13.3 0.0 collective-permute-done.1.refs_6_
  13.3 0.0 collective-permute-done.5.refs_8_
  13.3 0.0 collective-permute-done.6.refs_9_
  13.3 0.8 %finish0.1 = (f32[5,8,16,128]{3,2,1,0:T(8,128)S(1)}, f32[5,8,16,128]{3,2,1,0:T(8,128)S(1)}, f32[80,128]{1,0:T(8,128)S(1)}, f32[80,128]{1,0:T(8,128)S(1)}, f32[32,128]{1,0:T(8,128)S(1)}) custom-call(f32[5,8,16,128]{3,2,1,0:T(8,128)S(1)} %get-tuple-element.29.refs_0_, f32[12,8,16,128]{3,2,1,0:T(8,128)S(1)} %get-tuple-element.30.refs_1_.couple_ref, ...), custom_call_target="tpu_custom_call" | custom-call | flops 1000000 | bytes 3000000 | tf_op jit(solution)/shard_map/finish0/pallas_call | solution.py:316
  14.1 1.6 %collective-permute-start.8 = (f32[80,128]{1,0:T(8,128)S(1)}, f32[80,128]{1,0:T(8,128)S(1)}, u32[]{:S(2)}, u32[]{:S(2)}) collective-permute-start(f32[80,128]{1,0:T(8,128)S(1)} %get-tuple-element.45), channel_id=1, source_target_pairs={{0,1},{1,2},{2,3},{3,7},{4,0},{5,4},{6,5},{7,6},{8,9},{9,10},{10,1... | collective-permute-start | bytes 122888 | tf_op jit(solution)/shard_map/ppermute | solution.py:339
  15.7 0.0 collective-permute-start.9
  15.7 0.3 %collective-permute-start.7 = (f32[32,128]{1,0:T(8,128)S(1)}, f32[32,128]{1,0:T(8,128)S(1)}, u32[]{:S(2)}, u32[]{:S(2)}) collective-permute-start(f32[32,128]{1,0:T(8,128)S(1)} %get-tuple-element.43), channel_id=1, source_target_pairs={{0,4},{1,5},{2,6},{3,7},{4,0},{5,1},{6,2},{7,3},{8,12},{9,13},{10,... | collective-permute-start | bytes 49160 | tf_op jit(solution)/shard_map/ppermute | solution.py:339
  16.0 1.3 %collective-permute-start.10 = (f32[32,128]{1,0:T(8,128)S(1)}, f32[32,128]{1,0:T(8,128)S(1)}, u32[]{:S(2)}, u32[]{:S(2)}) collective-permute-start(f32[32,128]{1,0:T(8,128)S(1)} %get-tuple-element.43), channel_id=1, source_target_pairs={{0,12},{1,13},{2,14},{3,15},{4,8},{5,9},{6,10},{7,11},{8,4},{9,5},... | collective-permute-start | bytes 49160 | tf_op jit(solution)/shard_map/ppermute | solution.py:339
  17.3 0.0 collective-permute-done.7._.refs_8_
  17.3 0.4 %local1.1.refs_0_ = f32[5,8,16,128]{3,2,1,0:T(8,128)S(1)} custom-call(f32[5,8,16,128]{3,2,1,0:T(8,128)S(1)} %get-tuple-element.42.lam_ref, f32[12,8,16,128]{3,2,1,0:T(8,128)S(1)} %get-tuple-element.30.refs_1_.couple_ref, f32[32,128]{1,0:T(8,128)S(1)} %collective-permute-done.7._.refs_8_), custom_call_target="tpu_custom_call" | custom-call | flops 1000000 | bytes 3000000 | tf_op jit(solution)/shard_map/local1/pallas_call | solution.py:316
  17.7 1.4 %collective-permute-done.10.refs_7_ = f32[32,128]{1,0:T(8,128)S(1)} collective-permute-done((f32[32,128]{1,0:T(8,128)S(1)}, f32[32,128]{1,0:T(8,128)S(1)}, u32[]{:S(2)}, u32[]{:S(2)}) %collective-permute-start.10) | collective-permute-done | bytes 16416 | tf_op jit(solution)/shard_map/ppermute | solution.py:339
  19.2 0.0 collective-permute-done.8.refs_5_
  19.2 0.5 %collective-permute-done.9.refs_6_ = f32[80,128]{1,0:T(8,128)S(1)} collective-permute-done((f32[80,128]{1,0:T(8,128)S(1)}, f32[80,128]{1,0:T(8,128)S(1)}, u32[]{:S(2)}, u32[]{:S(2)}) %collective-permute-start.9) | collective-permute-done | bytes 40992 | tf_op jit(solution)/shard_map/ppermute | solution.py:339
  19.7 0.6 %finish1.1 = (f32[5,8,16,128]{3,2,1,0:T(8,128)S(1)}, f32[80,128]{1,0:T(8,128)S(1)}, f32[80,128]{1,0:T(8,128)S(1)}, f32[32,128]{1,0:T(8,128)S(1)}) custom-call(f32[5,8,16,128]{3,2,1,0:T(8,128)S(1)} %local1.1.refs_0_, f32[12,8,16,128]{3,2,1,0:T(8,128)S(1)} %get-tuple-element.30.refs_1_.couple_ref, f32[5,5,8,16,128]{4,3,2,1,0:T(8,128)S(1)} %get-tuple-element.31.refs_2_, ...), custom_call_target="tpu_custom_call" | custom-call | flops 1000000 | bytes 3000000 | tf_op jit(solution)/shard_map/finish1/pallas_call | solution.py:316
  20.3 1.6 %collective-permute-start.12 = (f32[80,128]{1,0:T(8,128)S(1)}, f32[80,128]{1,0:T(8,128)S(1)}, u32[]{:S(2)}, u32[]{:S(2)}) collective-permute-start(f32[80,128]{1,0:T(8,128)S(1)} %get-tuple-element.49), channel_id=1, source_target_pairs={{0,1},{1,2},{2,3},{3,7},{4,0},{5,4},{6,5},{7,6},{8,9},{9,10},{10,1... | collective-permute-start | bytes 122888 | tf_op jit(solution)/shard_map/ppermute | solution.py:339
  21.9 0.0 collective-permute-start.13
  21.9 0.0 collective-permute-start.11
  21.9 1.6 %collective-permute-start.14 = (f32[32,128]{1,0:T(8,128)S(1)}, f32[32,128]{1,0:T(8,128)S(1)}, u32[]{:S(2)}, u32[]{:S(2)}) collective-permute-start(f32[32,128]{1,0:T(8,128)S(1)} %get-tuple-element.48), channel_id=1, source_target_pairs={{0,12},{1,13},{2,14},{3,15},{4,8},{5,9},{6,10},{7,11},{8,4},{9,5},... | collective-permute-start | bytes 49160 | tf_op jit(solution)/shard_map/ppermute | solution.py:339
  23.5 0.0 collective-permute-done.11._.refs_8_
  23.5 0.4 %local2.1.refs_0_ = f32[5,8,16,128]{3,2,1,0:T(8,128)S(1)} custom-call(f32[5,8,16,128]{3,2,1,0:T(8,128)S(1)} %get-tuple-element.47.lam_ref, f32[12,8,16,128]{3,2,1,0:T(8,128)S(1)} %get-tuple-element.30.refs_1_.couple_ref, f32[32,128]{1,0:T(8,128)S(1)} %collective-permute-done.11._.refs_8_), custom_call_target="tpu_custom_call" | custom-call | flops 1000000 | bytes 3000000 | tf_op jit(solution)/shard_map/local2/pallas_call | solution.py:316
  23.9 1.1 %collective-permute-done.14.refs_7_ = f32[32,128]{1,0:T(8,128)S(1)} collective-permute-done((f32[32,128]{1,0:T(8,128)S(1)}, f32[32,128]{1,0:T(8,128)S(1)}, u32[]{:S(2)}, u32[]{:S(2)}) %collective-permute-start.14) | collective-permute-done | bytes 16416 | tf_op jit(solution)/shard_map/ppermute | solution.py:339
  25.1 0.0 collective-permute-done.12.refs_5_
  25.1 0.8 %collective-permute-done.13.refs_6_ = f32[80,128]{1,0:T(8,128)S(1)} collective-permute-done((f32[80,128]{1,0:T(8,128)S(1)}, f32[80,128]{1,0:T(8,128)S(1)}, u32[]{:S(2)}, u32[]{:S(2)}) %collective-permute-start.13) | collective-permute-done | bytes 40992 | tf_op jit(solution)/shard_map/ppermute | solution.py:339
  25.9 1.2 %finish2.1 = f32[5,8,16,128]{3,2,1,0:T(8,128)} custom-call(f32[5,8,16,128]{3,2,1,0:T(8,128)S(1)} %local2.1.refs_0_, f32[12,8,16,128]{3,2,1,0:T(8,128)S(1)} %get-tuple-element.30.refs_1_.couple_ref, f32[5,5,8,16,128]{4,3,2,1,0:T(8,128)S(1)} %get-tuple-element.31.refs_2_, f32[5,8,16,128]{3,2,1,0:T(8,128)S(1)} %get-tuple-element.44.refs_3_, ...), custom_call_target="tpu_custom_call" | custom-call | flops 1000000 | bytes 3000000 | tf_op jit(solution)/shard_map/finish2/pallas_call | solution.py:316
  (1 shorter events, 0.0 us)
Async XLA Ops:
  1.5 6.0 %collective-permute-start.3 = (f32[120,128]{1,0:T(8,128)S(1)}, f32[120,128]{1,0:T(8,128)S(1)}, u32[]{:S(2)}, u32[]{:S(2)}) collective-permute-start(f32[120,128]{1,0:T(8,128)S(1)} %get-tuple-element.37), channel_id=1, source_target_pairs={{0,16},{1,17},{2,18},{3,19},{4,20},{5,21},{6,22},{7,23},{8,24},{9,... | collective-permute-start | bytes 184328 | tf_op jit(solution)/shard_map/ppermute | solution.py:339
  4.5 5.1 %collective-permute-start.4 = (f32[120,128]{1,0:T(8,128)S(1)}, f32[120,128]{1,0:T(8,128)S(1)}, u32[]{:S(2)}, u32[]{:S(2)}) collective-permute-start(f32[120,128]{1,0:T(8,128)S(1)} %get-tuple-element.38), channel_id=1, source_target_pairs={{0,24},{1,25},{2,26},{3,27},{4,28},{5,29},{6,30},{7,31},{8,16},{9,... | collective-permute-start | bytes 184328 | tf_op jit(solution)/shard_map/ppermute | solution.py:339
  5.9 7.4 %collective-permute-start = (f32[80,128]{1,0:T(8,128)S(1)}, f32[80,128]{1,0:T(8,128)S(1)}, u32[]{:S(2)}, u32[]{:S(2)}) collective-permute-start(f32[80,128]{1,0:T(8,128)S(1)} %get-tuple-element.34), channel_id=1, source_target_pairs={{0,1},{1,2},{2,3},{3,7},{4,0},{5,4},{6,5},{7,6},{8,9},{9,10},{10,1... | collective-permute-start | bytes 122888 | tf_op jit(solution)/shard_map/ppermute | solution.py:339
  7.5 5.8 %collective-permute-start.1 = (f32[80,128]{1,0:T(8,128)S(1)}, f32[80,128]{1,0:T(8,128)S(1)}, u32[]{:S(2)}, u32[]{:S(2)}) collective-permute-start(f32[80,128]{1,0:T(8,128)S(1)} %get-tuple-element.35), channel_id=1, source_target_pairs={{1,0},{2,1},{3,2},{7,3},{0,4},{4,5},{5,6},{6,7},{9,8},{10,9},{11,1... | collective-permute-start | bytes 122888 | tf_op jit(solution)/shard_map/ppermute | solution.py:339
  9.6 3.7 %collective-permute-start.5 = (f32[76,128]{1,0:T(8,128)S(1)}, f32[76,128]{1,0:T(8,128)S(1)}, u32[]{:S(2)}, u32[]{:S(2)}) collective-permute-start(f32[76,128]{1,0:T(8,128)S(1)} %get-tuple-element.39), channel_id=1, source_target_pairs={{0,4},{1,5},{2,6},{3,7},{4,0},{5,1},{6,2},{7,3},{8,12},{9,13},{10,... | collective-permute-start | bytes 116744 | tf_op jit(solution)/shard_map/ppermute | solution.py:339
  9.6 3.7 %collective-permute-start.6 = (f32[76,128]{1,0:T(8,128)S(1)}, f32[76,128]{1,0:T(8,128)S(1)}, u32[]{:S(2)}, u32[]{:S(2)}) collective-permute-start(f32[76,128]{1,0:T(8,128)S(1)} %get-tuple-element.40), channel_id=1, source_target_pairs={{0,4},{1,5},{2,6},{3,7},{4,0},{5,1},{6,2},{7,3},{8,12},{9,13},{10,... | collective-permute-start | bytes 116744 | tf_op jit(solution)/shard_map/ppermute | solution.py:339
  10.1 3.2 %collective-permute-start.2 = (f32[32,128]{1,0:T(8,128)S(1)}, f32[32,128]{1,0:T(8,128)S(1)}, u32[]{:S(2)}, u32[]{:S(2)}) collective-permute-start(f32[32,128]{1,0:T(8,128)S(1)} %get-tuple-element.36.refs_0_), channel_id=1, source_target_pairs={{0,12},{1,13},{2,14},{3,15},{4,8},{5,9},{6,10},{7,11},{8,4},{9,5},... | collective-permute-start | bytes 49160 | tf_op jit(solution)/shard_map/ppermute | solution.py:339
  14.1 5.1 %collective-permute-start.8 = (f32[80,128]{1,0:T(8,128)S(1)}, f32[80,128]{1,0:T(8,128)S(1)}, u32[]{:S(2)}, u32[]{:S(2)}) collective-permute-start(f32[80,128]{1,0:T(8,128)S(1)} %get-tuple-element.45), channel_id=1, source_target_pairs={{0,1},{1,2},{2,3},{3,7},{4,0},{5,4},{6,5},{7,6},{8,9},{9,10},{10,1... | collective-permute-start | bytes 122888 | tf_op jit(solution)/shard_map/ppermute | solution.py:339
  15.7 4.0 %collective-permute-start.9 = (f32[80,128]{1,0:T(8,128)S(1)}, f32[80,128]{1,0:T(8,128)S(1)}, u32[]{:S(2)}, u32[]{:S(2)}) collective-permute-start(f32[80,128]{1,0:T(8,128)S(1)} %get-tuple-element.46), channel_id=1, source_target_pairs={{1,0},{2,1},{3,2},{7,3},{0,4},{4,5},{5,6},{6,7},{9,8},{10,9},{11,1... | collective-permute-start | bytes 122888 | tf_op jit(solution)/shard_map/ppermute | solution.py:339
  15.7 1.6 %collective-permute-start.7 = (f32[32,128]{1,0:T(8,128)S(1)}, f32[32,128]{1,0:T(8,128)S(1)}, u32[]{:S(2)}, u32[]{:S(2)}) collective-permute-start(f32[32,128]{1,0:T(8,128)S(1)} %get-tuple-element.43), channel_id=1, source_target_pairs={{0,4},{1,5},{2,6},{3,7},{4,0},{5,1},{6,2},{7,3},{8,12},{9,13},{10,... | collective-permute-start | bytes 49160 | tf_op jit(solution)/shard_map/ppermute | solution.py:339
  16.0 3.2 %collective-permute-start.10 = (f32[32,128]{1,0:T(8,128)S(1)}, f32[32,128]{1,0:T(8,128)S(1)}, u32[]{:S(2)}, u32[]{:S(2)}) collective-permute-start(f32[32,128]{1,0:T(8,128)S(1)} %get-tuple-element.43), channel_id=1, source_target_pairs={{0,12},{1,13},{2,14},{3,15},{4,8},{5,9},{6,10},{7,11},{8,4},{9,5},... | collective-permute-start | bytes 49160 | tf_op jit(solution)/shard_map/ppermute | solution.py:339
  20.3 4.8 %collective-permute-start.12 = (f32[80,128]{1,0:T(8,128)S(1)}, f32[80,128]{1,0:T(8,128)S(1)}, u32[]{:S(2)}, u32[]{:S(2)}) collective-permute-start(f32[80,128]{1,0:T(8,128)S(1)} %get-tuple-element.49), channel_id=1, source_target_pairs={{0,1},{1,2},{2,3},{3,7},{4,0},{5,4},{6,5},{7,6},{8,9},{9,10},{10,1... | collective-permute-start | bytes 122888 | tf_op jit(solution)/shard_map/ppermute | solution.py:339
  21.9 4.0 %collective-permute-start.13 = (f32[80,128]{1,0:T(8,128)S(1)}, f32[80,128]{1,0:T(8,128)S(1)}, u32[]{:S(2)}, u32[]{:S(2)}) collective-permute-start(f32[80,128]{1,0:T(8,128)S(1)} %get-tuple-element.50), channel_id=1, source_target_pairs={{1,0},{2,1},{3,2},{7,3},{0,4},{4,5},{5,6},{6,7},{9,8},{10,9},{11,1... | collective-permute-start | bytes 122888 | tf_op jit(solution)/shard_map/ppermute | solution.py:339
  21.9 1.6 %collective-permute-start.11 = (f32[32,128]{1,0:T(8,128)S(1)}, f32[32,128]{1,0:T(8,128)S(1)}, u32[]{:S(2)}, u32[]{:S(2)}) collective-permute-start(f32[32,128]{1,0:T(8,128)S(1)} %get-tuple-element.48), channel_id=1, source_target_pairs={{0,4},{1,5},{2,6},{3,7},{4,0},{5,1},{6,2},{7,3},{8,12},{9,13},{10,... | collective-permute-start | bytes 49160 | tf_op jit(solution)/shard_map/ppermute | solution.py:339
  21.9 3.2 %collective-permute-start.14 = (f32[32,128]{1,0:T(8,128)S(1)}, f32[32,128]{1,0:T(8,128)S(1)}, u32[]{:S(2)}, u32[]{:S(2)}) collective-permute-start(f32[32,128]{1,0:T(8,128)S(1)} %get-tuple-element.48), channel_id=1, source_target_pairs={{0,12},{1,13},{2,14},{3,15},{4,8},{5,9},{6,10},{7,11},{8,4},{9,5},... | collective-permute-start | bytes 49160 | tf_op jit(solution)/shard_map/ppermute | solution.py:339

commit v3 on v2

--- a/solution.py
+++ b/solution.py
@@ -9,6 +9,7 @@
 AXES = ("sec", "circ", "rad")
 SUB, LANES = 8, 128
 GROUP = 20
+EARLY = 3
 PARAMS = pltpu.CompilerParams(vmem_limit_bytes=16 * 1024 * 1024)
 
 
@@ -24,15 +25,13 @@
             for r in range(rads)
         ]
 
-    def snake(s, c, r):
-        if c % 2 == 0:
-            return (s, c, r + 1) if r < rads - 1 else (s, c + 1, r)
-        return (s, c, r - 1) if r > 0 else (s, c - 1, r)
-
-    ahead = pairs(snake)
+    def swap(s, c, r, odd):
+        q = r + 1 if (r + odd) % 2 == 0 else r - 1
+        return (s, c, q) if 0 <= q < rads else (s, c ^ 1, r)
+
     return {
-        "ahead": ahead,
-        "back": [(b, a) for a, b in ahead],
+        "ahead": pairs(lambda s, c, r: swap(s, c, r, 0)),
+        "back": pairs(lambda s, c, r: swap(s, c, r, 1)),
         "mate": pairs(lambda s, c, r: (s, c ^ 1, r)),
         "across": pairs(lambda s, c, r: (s, (c - 1 if c % 2 == 0 else c + 1) % circs, r)),
         "faces": [
@@ -77,24 +76,35 @@
         inside = (self.lane >= spot) & (self.lane < spot + 4)
         self.put(self.cols, (k // GROUP, half), inside, along(x, spot + 2))
 
-    def write(self, ahead_ref, back_ref, cols_ref):
-        even = lax.axis_index("circ") % 2 == 0
+    def write(self, ahead_ref, back_ref, across_ref, mate_refs):
+        even = lax.axis_index("rad") % 2 == 0
         for g in range(len(self.low)):
             rows = slice(SUB * g, SUB * (g + 1))
             ahead_ref[rows, :] = jnp.where(even, self.high[g], self.low[g])
             back_ref[rows, :] = jnp.where(even, self.low[g], self.high[g])
-        for (part, half), x in self.cols.items():
-            at = SUB * (2 * part + half)
-            cols_ref[at : at + SUB, :] = x
-
-
-def pack_kernel(adjoint_ref, donors_in, ahead_ref, back_ref, cols_ref, *refs):
-    *tile_refs, lam_ref, donors_ref, sems = refs
+        even = lax.axis_index("circ") % 2 == 0
+        for half in range(2):
+            x, y = self.cols[0, half], self.cols[1, half]
+            right = jnp.where(self.lane % 4 < 2, x, along(y, 2))
+            left = jnp.where(self.lane % 4 < 2, along(y, -2), x)
+            rows = slice(SUB * half, SUB * (half + 1))
+            across_ref[rows, :] = jnp.where(even, left, right)
+            mate_refs[half][...] = jnp.where(even, right, left)
+
+
+def pack_kernel(adjoint_ref, donors_in, couple_in, src_in, jac_in, *refs):
+    ahead_ref, back_ref, across_ref, mate_ref, lam_ref, couple_ref, src_ref, jac_ref = refs[:8]
+    *tile_refs, donors_ref, sems, more_sems = refs[8:]
     nv, na, nr, _ = lam_ref.shape
     listed = pltpu.make_async_copy(donors_in, donors_ref, sems.at[nv])
     listed.start()
     copies = [pltpu.make_async_copy(adjoint_ref.at[v], lam_ref.at[v], sems.at[v]) for v in range(nv)]
-    for copy in copies:
+    later = [
+        pltpu.make_async_copy(couple_in, couple_ref, more_sems.at[0]),
+        pltpu.make_async_copy(src_in, src_ref, more_sems.at[1]),
+        pltpu.make_async_copy(jac_in.at[: jac_ref.shape[0]], jac_ref, more_sems.at[2]),
+    ]
+    for copy in copies + later:
         copy.start()
     packer = Packer(na, nv)
     for v in range(nv):
@@ -102,7 +112,7 @@
         for a in range(na):
             for half in range(2):
                 packer.add(v, a, half, lam_ref[v, a, SUB * half : SUB * (half + 1), :])
-    packer.write(ahead_ref, back_ref, cols_ref)
+    packer.write(ahead_ref, back_ref, across_ref, [mate_ref.at[:SUB], mate_ref.at[SUB:]])
     listed.wait()
     me, circs, slots = lax.axis_index("circ"), donors_ref.shape[1], donors_ref.shape[2]
     for n, tile_ref in enumerate(tile_refs):
@@ -114,6 +124,8 @@
                     for a in range(2):
                         at = ((part * slots + k) * nv + v) * 2 + a
                         tile_ref[at : at + 1, :] = lam_ref[v, na - 2 + a, pl.ds(row, 1), :]
+    for copy in later:
+        copy.wait()
 
 
 def place_weights(targets_ref, counts_ref, weights_ref, placed_ref):
@@ -178,33 +190,26 @@
 
 
 def work_kernel(*refs):
-    lam_ref, couple_in, jac_in, src_in, weights_in, targets_in, counts_in = refs[:7]
-    couple_ref, jac_ref, src_ref, near_ref, inv_ref, placed_ref = refs[7:13]
-    weights_ref, targets_ref, counts_ref, big, small = refs[13:]
-    wide = [
-        pltpu.make_async_copy(couple_in, couple_ref, big.at[0]),
-        pltpu.make_async_copy(src_in, src_ref, big.at[1]),
-    ] + [
-        pltpu.make_async_copy(jac_in.at[s], jac_ref.at[s], big.at[2 + s])
-        for s in range(jac_ref.shape[0])
+    lam_ref, couple_ref, jac_in, weights_in, targets_in, counts_in = refs[:6]
+    jac_ref, near_ref, inv_ref, placed_ref = refs[6:10]
+    weights_ref, targets_ref, counts_ref, sems = refs[10:]
+    count = jac_ref.shape[0]
+    wide = pltpu.make_async_copy(jac_in.at[jac_in.shape[0] - count :], jac_ref, sems.at[0])
+    slim = [
+        pltpu.make_async_copy(weights_in, weights_ref, sems.at[1]),
+        pltpu.make_async_copy(targets_in, targets_ref, sems.at[2]),
+        pltpu.make_async_copy(counts_in, counts_ref, sems.at[3]),
     ]
-    slim = [
-        pltpu.make_async_copy(weights_in, weights_ref, small.at[0]),
-        pltpu.make_async_copy(targets_in, targets_ref, small.at[1]),
-        pltpu.make_async_copy(counts_in, counts_ref, small.at[2]),
-    ]
-    for copy in slim + wide:
+    for copy in slim + [wide]:
         copy.start()
+    local_sums(lam_ref, couple_ref, near_ref, inv_ref)
     for copy in slim:
         copy.wait()
     place_weights(targets_ref, counts_ref, weights_ref, placed_ref)
-    wide[0].wait()
-    local_sums(lam_ref, couple_ref, near_ref, inv_ref)
-    for copy in wide[1:]:
-        copy.wait()
-
-
-def local_kernel(lam_ref, couple_ref, _, near_ref):
+    wide.wait()
+
+
+def local_kernel(lam_ref, couple_ref, near_ref):
     local_sums(lam_ref, couple_ref, near_ref)
 
 
@@ -220,24 +225,27 @@
 
 
 def shares(routes):
-    return SUB * max(1, 4 // routes)
+    return SUB * max(1, 2 // routes)
 
 
 def finish_kernel(faces, last, *refs):
-    near_ref, couple_ref, jac_ref, src_ref, inv_ref, ahead_ref, back_ref, across_ref = refs[:8]
+    near_ref, couple_ref, jac_first, jac_rest, src_ref, inv_ref, ahead_ref, back_ref, across_ref = refs[:9]
+    jac = lambda s: (jac_first, s) if s < jac_first.shape[0] else (jac_rest, s - jac_first.shape[0])
     if faces:
-        relayed, direct = refs[8 : 8 + faces], refs[8 + faces : 8 + 2 * faces]
-        placed_ref, out_ref, rhs_ref, *rest = refs[8 + 2 * faces :]
+        relayed, direct = refs[9 : 9 + faces], refs[9 + faces : 9 + 2 * faces]
+        placed_ref, out_ref, rhs_ref, *rest = refs[9 + 2 * faces :]
         share = shares(faces)
         mate_at = lambda at: relayed[at // share][at % share : at % share + SUB, :]
     else:
-        mate_ref, out_ref, *rest = refs[8:]
+        mate_ref, out_ref, *rest = refs[9:]
         mate_at = lambda at: mate_ref[at : at + SUB, :]
+    if last:
+        result_ref, out_ref, sems = out_ref, *rest
+        copies = []
     nv, na = near_ref.shape[:2]
     sub, lane = iotas()
     circs, rads = lax.axis_size("circ"), lax.axis_size("rad")
     me, rad = lax.axis_index("circ"), lax.axis_index("rad")
-    even = me % 2 == 0
     has_low = rad > 0
     has_high = rad < rads - 1
 
@@ -245,18 +253,18 @@
     for g in range(nv * na // 4):
         rows = slice(SUB * g, SUB * (g + 1))
         x, y = ahead_ref[rows, :], back_ref[rows, :]
-        low_rows.append(jnp.where(even, x, y))
-        high_rows.append(jnp.where(even, y, x))
+        low_rows.append(jnp.where(rad % 2 == 0, y, x))
+        high_rows.append(jnp.where(rad % 2 == 0, x, y))
 
     wide, slim = {}, {}
-    for part in range(nv * na // GROUP):
-        for half in range(2):
-            at = SUB * (2 * part + half)
-            x, y = mate_at(at), across_ref[at : at + SUB, :]
-            right = along(jnp.where(even, x, y), -2)
-            left = along(jnp.where(even, y, x), 2)
-            wide[part, half] = jnp.where(lane % 4 < 2, right, left)
-            slim[part, half] = jnp.where(lane % 4 < 2, along(right, 1), along(left, -1))
+    for half in range(2):
+        at = SUB * half
+        x, y = mate_at(at), across_ref[at : at + SUB, :]
+        right = jnp.where(me % 2 == 0, x, y)
+        left = jnp.where(me % 2 == 0, y, x)
+        for part, (r, l) in enumerate(((along(right, -2), along(left, 2)), (right, left))):
+            wide[part, half] = jnp.where(lane % 4 < 2, r, l)
+            slim[part, half] = jnp.where(lane % 4 < 2, along(r, 1), along(l, -1))
 
     packer = None if last else Packer(na, nv)
     for a in range(na):
@@ -301,23 +309,32 @@
                             acc = acc + placed_ref[donor, t, rows, :] * tile
                 if faces:
                     rhs_ref[s, a, rows, :] = acc
+                jac_ref, row = jac(s)
                 for b in range(nv):
-                    acc = acc + jac_ref[s, b, a, rows, :] * near[b]
+                    acc = acc + jac_ref[row, b, a, rows, :] * near[b]
                 x = acc * inv
                 out_ref[s, a, rows, :] = x
                 if packer is not None:
                     packer.add(s, a, half, x)
-    if packer is not None:
-        packer.write(*rest)
-
-
-def call(kernel, name, outs, args, specs=None, scratch=(), us=1):
+        if last:
+            copy = pltpu.make_async_copy(out_ref.at[:, a], result_ref.at[:, a], sems.at[a])
+            copy.start()
+            copies.append(copy)
+    if last:
+        for copy in copies:
+            copy.wait()
+    else:
+        ahead_to, back_to, across_to, mate_to = rest
+        packer.write(ahead_to, back_to, across_to, [mate_to.at[:SUB], mate_to.at[SUB:]])
+
+
+def call(kernel, name, outs, args, specs=None, scratch=(), us=1, out_specs=None):
     vmem = pl.BlockSpec(memory_space=pltpu.VMEM)
     return pl.pallas_call(
         kernel,
         out_shape=outs,
         in_specs=[vmem] * len(args) if specs is None else specs,
-        out_specs=[vmem] * len(outs),
+        out_specs=[vmem] * len(outs) if out_specs is None else out_specs,
         scratch_shapes=list(scratch),
         compiler_params=PARAMS,
         cost_estimate=pl.CostEstimate(
@@ -333,7 +350,6 @@
     inside = pl.BlockSpec(memory_space=pltpu.VMEM)
     outside = pl.BlockSpec(memory_space=pltpu.HBM)
     far = lambda x: pltpu.with_memory_space_constraint(x, pltpu.HBM)
-    unread = pl.BlockSpec(memory_space=pl.ANY)
 
     def sent(x, pairs):
         return lax.ppermute(x, AXES, pairs)
@@ -341,37 +357,39 @@
     def per_device(adjoint, source, jacobian, couple, donor_row, target_row, tile_count, weights):
         nv, na, nr, nc = adjoint.shape[1:]
         donors, slots = donor_row.shape[2:]
-        edges = [vmem(2 * nv * na, nc), vmem(2 * nv * na, nc), vmem(4 * SUB, nc)]
         count = len(route["faces"])
-        ahead, back, cols, *tiles, lam = call(
+        sides = 2 * nv * na
+        edges = lambda across: [vmem(sides + SUB, nc), vmem(sides, nc), vmem(across, nc), vmem(nr, nc)]
+        early = EARLY
+        ahead, back, cross, cols, lam, cpl, rhs, jac_first, *tiles = call(
             pack_kernel, "pack",
-            edges + [vmem(4 * slots * nv, nc)] * count + [vmem(nv, na, nr, nc)],
-            [far(adjoint[0]), far(donor_row[0])], [outside] * 2,
-            [pltpu.SMEM(donor_row.shape[1:], jnp.int32), pltpu.SemaphoreType.DMA((nv + 1,))],
+            edges(sides - SUB) + [vmem(nv, na, nr, nc), vmem(12, na, nr, nc), vmem(nv, na, nr, nc),
+                                  vmem(early, nv, na, nr, nc)] + [vmem(4 * slots * nv, nc)] * count,
+            [far(adjoint[0]), far(donor_row[0]), far(couple[0]), far(source[0]), far(jacobian[0])], [outside] * 5,
+            [pltpu.SMEM(donor_row.shape[1:], jnp.int32), pltpu.SemaphoreType.DMA((nv + 1,)),
+             pltpu.SemaphoreType.DMA((3,))],
         )
-        rhs = None
         for sweep in range(SWEEPS):
             first, last = sweep == 0, sweep == SWEEPS - 1
             if first:
                 tiles = [sent(x, pairs) for x, pairs in zip(tiles, route["faces"])]
             ahead = sent(ahead, route["ahead"])
             back = sent(back, route["back"])
-            across = sent(cols, route["across"])
+            across = sent(cross, route["across"])
             if first:
                 relayed = call(
                     relay_kernel, "relay", [vmem(shares(count) + 2 * slots * nv, nc)] * count, [cols, *tiles]
                 )
                 relayed = [sent(x, route["mate"]) for x in relayed]
-                cpl, jac, rhs, near, inv, placed = call(
+                jac_rest, near, inv, placed = call(
                     work_kernel, "work",
-                    [vmem(12, na, nr, nc), vmem(nv, nv, na, nr, nc), vmem(nv, na, nr, nc),
-                     vmem(nv, na, nr, nc), vmem(na, nr, nc), vmem(donors, slots, nr, nc)],
-                    [lam, *map(far, (couple[0], jacobian[0], source[0], weights.reshape(-1, nc),
-                                     target_row[0], tile_count[0]))],
-                    [inside] + [outside] * 6,
+                    [vmem(nv - early, nv, na, nr, nc), vmem(nv, na, nr, nc), vmem(na, nr, nc),
+                     vmem(donors, slots, nr, nc)],
+                    [lam, cpl, *map(far, (jacobian[0], weights.reshape(-1, nc), target_row[0], tile_count[0]))],
+                    [inside] * 2 + [outside] * 4,
                     [pltpu.VMEM((donors * slots, nc), jnp.float32),
                      pltpu.SMEM(target_row.shape[1:], jnp.int32), pltpu.SMEM(tile_count.shape[1:], jnp.int32),
-                     pltpu.SemaphoreType.DMA((2 + nv,)), pltpu.SemaphoreType.DMA((3,))],
+                     pltpu.SemaphoreType.DMA((4,))],
                 )
                 extra = relayed + tiles + [placed]
             else:
@@ -379,20 +397,24 @@
                 extra = [mate]
                 near = call(
                     local_kernel, f"local{sweep}", [vmem(nv, na, nr, nc)],
-                    [lam, cpl, mate], [inside, inside, unread],
+                    [lam, cpl],
                 )[0]
+            scratch, spaces = [], None
             if last:
-                outs = [jax.ShapeDtypeStruct((nv, na, nr, nc), jnp.float32)]
+                outs, spaces = [jax.ShapeDtypeStruct((nv, na, nr, nc), jnp.float32)], [outside]
+                scratch = [pltpu.VMEM((nv, na, nr, nc), jnp.float32), pltpu.SemaphoreType.DMA((na,))]
             else:
-                outs = [vmem(nv, na, nr, nc)] * (2 if first else 1) + edges
+                outs = [vmem(nv, na, nr, nc)] * (2 if first else 1) + edges(nr + SUB)
             lam, *more = call(
                 lambda *refs, n=count if first else 0, last=last: finish_kernel(n, last, *refs),
-                f"finish{sweep}", outs, [near, cpl, jac, rhs, inv, ahead, back, across] + extra,
+                f"finish{sweep}", outs,
+                [near, cpl, jac_first, jac_rest, rhs, inv, ahead, back, across] + extra,
+                None, scratch, 1, spaces,
             )
             if first:
                 rhs, *more = more
             if not last:
-                ahead, back, cols = more
+                ahead, back, cross, cols = more
         return lam[None]
 
     in_specs = (

time: 27.3 us -> 25.5 us (0.934)
  waiting for transfers between devices: 6.1 us -> 4.18 us
  starting transfers between devices: 14.1 us -> 14.9 us
  Pallas kernels: 6.77 us -> 6.13 us
    ppermute x15, waiting for transfers between devices: 6.1 us -> 4.18 us  [sent(): return lax.ppermute(x, AXES, pairs)]
    ppermute x15, starting transfers between devices: 14.1 us -> 14.9 us  [sent(): return lax.ppermute(x, AXES, pairs)]
    pallas_call x8, Pallas kernels: 6.77 us -> 6.13 us  [call(): pl.pallas_call(kernel, out_shape=outs, in_specs=[vmem] * len(args) if spe...]
  transfers between devices with their start and end apart: 15 -> 15, of which waited for: 6 -> 5; matrix products, arithmetic and copies ran while one was open for 0% -> 0% of each run, Pallas kernels for 10% -> 8%
where the time goes in v3:
time: 25.5 us; the launch traced here: 25.3 us
  starting transfers between devices  14.9 us (58%)
  Pallas kernels  6.13 us (24%)
  waiting for transfers between devices  4.18 us (16%)
    ppermute x15, starting transfers between devices, sent(): return lax.ppermute(x, AXES, pairs)  14.9 us
    pallas_call x8, Pallas kernels, call(): pl.pallas_call(kernel, out_shape=outs, in_specs=[vmem] * len(args) if spe...  6.13 us
    ppermute x15, waiting for transfers between devices, sent(): return lax.ppermute(x, AXES, pairs)  4.18 us
  transfers between devices with their start and end apart: 15, of which 5 were waited for; matrix products, arithmetic and copies ran while one was open for 0% of the time, Pallas kernels for 8%

profile of v3, /device:TPU:0, one launch (start us, length us, event | category | flops | bytes accessed | tf_op | source)
XLA Modules:
  0.0 25.3 jit_solution(2668239893651938890)
XLA Ops:
  0.0 1.8 %pack.1 = (f32[88,128]{1,0:T(8,128)S(1)}, f32[80,128]{1,0:T(8,128)S(1)}, f32[72,128]{1,0:T(8,128)S(1)}, f32[16,128]{1,0:T(8,128)S(1)}, f32[5,8,16,128]{3,2,1,0:T...) custom-call(f32[5,8,16,128]{3,2,1,0:T(8,128)} %bitcast.12, ...), custom_call_target="tpu_custom_call" | custom-call | flops 1000000 | bytes 3000000 | tf_op jit(solution)/shard_map/pack/pallas_call | solution.py:333
  1.8 3.0 %collective-permute-start.3 = (f32[120,128]{1,0:T(8,128)S(1)}, f32[120,128]{1,0:T(8,128)S(1)}, u32[]{:S(2)}, u32[]{:S(2)}) collective-permute-start(f32[120,128]{1,0:T(8,128)S(1)} %get-tuple-element.43), channel_id=1, source_target_pairs={{0,16},{1,17},{2,18},{3,19},{4,20},{5,21},{6,22},{7,23},{8,24},{9,... | collective-permute-start | bytes 184328 | tf_op jit(solution)/shard_map/ppermute | solution.py:355
  4.8 1.4 %collective-permute-start.4 = (f32[120,128]{1,0:T(8,128)S(1)}, f32[120,128]{1,0:T(8,128)S(1)}, u32[]{:S(2)}, u32[]{:S(2)}) collective-permute-start(f32[120,128]{1,0:T(8,128)S(1)} %get-tuple-element.44), channel_id=1, source_target_pairs={{0,24},{1,25},{2,26},{3,27},{4,28},{5,29},{6,30},{7,31},{8,16},{9,... | collective-permute-start | bytes 184328 | tf_op jit(solution)/shard_map/ppermute | solution.py:355
  6.2 1.6 %collective-permute-start = (f32[88,128]{1,0:T(8,128)S(1)}, f32[88,128]{1,0:T(8,128)S(1)}, u32[]{:S(2)}, u32[]{:S(2)}) collective-permute-start(f32[88,128]{1,0:T(8,128)S(1)} %get-tuple-element.39), channel_id=1, source_target_pairs={{0,1},{1,0},{2,3},{3,2},{4,5},{5,4},{6,7},{7,6},{8,9},{9,8},{10,11... | collective-permute-start | bytes 135176 | tf_op jit(solution)/shard_map/ppermute | solution.py:355
  7.8 0.0 collective-permute-start.1
  7.8 0.6 %collective-permute-start.2 = (f32[72,128]{1,0:T(8,128)S(1)}, f32[72,128]{1,0:T(8,128)S(1)}, u32[]{:S(2)}, u32[]{:S(2)}) collective-permute-start(f32[72,128]{1,0:T(8,128)S(1)} %get-tuple-element.41), channel_id=1, source_target_pairs={{0,12},{1,13},{2,14},{3,15},{4,8},{5,9},{6,10},{7,11},{8,4},{9,5},... | collective-permute-start | bytes 110600 | tf_op jit(solution)/shard_map/ppermute | solution.py:355
  8.5 0.0 collective-permute-done.3.refs_1_.refs_11_
  8.5 1.5 %collective-permute-done.4.refs_2_.refs_12_ = f32[120,128]{1,0:T(8,128)S(1)} collective-permute-done((f32[120,128]{1,0:T(8,128)S(1)}, f32[120,128]{1,0:T(8,128)S(1)}, u32[]{:S(2)}, u32[]{:S(2)}) %collective-permute-start.4) | collective-permute-done | bytes 61472 | tf_op jit(solution)/shard_map/ppermute | solution.py:355
  9.9 0.0 collective-permute-start.5
  9.9 0.5 %collective-permute-start.6 = (f32[68,128]{1,0:T(8,128)S(1)}, f32[68,128]{1,0:T(8,128)S(1)}, u32[]{:S(2)}, u32[]{:S(2)}) collective-permute-start(f32[68,128]{1,0:T(8,128)S(1)} %get-tuple-element.46), channel_id=1, source_target_pairs={{0,4},{1,5},{2,6},{3,7},{4,0},{5,1},{6,2},{7,3},{8,12},{9,13},{10,... | collective-permute-start | bytes 104456 | tf_op jit(solution)/shard_map/ppermute | solution.py:355
  10.5 1.1 %work.1 = (f32[2,5,8,16,128]{4,3,2,1,0:T(8,128)S(1)}, f32[5,8,16,128]{3,2,1,0:T(8,128)S(1)}, f32[8,16,128]{2,1,0:T(8,128)S(1)}, f32[4,6,16,128]{3,2,1,0:T(8,128)S(1)}) custom-call(f32[5,8,16,128]{3,2,1,0:T(8,128)S(1)} %get-tuple-element.32.refs_0_, f32[12,8,16,128]{3,2,1,0:T(8,128)S(1)} %get-tuple-element.33.refs_1_.couple_ref, ...), custom_call_target="tpu_custom_call" | custom-call | flops 1000000 | bytes 3000000 | tf_op jit(solution)/shard_map/work/pallas_call | solution.py:333
  11.6 0.0 collective-permute-done.2.refs_8_
  11.6 0.0 collective-permute-done.1.refs_7_
  11.6 0.0 collective-permute-done.refs_6_
  11.6 0.0 collective-permute-done.5.refs_9_
  11.6 0.0 collective-permute-done.6.refs_10_
  11.7 0.7 %finish0.1 = (f32[5,8,16,128]{3,2,1,0:T(8,128)S(1)}, f32[5,8,16,128]{3,2,1,0:T(8,128)S(1)}, f32[88,128]{1,0:T(8,128)S(1)}, f32[80,128]{1,0:T(8,128)S(1)}, f32[24,128]{1,0:T(8,128)S(1)}, /*index=5*/f32[16,128]{1,0:T(8,128)S(1)}) custom-call(f32[5,8,16,128]{3,2,1,0:T(8,128)S(1)} %get-tuple-element.34.refs_0_, ...), custom_call_target="tpu_custom_call" | custom-call | flops 1000000 | bytes 3000000 | tf_op jit(solution)/shard_map/finish0/pallas_call | solution.py:333
  12.4 2.8 %collective-permute-start.7 = (f32[88,128]{1,0:T(8,128)S(1)}, f32[88,128]{1,0:T(8,128)S(1)}, u32[]{:S(2)}, u32[]{:S(2)}) collective-permute-start(f32[88,128]{1,0:T(8,128)S(1)} %get-tuple-element.50), channel_id=1, source_target_pairs={{0,1},{1,0},{2,3},{3,2},{4,5},{5,4},{6,7},{7,6},{8,9},{9,8},{10,11... | collective-permute-start | bytes 135176 | tf_op jit(solution)/shard_map/ppermute | solution.py:355
  15.2 0.0 collective-permute-start.8
  15.2 1.0 %collective-permute-start.9 = (f32[24,128]{1,0:T(8,128)S(1)}, f32[24,128]{1,0:T(8,128)S(1)}, u32[]{:S(2)}, u32[]{:S(2)}) collective-permute-start(f32[24,128]{1,0:T(8,128)S(1)} %get-tuple-element.52), channel_id=1, source_target_pairs={{0,12},{1,13},{2,14},{3,15},{4,8},{5,9},{6,10},{7,11},{8,4},{9,5},... | collective-permute-start | bytes 36872 | tf_op jit(solution)/shard_map/ppermute | solution.py:355
  16.2 0.0 collective-permute-start.10
  16.2 0.4 %local1.1.refs_0_ = f32[5,8,16,128]{3,2,1,0:T(8,128)S(1)} custom-call(f32[5,8,16,128]{3,2,1,0:T(8,128)S(1)} %get-tuple-element.48.lam_ref, f32[12,8,16,128]{3,2,1,0:T(8,128)S(1)} %get-tuple-element.33.refs_1_.couple_ref), custom_call_target="tpu_custom_call" | custom-call | flops 1000000 | bytes 3000000 | tf_op jit(solution)/shard_map/local1/pallas_call | solution.py:333
  16.6 0.8 %collective-permute-done.10.refs_9_ = f32[16,128]{1,0:T(8,128)S(1)} collective-permute-done((f32[16,128]{1,0:T(8,128)S(1)}, f32[16,128]{1,0:T(8,128)S(1)}, u32[]{:S(2)}, u32[]{:S(2)}) %collective-permute-start.10) | collective-permute-done | bytes 8224 | tf_op jit(solution)/shard_map/ppermute | solution.py:355
  17.3 0.9 %collective-permute-done.9.refs_8_ = f32[24,128]{1,0:T(8,128)S(1)} collective-permute-done((f32[24,128]{1,0:T(8,128)S(1)}, f32[24,128]{1,0:T(8,128)S(1)}, u32[]{:S(2)}, u32[]{:S(2)}) %collective-permute-start.9) | collective-permute-done | bytes 12320 | tf_op jit(solution)/shard_map/ppermute | solution.py:355
  18.3 0.0 collective-permute-done.8.refs_7_
  18.3 0.0 collective-permute-done.7.refs_6_
  18.3 0.6 %finish1.1 = (f32[5,8,16,128]{3,2,1,0:T(8,128)S(1)}, f32[88,128]{1,0:T(8,128)S(1)}, f32[80,128]{1,0:T(8,128)S(1)}, f32[24,128]{1,0:T(8,128)S(1)}, f32[16,128]{1,0:T(8,128)S(1)}) custom-call(f32[5,8,16,128]{3,2,1,0:T(8,128)S(1)} %local1.1.refs_0_, f32[12,8,16,128]{3,2,1,0:T(8,128)S(1)} %get-tuple-element.33.refs_1_.couple_ref, ...), custom_call_target="tpu_custom_call" | custom-call | flops 1000000 | bytes 3000000 | tf_op jit(solution)/shard_map/finish1/pallas_call | solution.py:333
  18.8 2.0 %collective-permute-start.11 = (f32[88,128]{1,0:T(8,128)S(1)}, f32[88,128]{1,0:T(8,128)S(1)}, u32[]{:S(2)}, u32[]{:S(2)}) collective-permute-start(f32[88,128]{1,0:T(8,128)S(1)} %get-tuple-element.55), channel_id=1, source_target_pairs={{0,1},{1,0},{2,3},{3,2},{4,5},{5,4},{6,7},{7,6},{8,9},{9,8},{10,11... | collective-permute-start | bytes 135176 | tf_op jit(solution)/shard_map/ppermute | solution.py:355
  20.9 0.0 collective-permute-start.12
  20.9 1.9 %collective-permute-start.13 = (f32[24,128]{1,0:T(8,128)S(1)}, f32[24,128]{1,0:T(8,128)S(1)}, u32[]{:S(2)}, u32[]{:S(2)}) collective-permute-start(f32[24,128]{1,0:T(8,128)S(1)} %get-tuple-element.57), channel_id=1, source_target_pairs={{0,12},{1,13},{2,14},{3,15},{4,8},{5,9},{6,10},{7,11},{8,4},{9,5},... | collective-permute-start | bytes 36872 | tf_op jit(solution)/shard_map/ppermute | solution.py:355
  22.8 0.0 collective-permute-start.14
  22.8 0.4 %local2.1.refs_0_ = f32[5,8,16,128]{3,2,1,0:T(8,128)S(1)} custom-call(f32[5,8,16,128]{3,2,1,0:T(8,128)S(1)} %get-tuple-element.54.lam_ref, f32[12,8,16,128]{3,2,1,0:T(8,128)S(1)} %get-tuple-element.33.refs_1_.couple_ref), custom_call_target="tpu_custom_call" | custom-call | flops 1000000 | bytes 3000000 | tf_op jit(solution)/shard_map/local2/pallas_call | solution.py:333
  23.2 0.8 %collective-permute-done.14.refs_9_ = f32[16,128]{1,0:T(8,128)S(1)} collective-permute-done((f32[16,128]{1,0:T(8,128)S(1)}, f32[16,128]{1,0:T(8,128)S(1)}, u32[]{:S(2)}, u32[]{:S(2)}) %collective-permute-start.14) | collective-permute-done | bytes 8224 | tf_op jit(solution)/shard_map/ppermute | solution.py:355
  24.0 0.2 collective-permute-done.13.refs_8_
  24.2 0.0 collective-permute-done.12.refs_7_
  24.2 0.0 collective-permute-done.11.refs_6_
  24.2 1.1 %finish2.1 = f32[5,8,16,128]{3,2,1,0:T(8,128)} custom-call(f32[5,8,16,128]{3,2,1,0:T(8,128)S(1)} %local2.1.refs_0_, f32[12,8,16,128]{3,2,1,0:T(8,128)S(1)} %get-tuple-element.33.refs_1_.couple_ref, f32[3,5,8,16,128]{4,3,2,1,0:T(8,128)S(1)} %get-tuple-element.35.refs_2_, f32[2,5,8,16,128]{4,3,2,1,0:T(8,128)S(1)} %get-tuple-element.36.refs_3_, ...), custom_call_target="tpu_custom_call" | custom-call | flops 1000000 | bytes 3000000 | tf_op jit(solution)/shard_map/finish2/pallas_call | solution.py:333
  (1 shorter events, 0.0 us)
Async XLA Ops:
  1.8 6.7 %collective-permute-start.3 = (f32[120,128]{1,0:T(8,128)S(1)}, f32[120,128]{1,0:T(8,128)S(1)}, u32[]{:S(2)}, u32[]{:S(2)}) collective-permute-start(f32[120,128]{1,0:T(8,128)S(1)} %get-tuple-element.43), channel_id=1, source_target_pairs={{0,16},{1,17},{2,18},{3,19},{4,20},{5,21},{6,22},{7,23},{8,24},{9,... | collective-permute-start | bytes 184328 | tf_op jit(solution)/shard_map/ppermute | solution.py:355
  4.8 5.1 %collective-permute-start.4 = (f32[120,128]{1,0:T(8,128)S(1)}, f32[120,128]{1,0:T(8,128)S(1)}, u32[]{:S(2)}, u32[]{:S(2)}) collective-permute-start(f32[120,128]{1,0:T(8,128)S(1)} %get-tuple-element.44), channel_id=1, source_target_pairs={{0,24},{1,25},{2,26},{3,27},{4,28},{5,29},{6,30},{7,31},{8,16},{9,... | collective-permute-start | bytes 184328 | tf_op jit(solution)/shard_map/ppermute | solution.py:355
  6.2 5.4 %collective-permute-start = (f32[88,128]{1,0:T(8,128)S(1)}, f32[88,128]{1,0:T(8,128)S(1)}, u32[]{:S(2)}, u32[]{:S(2)}) collective-permute-start(f32[88,128]{1,0:T(8,128)S(1)} %get-tuple-element.39), channel_id=1, source_target_pairs={{0,1},{1,0},{2,3},{3,2},{4,5},{5,4},{6,7},{7,6},{8,9},{9,8},{10,11... | collective-permute-start | bytes 135176 | tf_op jit(solution)/shard_map/ppermute | solution.py:355
  7.8 3.8 %collective-permute-start.1 = (f32[80,128]{1,0:T(8,128)S(1)}, f32[80,128]{1,0:T(8,128)S(1)}, u32[]{:S(2)}, u32[]{:S(2)}) collective-permute-start(f32[80,128]{1,0:T(8,128)S(1)} %get-tuple-element.40), channel_id=1, source_target_pairs={{0,4},{1,2},{2,1},{3,7},{4,0},{5,6},{6,5},{7,3},{8,12},{9,10},{10,... | collective-permute-start | bytes 122888 | tf_op jit(solution)/shard_map/ppermute | solution.py:355
  7.8 3.8 %collective-permute-start.2 = (f32[72,128]{1,0:T(8,128)S(1)}, f32[72,128]{1,0:T(8,128)S(1)}, u32[]{:S(2)}, u32[]{:S(2)}) collective-permute-start(f32[72,128]{1,0:T(8,128)S(1)} %get-tuple-element.41), channel_id=1, source_target_pairs={{0,12},{1,13},{2,14},{3,15},{4,8},{5,9},{6,10},{7,11},{8,4},{9,5},... | collective-permute-start | bytes 110600 | tf_op jit(solution)/shard_map/ppermute | solution.py:355
  9.9 1.7 %collective-permute-start.5 = (f32[68,128]{1,0:T(8,128)S(1)}, f32[68,128]{1,0:T(8,128)S(1)}, u32[]{:S(2)}, u32[]{:S(2)}) collective-permute-start(f32[68,128]{1,0:T(8,128)S(1)} %get-tuple-element.45), channel_id=1, source_target_pairs={{0,4},{1,5},{2,6},{3,7},{4,0},{5,1},{6,2},{7,3},{8,12},{9,13},{10,... | collective-permute-start | bytes 104456 | tf_op jit(solution)/shard_map/ppermute | solution.py:355
  9.9 1.7 %collective-permute-start.6 = (f32[68,128]{1,0:T(8,128)S(1)}, f32[68,128]{1,0:T(8,128)S(1)}, u32[]{:S(2)}, u32[]{:S(2)}) collective-permute-start(f32[68,128]{1,0:T(8,128)S(1)} %get-tuple-element.46), channel_id=1, source_target_pairs={{0,4},{1,5},{2,6},{3,7},{4,0},{5,1},{6,2},{7,3},{8,12},{9,13},{10,... | collective-permute-start | bytes 104456 | tf_op jit(solution)/shard_map/ppermute | solution.py:355
  12.4 5.9 %collective-permute-start.7 = (f32[88,128]{1,0:T(8,128)S(1)}, f32[88,128]{1,0:T(8,128)S(1)}, u32[]{:S(2)}, u32[]{:S(2)}) collective-permute-start(f32[88,128]{1,0:T(8,128)S(1)} %get-tuple-element.50), channel_id=1, source_target_pairs={{0,1},{1,0},{2,3},{3,2},{4,5},{5,4},{6,7},{7,6},{8,9},{9,8},{10,11... | collective-permute-start | bytes 135176 | tf_op jit(solution)/shard_map/ppermute | solution.py:355
  15.2 3.1 %collective-permute-start.8 = (f32[80,128]{1,0:T(8,128)S(1)}, f32[80,128]{1,0:T(8,128)S(1)}, u32[]{:S(2)}, u32[]{:S(2)}) collective-permute-start(f32[80,128]{1,0:T(8,128)S(1)} %get-tuple-element.51), channel_id=1, source_target_pairs={{0,4},{1,2},{2,1},{3,7},{4,0},{5,6},{6,5},{7,3},{8,12},{9,10},{10,... | collective-permute-start | bytes 122888 | tf_op jit(solution)/shard_map/ppermute | solution.py:355
  15.2 3.1 %collective-permute-start.9 = (f32[24,128]{1,0:T(8,128)S(1)}, f32[24,128]{1,0:T(8,128)S(1)}, u32[]{:S(2)}, u32[]{:S(2)}) collective-permute-start(f32[24,128]{1,0:T(8,128)S(1)} %get-tuple-element.52), channel_id=1, source_target_pairs={{0,12},{1,13},{2,14},{3,15},{4,8},{5,9},{6,10},{7,11},{8,4},{9,5},... | collective-permute-start | bytes 36872 | tf_op jit(solution)/shard_map/ppermute | solution.py:355
  16.2 1.2 %collective-permute-start.10 = (f32[16,128]{1,0:T(8,128)S(1)}, f32[16,128]{1,0:T(8,128)S(1)}, u32[]{:S(2)}, u32[]{:S(2)}) collective-permute-start(f32[16,128]{1,0:T(8,128)S(1)} %get-tuple-element.53), channel_id=1, source_target_pairs={{0,4},{1,5},{2,6},{3,7},{4,0},{5,1},{6,2},{7,3},{8,12},{9,13},{10,... | collective-permute-start | bytes 24584 | tf_op jit(solution)/shard_map/ppermute | solution.py:355
  18.8 5.4 %collective-permute-start.11 = (f32[88,128]{1,0:T(8,128)S(1)}, f32[88,128]{1,0:T(8,128)S(1)}, u32[]{:S(2)}, u32[]{:S(2)}) collective-permute-start(f32[88,128]{1,0:T(8,128)S(1)} %get-tuple-element.55), channel_id=1, source_target_pairs={{0,1},{1,0},{2,3},{3,2},{4,5},{5,4},{6,7},{7,6},{8,9},{9,8},{10,11... | collective-permute-start | bytes 135176 | tf_op jit(solution)/shard_map/ppermute | solution.py:355
  20.9 3.3 %collective-permute-start.12 = (f32[80,128]{1,0:T(8,128)S(1)}, f32[80,128]{1,0:T(8,128)S(1)}, u32[]{:S(2)}, u32[]{:S(2)}) collective-permute-start(f32[80,128]{1,0:T(8,128)S(1)} %get-tuple-element.56), channel_id=1, source_target_pairs={{0,4},{1,2},{2,1},{3,7},{4,0},{5,6},{6,5},{7,3},{8,12},{9,10},{10,... | collective-permute-start | bytes 122888 | tf_op jit(solution)/shard_map/ppermute | solution.py:355
  20.9 3.3 %collective-permute-start.13 = (f32[24,128]{1,0:T(8,128)S(1)}, f32[24,128]{1,0:T(8,128)S(1)}, u32[]{:S(2)}, u32[]{:S(2)}) collective-permute-start(f32[24,128]{1,0:T(8,128)S(1)} %get-tuple-element.57), channel_id=1, source_target_pairs={{0,12},{1,13},{2,14},{3,15},{4,8},{5,9},{6,10},{7,11},{8,4},{9,5},... | collective-permute-start | bytes 36872 | tf_op jit(solution)/shard_map/ppermute | solution.py:355
  22.8 1.2 %collective-permute-start.14 = (f32[16,128]{1,0:T(8,128)S(1)}, f32[16,128]{1,0:T(8,128)S(1)}, u32[]{:S(2)}, u32[]{:S(2)}) collective-permute-start(f32[16,128]{1,0:T(8,128)S(1)} %get-tuple-element.58), channel_id=1, source_target_pairs={{0,4},{1,5},{2,6},{3,7},{4,0},{5,1},{6,2},{7,3},{8,12},{9,13},{10,... | collective-permute-start | bytes 24584 | tf_op jit(solution)/shard_map/ppermute | solution.py:355

commit v4 on v3

v4 whole, which is shorter than its diff:
```python
import functools

import jax
import jax.numpy as jnp
from jax import lax
from jax.experimental import pallas as pl
from jax.experimental.pallas import tpu as pltpu
from jax.sharding import PartitionSpec as P

SWEEPS = 3
AXES = ("sec", "circ", "rad")
SUB, LANES = 8, 128
PARAMS = pltpu.CompilerParams(vmem_limit_bytes=16 * 1024 * 1024)


def routes(mesh):
    secs, circs, rads = (mesh.shape[a] for a in AXES)

    def pairs(target):
        flat = lambda s, c, r: (s * circs + c) * rads + r
        return [
            (flat(s, c, r), flat(*target(s, c, r)))
            for s in range(secs)
            for c in range(circs)
            for r in range(rads)
        ]

    def swap(s, c, r, odd):
        q = r + 1 if (r + odd) % 2 == 0 else r - 1
        return (s, c, q) if 0 <= q < rads else (s, c ^ 1, r)

    return {
        "ahead": pairs(lambda s, c, r: swap(s, c, r, 0)),
        "back": pairs(lambda s, c, r: swap(s, c, r, 1)),
        "mate": pairs(lambda s, c, r: (s, c ^ 1, r)),
        "across": pairs(lambda s, c, r: (s, (c - 1 if c % 2 == 0 else c + 1) % circs, r)),
        "faces": [
            pairs(lambda s, c, r: (1, (c + k) % circs, r) if s == 0 else (0, (c - k) % circs, r))
            for k in range(0, circs, 2)
        ],
    }


def iotas():
    sub = lax.broadcasted_iota(jnp.int32, (SUB, LANES), 0)
    lane = lax.broadcasted_iota(jnp.int32, (SUB, LANES), 1)
    return sub, lane


def down(x, by):
    return pltpu.roll(x, by % SUB, 0) if by % SUB else x


def along(x, by):
    return pltpu.roll(x, by % LANES, 1) if by % LANES else x


def half_rows(half):
    return slice(SUB * half, SUB * (half + 1))


def slot(v, a, na):
    return v % 2, 4 * (na * (v // 2) + a) + 2 * (v % 2)


class Packer:
    def __init__(self, na, nv):
        self.sub, self.lane = iotas()
        self.na = na
        self.low, self.high, self.cols = {}, {}, {}

    def put(self, book, key, keep, x):
        book[key] = jnp.where(keep, x, book[key]) if key in book else x

    def add(self, v, a, half, x):
        k = v * self.na + a
        group, j = k // 4, k % 4
        inside = (self.sub >= 2 * j) & (self.sub < 2 * j + 2)
        if half == 0:
            self.put(self.low, group, inside, down(x, 2 * j))
        else:
            self.put(self.high, group, inside, down(x, 2 * j + 2))
        part, spot = slot(v, a, self.na)
        inside = (self.lane >= spot) & (self.lane < spot + 4)
        self.put(self.cols, (part, half), inside, along(x, spot + 2))

    def write(self, ahead_ref, back_ref, across_ref, mate_refs):
        even = lax.axis_index("rad") % 2 == 0
        for g in range(len(self.low)):
            rows = slice(SUB * g, SUB * (g + 1))
            ahead_ref[rows, :] = jnp.where(even, self.high[g], self.low[g])
            back_ref[rows, :] = jnp.where(even, self.low[g], self.high[g])
        even = lax.axis_index("circ") % 2 == 0
        for half in range(2):
            x, y = self.cols[0, half], self.cols[1, half]
            right = jnp.where(self.lane % 4 < 2, x, y)
            left = jnp.where(self.lane % 4 < 2, y, x)
            rows = slice(SUB * half, SUB * (half + 1))
            across_ref[rows, :] = jnp.where(even, left, right)
            mate_refs[half][...] = jnp.where(even, right, left)


def pack_kernel(lam_ref, ahead_ref, back_ref, across_ref, mate_ref):
    nv, na = lam_ref.shape[:2]
    packer = Packer(na, nv)
    for a in range(na):
        for v in range(nv):
            for half in range(2):
                packer.add(v, a, half, lam_ref[v, a, SUB * half : SUB * (half + 1), :])
    packer.write(ahead_ref, back_ref, across_ref, [mate_ref.at[:SUB], mate_ref.at[SUB:]])


def load_kernel(adjoint_ref, donors_in, couple_in, src_in, jac_in, targets_in, counts_in, weights_in, *refs):
    lam_ref, couple_ref, src_ref, jac_ref, placed_ref, inv_ref, cols_ref, rows_ref, *tile_refs = refs[:-5]
    donors_ref, targets_ref, counts_ref, weights_ref, sems = refs[-5:]
    nv, na, nr, _ = lam_ref.shape
    copies = [
        pltpu.make_async_copy(donors_in, donors_ref, sems.at[0]),
        pltpu.make_async_copy(adjoint_ref, lam_ref, sems.at[1]),
        pltpu.make_async_copy(targets_in, targets_ref, sems.at[2]),
        pltpu.make_async_copy(counts_in, counts_ref, sems.at[3]),
        pltpu.make_async_copy(weights_in, weights_ref, sems.at[4]),
        pltpu.make_async_copy(couple_in, couple_ref, sems.at[5]),
        pltpu.make_async_copy(src_in, src_ref, sems.at[6]),
    ]
    copies += [pltpu.make_async_copy(jac_in.at[s], jac_ref.at[s], sems.at[7 + s]) for s in range(nv)]
    for copy in copies:
        copy.start()
    copies[0].wait()
    copies[1].wait()
    me, circs, slots = lax.axis_index("circ"), donors_ref.shape[1], donors_ref.shape[2]
    for n, tile_ref in enumerate(tile_refs):
        reader = jnp.where(me + 2 * n >= circs, me + 2 * n - circs, me + 2 * n)
        for part, to in enumerate((reader, reader + 1 - 2 * (reader % 2))):
            for k in range(slots):
                row = jnp.clip(donors_ref[me, to, k], 0, nr - 1)
                for v in range(nv):
                    for a in range(2):
                        at = ((part * slots + k) * nv + v) * 2 + a
                        tile_ref[at : at + 1, :] = lam_ref[v, na - 2 + a, pl.ds(row, 1), :]
    for copy in copies[2:5]:
        copy.wait()
    place_weights(targets_ref, counts_ref, weights_ref, placed_ref)
    copies[5].wait()
    coefs_of(couple_ref, inv_ref, cols_ref, rows_ref)
    for copy in copies[6:]:
        copy.wait()


def place_weights(targets_ref, counts_ref, weights_ref, placed_ref):
    me = lax.axis_index("circ")
    stator = lax.axis_index("sec") == 1
    sub, _ = iotas()
    slots = targets_ref.shape[-1]
    for d in range(targets_ref.shape[0]):
        for k in range(slots):
            live = (k < counts_ref[d, me]) & stator
            row = jnp.where(live, targets_ref[d, me, k], -1)
            w = jnp.broadcast_to(weights_ref[d * slots + k : d * slots + k + 1, :], (SUB, LANES))
            for h in range(2):
                placed_ref[d, k, SUB * h : SUB * (h + 1), :] = jnp.where(sub + SUB * h == row, w, 0.0)


def inner_coefs(c, half, sub, lane):
    c = list(c)
    if half == 0:
        c[4] = jnp.where(sub >= 2, c[4], 0.0)
        c[5] = jnp.where(sub >= 1, c[5], 0.0)
    else:
        c[6] = jnp.where(sub < SUB - 1, c[6], 0.0)
        c[7] = jnp.where(sub < SUB - 2, c[7], 0.0)
    c[8] = jnp.where(lane >= 2, c[8], 0.0)
    c[9] = jnp.where(lane >= 1, c[9], 0.0)
    c[10] = jnp.where(lane < LANES - 1, c[10], 0.0)
    c[11] = jnp.where(lane < LANES - 2, c[11], 0.0)
    return c


def local_sums(lam_ref, a, coef, sub):
    nv, na = lam_ref.shape[:2]
    sums = []
    for v in range(nv):
        x = [lam_ref[v, a, half_rows(h), :] for h in range(2)]
        moved = {o: [down(x[h], -o) for h in range(2)] for o in (-2, -1, 1, 2)}
        both = []
        for half in range(2):
            c = coef[half]
            total = None
            for i, o in enumerate((-2, -1, 1, 2)):
                if 0 <= a + o < na:
                    term = c[i] * lam_ref[v, a + o, half_rows(half), :]
                    total = term if total is None else total + term
            for i, o in enumerate((-2, -1, 1, 2)):
                m = moved[o]
                if o < 0:
                    y = m[0] if half == 0 else jnp.where(sub >= -o, m[1], m[0])
                else:
                    y = m[1] if half == 1 else jnp.where(sub < SUB - o, m[0], m[1])
                total = total + c[4 + i] * y
            for i, o in enumerate((-2, -1, 1, 2)):
                total = total + c[8 + i] * along(x[half], -o)
            both.append(total)
        sums.append(both)
    return sums


class Gather:
    def __init__(self, sub, lane):
        self.sub, self.lane = sub, lane
        self.got = {}

    def put(self, key, keep, x):
        self.got[key] = jnp.where(keep, x, self.got[key]) if key in self.got else x

    def cols(self, name, half, a, x):
        inside = (self.lane >= 4 * a) & (self.lane < 4 * a + 4)
        self.put((name, half), inside, along(x, 4 * a + 2))

    def rows(self, name, half, a, x):
        j = a % 4
        inside = (self.sub >= 2 * j) & (self.sub < 2 * j + 2)
        self.put((name, a // 4), inside, down(x, 2 * j + 2 * half))


def coefs_of(couple_ref, inv_ref, cols_ref, rows_ref):
    na = couple_ref.shape[1]
    sub, lane = iotas()
    rad = lax.axis_index("rad")
    has_low, has_high = rad > 0, rad < lax.axis_size("rad") - 1
    gather = Gather(sub, lane)
    for a in range(na):
        for half in range(2):
            c = [couple_ref[i, a, half_rows(half), :] for i in range(12)]
            total = c[0]
            for i in range(1, 12):
                total = total + c[i]
            inv_ref[a, half_rows(half), :] = 1.0 / (1.0 + total)
            gather.cols("outer", half, a, jnp.where(lane < 2, c[8], jnp.where(lane >= LANES - 2, c[11], 0.0)))
            gather.cols("inner", half, a, jnp.where(lane < 1, c[9], jnp.where(lane >= LANES - 1, c[10], 0.0)))
            if half == 0:
                gather.rows("low far", 0, a, jnp.where(has_low, c[4], 0.0))
                gather.rows("low nigh", 0, a, jnp.where(has_low & (sub < 1), c[5], 0.0))
            else:
                gather.rows("high far", 1, a, jnp.where(has_high, c[7], 0.0))
                gather.rows("high nigh", 1, a, jnp.where(has_high & (sub >= SUB - 1), c[6], 0.0))
    for i, name in enumerate(("outer", "inner")):
        for half in range(2):
            cols_ref[i, half_rows(half), :] = gather.got[name, half]
    for i, name in enumerate(("low far", "low nigh", "high far", "high nigh")):
        for q in range(na // 4):
            rows_ref[i, half_rows(q), :] = gather.got[name, q]


def work_kernel(lam_ref, couple_ref, near_ref):
    sub, lane = iotas()
    for a in range(lam_ref.shape[1]):
        coef = [
            inner_coefs([couple_ref[i, a, half_rows(h), :] for i in range(12)], h, sub, lane) for h in range(2)
        ]
        for v, both in enumerate(local_sums(lam_ref, a, coef, sub)):
            for half, x in enumerate(both):
                near_ref[v, a, half_rows(half), :] = x


def donor_at(at):
    return jnp.where(at < 0, at + lax.axis_size("circ"), at)


def add_tiles(x, sources, placed_ref, s, a, half, nv):
    for tile_ref, start, donor in sources:
        for t in range(placed_ref.shape[1]):
            at = start + (t * nv + s) * 2 + a
            tile = jnp.broadcast_to(tile_ref[at : at + 1, :], (SUB, LANES))
            x = x + placed_ref[donor, t, half_rows(half), :] * tile
    return x


def local_kernel(prepare, lam_ref, couple_ref, jac_ref, rhs_ref, inv_ref, base_ref, *edge_refs):
    nv, na = lam_ref.shape[:2]
    sub, lane = iotas()
    gathers = {}
    for a in range(na):
        coef = [
            inner_coefs([couple_ref[i, a, half_rows(h), :] for i in range(12)], h, sub, lane) for h in range(2)
        ]
        near = local_sums(lam_ref, a, coef, sub)
        for half in range(2):
            inv = inv_ref[a, half_rows(half), :]
            for s in range(nv):
                acc = rhs_ref[s, a, half_rows(half), :]
                for b in range(nv):
                    m = jac_ref[s, b, a, half_rows(half), :]
                    acc = acc + m * near[b][half]
                    if prepare:
                        m = m * inv
                        gather = gathers.setdefault((s, b), Gather(sub, lane))
                        gather.cols("cols", half, a, m)
                        gather.rows("high" if half else "low", half, a, m)
                base_ref[s, a, half_rows(half), :] = acc * inv
    if prepare:
        cols_ref, low_ref, high_ref = edge_refs
        for (s, b), gather in gathers.items():
            for half in range(2):
                cols_ref[s, b, half_rows(half), :] = gather.got["cols", half]
            for q in range(na // 4):
                low_ref[s, b, half_rows(q), :] = gather.got["low", q]
                high_ref[s, b, half_rows(q), :] = gather.got["high", q]


def relay_kernel(first, cols_ref, tile_ref, out_ref, *, share):
    half = out_ref.shape[0] - share
    out_ref[share:, :] = tile_ref[half : 2 * half, :]
    if first < cols_ref.shape[0]:
        out_ref[:share, :] = cols_ref[first : first + share, :]


def shares(routes):
    return SUB * max(1, 2 // routes)


def halo_sums(nv, na, ahead_ref, back_ref, across_ref, mate_at, cols_ref, rows_ref):
    sub, lane = iotas()
    me, rad = lax.axis_index("circ"), lax.axis_index("rad")
    out = []
    right, left = [], []
    for half in range(2):
        x, y = mate_at(half), across_ref[half_rows(half), :]
        right.append(jnp.where(me % 2 == 0, x, y))
        left.append(jnp.where(me % 2 == 0, y, x))
    for v in range(nv):
        _, spot = slot(v, 0, na)
        cols = []
        for half in range(2):
            r, l = right[half], left[half]
            wide = jnp.where(lane % 4 < 2, along(r, -spot - 2), along(l, 2 - spot))
            slim = jnp.where(lane % 4 < 2, along(r, -spot - 1), along(l, 1 - spot))
            cols.append(cols_ref[0, half_rows(half), :] * wide + cols_ref[1, half_rows(half), :] * slim)
        low, high = [], []
        for q in range(na // 4):
            rows = half_rows(v * (na // 4) + q)
            x, y = ahead_ref[rows, :], back_ref[rows, :]
            m, p = jnp.where(rad % 2 == 0, y, x), jnp.where(rad % 2 == 0, x, y)
            low.append(rows_ref[0, half_rows(q), :] * m + rows_ref[1, half_rows(q), :] * down(m, -1))
            high.append(rows_ref[2, half_rows(q), :] * p + rows_ref[3, half_rows(q), :] * down(p, 1))
        out.append((cols, low, high))
    return out


def spread(x, part, a, half, sub, lane):
    cols, low, high = part
    x = x + jnp.where((lane < 2) | (lane >= LANES - 2), along(cols[half], LANES - 2 - 4 * a), 0.0)
    j = a % 4
    if half == 0:
        return x + jnp.where(sub < 2, down(low[a // 4], -2 * j), 0.0)
    return x + jnp.where(sub >= SUB - 2, down(high[a // 4], SUB - 2 - 2 * j), 0.0)


def first_finish(routes, *refs):
    near_ref, jac_ref, src_ref, inv_ref, placed_ref, cols_ref, rows_ref = refs[:7]
    ahead_ref, back_ref, across_ref, *relayed = refs[7 : 10 + routes]
    direct = refs[10 + routes : 10 + 2 * routes]
    out_ref, rhs_ref, ahead_to, back_to, across_to, mate_to = refs[10 + 2 * routes :]
    nv, na = near_ref.shape[:2]
    sub, lane = iotas()
    share = shares(routes)
    mate_at = lambda half: relayed[SUB * half // share][SUB * half % share : SUB * half % share + SUB, :]
    parts = halo_sums(nv, na, ahead_ref, back_ref, across_ref, mate_at, cols_ref, rows_ref)
    me = lax.axis_index("circ")
    sources = [(ref, 0, donor_at(me - 2 * n)) for n, ref in enumerate(direct)]
    sources += [(ref, share, donor_at(me + 1 - 2 * (me % 2) - 2 * n)) for n, ref in enumerate(relayed)]
    packer = Packer(na, nv)
    for a in range(na):
        for half in range(2):
            rows = half_rows(half)
            near = [spread(near_ref[v, a, rows, :], parts[v], a, half, sub, lane) for v in range(nv)]
            inv = inv_ref[a, rows, :]
            for s in range(nv):
                acc = src_ref[s, a, rows, :]
                if a < 2:
                    acc = add_tiles(acc, sources, placed_ref, s, a, half, nv)
                rhs_ref[s, a, rows, :] = acc
                for b in range(nv):
                    acc = acc + jac_ref[s, b, a, rows, :] * near[b]
                x = acc * inv
                out_ref[s, a, rows, :] = x
                packer.add(s, a, half, x)
    packer.write(ahead_to, back_to, across_to, [mate_to.at[:SUB], mate_to.at[SUB:]])


def finish_kernel(last, *refs):
    base_ref, cols_ref, rows_ref, edge_cols, edge_low, edge_high = refs[:6]
    ahead_ref, back_ref, across_ref, mate_ref, out_ref, *rest = refs[6:]
    nv, na = base_ref.shape[:2]
    sub, lane = iotas()
    if last:
        result_ref, out_ref, sems = out_ref, *rest
        copies = []
    sums = halo_sums(
        nv, na, ahead_ref, back_ref, across_ref, lambda half: mate_ref[half_rows(half), :], cols_ref, rows_ref
    )
    parts = []
    for s in range(nv):
        turned = []
        for kind, edge_ref in enumerate((edge_cols, edge_low, edge_high)):
            turned.append([])
            for q in range(2 if kind == 0 else na // 4):
                total = edge_ref[s, 0, half_rows(q), :] * sums[0][kind][q]
                for b in range(1, nv):
                    total = total + edge_ref[s, b, half_rows(q), :] * sums[b][kind][q]
                turned[-1].append(total)
        parts.append(turned)
    packer = None if last else Packer(na, nv)
    for a in range(na):
        for half in range(2):
            for s in range(nv):
                x = spread(base_ref[s, a, half_rows(half), :], parts[s], a, half, sub, lane)
                out_ref[s, a, half_rows(half), :] = x
                if packer is not None:
                    packer.add(s, a, half, x)
        if last:
            copy = pltpu.make_async_copy(out_ref.at[:, a], result_ref.at[:, a], sems.at[a])
            copy.start()
            copies.append(copy)
    if last:
        for copy in copies:
            copy.wait()
    else:
        ahead_to, back_to, across_to, mate_to = rest
        packer.write(ahead_to, back_to, across_to, [mate_to.at[:SUB], mate_to.at[SUB:]])


def call(kernel, name, outs, args, specs=None, scratch=(), us=1, out_specs=None):
    vmem = pl.BlockSpec(memory_space=pltpu.VMEM)
    return pl.pallas_call(
        kernel,
        out_shape=outs,
        in_specs=[vmem] * len(args) if specs is None else specs,
        out_specs=[vmem] * len(outs) if out_specs is None else out_specs,
        scratch_shapes=list(scratch),
        compiler_params=PARAMS,
        cost_estimate=pl.CostEstimate(
            flops=us * 1_000_000, bytes_accessed=us * 3_000_000, transcendentals=0
        ),
        name=name,
    )(*args)


def solution(mesh):
    route = routes(mesh)
    vmem = lambda *shape: pltpu.VMEM(shape, jnp.float32)
    inside = pl.BlockSpec(memory_space=pltpu.VMEM)
    outside = pl.BlockSpec(memory_space=pltpu.HBM)
    far = lambda x: pltpu.with_memory_space_constraint(x, pltpu.HBM)

    def sent(x, pairs):
        return lax.ppermute(x, AXES, pairs)

    def per_device(adjoint, source, jacobian, couple, donor_row, target_row, tile_count, weights):
        nv, na, nr, nc = adjoint.shape[1:]
        donors, slots = donor_row.shape[2:]
        count = len(route["faces"])
        sides = 2 * nv * na
        edges = lambda across: [vmem(sides + SUB, nc), vmem(sides, nc), vmem(across, nc), vmem(nr, nc)]
        block = vmem(nv, na, nr, nc)
        lam, cpl, rhs, jac, placed, inv, edge_coefs, row_coefs, *tiles = call(
            load_kernel, "load",
            [block, vmem(12, na, nr, nc), block, vmem(nv, nv, na, nr, nc), vmem(donors, slots, nr, nc),
             vmem(na, nr, nc), vmem(2, nr, nc), vmem(4, 2 * na, nc)]
            + [vmem(4 * slots * nv + SUB * n, nc) for n in range(count)],
            [*map(far, (adjoint[0], donor_row[0], couple[0], source[0], jacobian[0], target_row[0],
                        tile_count[0], weights.reshape(-1, nc)))],
            [outside] * 8,
            [pltpu.SMEM(donor_row.shape[1:], jnp.int32), pltpu.SMEM(target_row.shape[1:], jnp.int32),
             pltpu.SMEM(tile_count.shape[1:], jnp.int32), pltpu.VMEM((donors * slots, nc), jnp.float32),
             pltpu.SemaphoreType.DMA((7 + nv,))],
        )
        ahead, back, cross, cols = call(pack_kernel, "pack", edges(sides - SUB), [lam])
        tiles = [sent(x, pairs) for x, pairs in zip(tiles, route["faces"])]
        for sweep in range(SWEEPS):
            last = sweep == SWEEPS - 1
            ahead = sent(ahead, route["ahead"])
            back = sent(back, route["back"])
            across = sent(cross, route["across"])
            if sweep == 0:
                share = shares(count)
                relayed = [
                    call(functools.partial(relay_kernel, share * n, share=share), f"relay{n}",
                         [vmem(share + 2 * slots * nv, nc)], [cols, x])[0]
                    for n, x in enumerate(tiles)
                ]
                relayed = [sent(x, route["mate"]) for x in relayed]
                near, = call(work_kernel, "work", [block], [lam, cpl])
                lam, rhs, ahead, back, cross, cols = call(
                    functools.partial(first_finish, count), "finish0", [block] * 2 + edges(nr + SUB),
                    [near, jac, rhs, inv, placed, edge_coefs, row_coefs, ahead, back, across,
                     *relayed, *tiles],
                )
                continue
            mate = sent(cols, route["mate"])
            prepare = sweep == 1
            base, *more = call(
                functools.partial(local_kernel, prepare), f"local{sweep}",
                [block] + ([vmem(nv, nv, nr, nc)] + [vmem(nv, nv, 2 * na, nc)] * 2 if prepare else []),
                [lam, cpl, jac, rhs, inv],
            )
            if prepare:
                matrices = more
            scratch, spaces, outs = [], None, [block] + edges(nr + SUB)
            if last:
                outs, spaces = [jax.ShapeDtypeStruct((nv, na, nr, nc), jnp.float32)], [outside]
                scratch = [pltpu.VMEM((nv, na, nr, nc), jnp.float32), pltpu.SemaphoreType.DMA((na,))]
            lam, *more = call(
                functools.partial(finish_kernel, last), f"finish{sweep}", outs,
                [base, edge_coefs, row_coefs, *matrices, ahead, back, across, mate], None, scratch, 1, spaces,
            )
            if not last:
                ahead, back, cross, cols = more
        return lam[None]

    in_specs = (
        P("sec", None, None, "rad", "circ"),
        P("sec", None, None, "rad", "circ"),
        P("sec", None, None, None, "rad", "circ"),
        P("sec", None, None, "rad", "circ"),
        P("rad", None, None, None),
        P("rad", None, None, None),
        P("rad", None, None),
        P("rad", None, "circ", None, None),
    )
    out_specs = P("sec", None, None, "rad", "circ")
    return jax.shard_map(
        per_device, mesh=mesh, in_specs=in_specs, out_specs=out_specs, check_vma=False
    )
```

time: 25.5 us -> 25 us (0.980)
  starting transfers between devices: 14.9 us -> 14.1 us
  waiting for transfers between devices: 4.18 us -> 4.61 us
    ppermute x15, starting transfers between devices: 14.9 us -> 14.1 us  [sent(): return lax.ppermute(x, AXES, pairs)]
    ppermute x15, waiting for transfers between devices: 4.18 us -> 4.61 us  [sent(): return lax.ppermute(x, AXES, pairs)]
    pallas_call x8 -> x10, Pallas kernels: 6.13 us -> 6 us  [call(): pl.pallas_call(kernel, out_shape=outs, in_specs=[vmem] * len(args) if spe...]
  transfers between devices with their start and end apart: 15 -> 15, of which waited for: 5 -> 6; matrix products, arithmetic and copies ran while one was open for 0% -> 0% of each run, Pallas kernels for 8% -> 8%
where the time goes in v4:
time: 25 us; the launch traced here: 24.7 us
  starting transfers between devices  14.1 us (56%)
  Pallas kernels  6 us (24%)
  waiting for transfers between devices  4.61 us (18%)
    ppermute x15, starting transfers between devices, sent(): return lax.ppermute(x, AXES, pairs)  14.1 us
    pallas_call x10, Pallas kernels, call(): pl.pallas_call(kernel, out_shape=outs, in_specs=[vmem] * len(args) if spe...  6 us
    ppermute x15, waiting for transfers between devices, sent(): return lax.ppermute(x, AXES, pairs)  4.61 us
  transfers between devices with their start and end apart: 15, of which 6 were waited for; matrix products, arithmetic and copies ran while one was open for 0% of the time, Pallas kernels for 8%

profile of v4, /device:TPU:0, one launch (start us, length us, event | category | flops | bytes accessed | tf_op | source)
XLA Modules:
  0.0 24.7 jit_solution(4547103567220791711)
XLA Ops:
  0.0 1.9 %load.1 = (f32[5,8,16,128]{3,2,1,0:T(8,128)S(1)}, f32[12,8,16,128]{3,2,1,0:T(8,128)S(1)}, f32[5,8,16,128]{3,2,1,0:T(8,128)S(1)}, f32[5,5,8,16,128]{4,3,2,1,0:T(8...) custom-call(f32[5,8,16,128]{3,2,1,0:T(8,128)} %bitcast.11, ...), custom_call_target="tpu_custom_call" | custom-call | flops 1000000 | bytes 3000000 | tf_op jit(solution)/shard_map/load/pallas_call | solution.py:434
  1.9 4.0 %collective-permute-start.5 = (f32[128,128]{1,0:T(8,128)S(1)}, f32[128,128]{1,0:T(8,128)S(1)}, u32[]{:S(2)}, u32[]{:S(2)}) collective-permute-start(f32[128,128]{1,0:T(8,128)S(1)} %get-tuple-element.47), channel_id=1, source_target_pairs={{0,24},{1,25},{2,26},{3,27},{4,28},{5,29},{6,30},{7,31},{8,16},{9,... | collective-permute-start | bytes 196616 | tf_op jit(solution)/shard_map/ppermute | solution.py:456
  5.9 0.5 %collective-permute-start.3 = (f32[120,128]{1,0:T(8,128)S(1)}, f32[120,128]{1,0:T(8,128)S(1)}, u32[]{:S(2)}, u32[]{:S(2)}) collective-permute-start(f32[120,128]{1,0:T(8,128)S(1)} %get-tuple-element.46), channel_id=1, source_target_pairs={{0,16},{1,17},{2,18},{3,19},{4,20},{5,21},{6,22},{7,23},{8,24},{9,... | collective-permute-start | bytes 184328 | tf_op jit(solution)/shard_map/ppermute | solution.py:456
  6.4 0.1 pack.1
  6.6 1.6 %collective-permute-start = (f32[88,128]{1,0:T(8,128)S(1)}, f32[88,128]{1,0:T(8,128)S(1)}, u32[]{:S(2)}, u32[]{:S(2)}) collective-permute-start(f32[88,128]{1,0:T(8,128)S(1)} %get-tuple-element.42), channel_id=1, source_target_pairs={{0,1},{1,0},{2,3},{3,2},{4,5},{5,4},{6,7},{7,6},{8,9},{9,8},{10,11... | collective-permute-start | bytes 135176 | tf_op jit(solution)/shard_map/ppermute | solution.py:456
  8.2 0.0 collective-permute-start.1
  8.2 0.6 %collective-permute-start.2 = (f32[72,128]{1,0:T(8,128)S(1)}, f32[72,128]{1,0:T(8,128)S(1)}, u32[]{:S(2)}, u32[]{:S(2)}) collective-permute-start(f32[72,128]{1,0:T(8,128)S(1)} %get-tuple-element.44), channel_id=1, source_target_pairs={{0,12},{1,13},{2,14},{3,15},{4,8},{5,9},{6,10},{7,11},{8,4},{9,5},... | collective-permute-start | bytes 110600 | tf_op jit(solution)/shard_map/ppermute | solution.py:456
  8.8 1.3 %collective-permute-done.3.tile_ref.refs_12_ = f32[120,128]{1,0:T(8,128)S(1)} collective-permute-done((f32[120,128]{1,0:T(8,128)S(1)}, f32[120,128]{1,0:T(8,128)S(1)}, u32[]{:S(2)}, u32[]{:S(2)}) %collective-permute-start.3) | collective-permute-done | bytes 61472 | tf_op jit(solution)/shard_map/ppermute | solution.py:456
  10.1 0.0 collective-permute-start.4
  10.1 0.0 collective-permute-done.5.tile_ref.refs_13_
  10.1 0.5 %collective-permute-start.6 = (f32[68,128]{1,0:T(8,128)S(1)}, f32[68,128]{1,0:T(8,128)S(1)}, u32[]{:S(2)}, u32[]{:S(2)}) collective-permute-start(f32[68,128]{1,0:T(8,128)S(1)} %relay1.1), channel_id=1, source_target_pairs={{0,4},{1,5},{2,6},{3,7},{4,0},{5,1},{6,2},{7,3},{8,12},{9,13},{10,... | collective-permute-start | bytes 104456 | tf_op jit(solution)/shard_map/ppermute | solution.py:456
  10.6 0.4 %work.1.refs_0_ = f32[5,8,16,128]{3,2,1,0:T(8,128)S(1)} custom-call(f32[5,8,16,128]{3,2,1,0:T(8,128)S(1)} %get-tuple-element.34.lam_ref, f32[12,8,16,128]{3,2,1,0:T(8,128)S(1)} %get-tuple-element.35.couple_ref), custom_call_target="tpu_custom_call" | custom-call | flops 1000000 | bytes 3000000 | tf_op jit(solution)/shard_map/work/pallas_call | solution.py:434
  11.1 0.5 %collective-permute-done.2.refs_9_ = f32[72,128]{1,0:T(8,128)S(1)} collective-permute-done((f32[72,128]{1,0:T(8,128)S(1)}, f32[72,128]{1,0:T(8,128)S(1)}, u32[]{:S(2)}, u32[]{:S(2)}) %collective-permute-start.2) | collective-permute-done | bytes 36896 | tf_op jit(solution)/shard_map/ppermute | solution.py:456
  11.6 0.0 collective-permute-done.1.refs_8_
  11.6 0.0 collective-permute-done.refs_7_
  11.6 0.0 collective-permute-done.4.refs_10_
  11.6 0.0 collective-permute-done.6.refs_11_
  11.6 0.7 %finish0.1 = (f32[5,8,16,128]{3,2,1,0:T(8,128)S(1)}, f32[5,8,16,128]{3,2,1,0:T(8,128)S(1)}, f32[88,128]{1,0:T(8,128)S(1)}, f32[80,128]{1,0:T(8,128)S(1)}, f32[24,128]{1,0:T(8,128)S(1)}, /*index=5*/f32[16,128]{1,0:T(8,128)S(1)}) custom-call(f32[5,8,16,128]{3,2,1,0:T(8,128)S(1)} %work.1.refs_0_, f32[5,5,8,16,128]{4,3,2,1,0:T(8,128)S(1)} %get-tuple-element.36.refs_1_.jac_ref, ...), custom_call_target="tpu_custom_call" | custom-call | flops 1000000 | bytes 3000000 | tf_op jit(solution)/shard_map/finish0/pallas_call | solution.py:434
  12.3 3.2 %collective-permute-start.7 = (f32[88,128]{1,0:T(8,128)S(1)}, f32[88,128]{1,0:T(8,128)S(1)}, u32[]{:S(2)}, u32[]{:S(2)}) collective-permute-start(f32[88,128]{1,0:T(8,128)S(1)} %get-tuple-element.54), channel_id=1, source_target_pairs={{0,1},{1,0},{2,3},{3,2},{4,5},{5,4},{6,7},{7,6},{8,9},{9,8},{10,11... | collective-permute-start | bytes 135176 | tf_op jit(solution)/shard_map/ppermute | solution.py:456
  15.5 0.0 collective-permute-start.8
  15.5 1.0 %collective-permute-start.9 = (f32[24,128]{1,0:T(8,128)S(1)}, f32[24,128]{1,0:T(8,128)S(1)}, u32[]{:S(2)}, u32[]{:S(2)}) collective-permute-start(f32[24,128]{1,0:T(8,128)S(1)} %get-tuple-element.56), channel_id=1, source_target_pairs={{0,12},{1,13},{2,14},{3,15},{4,8},{5,9},{6,10},{7,11},{8,4},{9,5},... | collective-permute-start | bytes 36872 | tf_op jit(solution)/shard_map/ppermute | solution.py:456
  16.5 0.0 collective-permute-start.10
  16.5 0.9 %local1.1 = (f32[5,8,16,128]{3,2,1,0:T(8,128)S(1)}, f32[5,5,16,128]{3,2,1,0:T(8,128)S(1)}, f32[5,5,16,128]{3,2,1,0:T(8,128)S(1)}, f32[5,5,16,128]{3,2,1,0:T(8,128)S(1)}) custom-call(f32[5,8,16,128]{3,2,1,0:T(8,128)S(1)} %get-tuple-element.48.lam_ref, f32[12,8,16,128]{3,2,1,0:T(8,128)S(1)} %get-tuple-element.35.couple_ref, ...), custom_call_target="tpu_custom_call" | custom-call | flops 1000000 | bytes 3000000 | tf_op jit(solution)/shard_map/local1/pallas_call | solution.py:434
  17.4 0.2 collective-permute-done.10.refs_9_
  17.7 0.9 %collective-permute-done.9.refs_8_ = f32[24,128]{1,0:T(8,128)S(1)} collective-permute-done((f32[24,128]{1,0:T(8,128)S(1)}, f32[24,128]{1,0:T(8,128)S(1)}, u32[]{:S(2)}, u32[]{:S(2)}) %collective-permute-start.9) | collective-permute-done | bytes 12320 | tf_op jit(solution)/shard_map/ppermute | solution.py:456
  18.6 0.0 collective-permute-done.8.refs_7_
  18.6 0.0 collective-permute-done.7.refs_6_
  18.6 0.4 %finish1.1 = (f32[5,8,16,128]{3,2,1,0:T(8,128)S(1)}, f32[88,128]{1,0:T(8,128)S(1)}, f32[80,128]{1,0:T(8,128)S(1)}, f32[24,128]{1,0:T(8,128)S(1)}, f32[16,128]{1,0:T(8,128)S(1)}) custom-call(f32[5,8,16,128]{3,2,1,0:T(8,128)S(1)} %get-tuple-element.50.refs_0_, f32[2,16,128]{2,1,0:T(8,128)S(1)} %get-tuple-element.40.refs_5_.refs_1_, ...), custom_call_target="tpu_custom_call" | custom-call | flops 1000000 | bytes 3000000 | tf_op jit(solution)/shard_map/finish1/pallas_call | solution.py:434
  19.0 1.6 %collective-permute-start.11 = (f32[88,128]{1,0:T(8,128)S(1)}, f32[88,128]{1,0:T(8,128)S(1)}, u32[]{:S(2)}, u32[]{:S(2)}) collective-permute-start(f32[88,128]{1,0:T(8,128)S(1)} %get-tuple-element.59), channel_id=1, source_target_pairs={{0,1},{1,0},{2,3},{3,2},{4,5},{5,4},{6,7},{7,6},{8,9},{9,8},{10,11... | collective-permute-start | bytes 135176 | tf_op jit(solution)/shard_map/ppermute | solution.py:456
  20.6 0.0 collective-permute-start.12
  20.6 1.0 %collective-permute-start.13 = (f32[24,128]{1,0:T(8,128)S(1)}, f32[24,128]{1,0:T(8,128)S(1)}, u32[]{:S(2)}, u32[]{:S(2)}) collective-permute-start(f32[24,128]{1,0:T(8,128)S(1)} %get-tuple-element.61), channel_id=1, source_target_pairs={{0,12},{1,13},{2,14},{3,15},{4,8},{5,9},{6,10},{7,11},{8,4},{9,5},... | collective-permute-start | bytes 36872 | tf_op jit(solution)/shard_map/ppermute | solution.py:456
  21.6 0.0 collective-permute-start.14
  21.6 0.5 %local2.1.refs_0_ = f32[5,8,16,128]{3,2,1,0:T(8,128)S(1)} custom-call(f32[5,8,16,128]{3,2,1,0:T(8,128)S(1)} %get-tuple-element.58.lam_ref, f32[12,8,16,128]{3,2,1,0:T(8,128)S(1)} %get-tuple-element.35.couple_ref, f32[5,5,8,16,128]{4,3,2,1,0:T(8,128)S(1)} %get-tuple-element.36.refs_1_.jac_ref, f32[5,8,16,128]{3,2,1,0:T(8,128)S(1)} %get-tuple-element.49.rhs_ref, ...), custom_call_target="tpu_custom_call" | custom-call | flops 1000000 | bytes 3000000 | tf_op jit(solution)/shard_map/local2/pallas_call | solution.py:434
  22.1 0.6 %collective-permute-done.14.refs_9_ = f32[16,128]{1,0:T(8,128)S(1)} collective-permute-done((f32[16,128]{1,0:T(8,128)S(1)}, f32[16,128]{1,0:T(8,128)S(1)}, u32[]{:S(2)}, u32[]{:S(2)}) %collective-permute-start.14) | collective-permute-done | bytes 8224 | tf_op jit(solution)/shard_map/ppermute | solution.py:456
  22.8 1.0 %collective-permute-done.13.refs_8_ = f32[24,128]{1,0:T(8,128)S(1)} collective-permute-done((f32[24,128]{1,0:T(8,128)S(1)}, f32[24,128]{1,0:T(8,128)S(1)}, u32[]{:S(2)}, u32[]{:S(2)}) %collective-permute-start.13) | collective-permute-done | bytes 12320 | tf_op jit(solution)/shard_map/ppermute | solution.py:456
  23.8 0.0 collective-permute-done.12.refs_7_
  23.8 0.0 collective-permute-done.11.refs_6_
  23.8 1.0 %finish2.1 = f32[5,8,16,128]{3,2,1,0:T(8,128)} custom-call(f32[5,8,16,128]{3,2,1,0:T(8,128)S(1)} %local2.1.refs_0_, f32[2,16,128]{2,1,0:T(8,128)S(1)} %get-tuple-element.40.refs_5_.refs_1_, f32[4,16,128]{2,1,0:T(8,128)S(1)} %get-tuple-element.41.refs_6_.refs_2_, f32[5,5,16,128]{3,2,1,0:T(8,128)S(1)} %get-tuple-element.51.refs_3_, ...), custom_call_target="tpu_custom_call" | custom-call | flops 1000000 | bytes 3000000 | tf_op jit(solution)/shard_map/finish2/pallas_call | solution.py:434
  (2 shorter events, 0.0 us)
Async XLA Ops:
  1.9 8.2 %collective-permute-start.5 = (f32[128,128]{1,0:T(8,128)S(1)}, f32[128,128]{1,0:T(8,128)S(1)}, u32[]{:S(2)}, u32[]{:S(2)}) collective-permute-start(f32[128,128]{1,0:T(8,128)S(1)} %get-tuple-element.47), channel_id=1, source_target_pairs={{0,24},{1,25},{2,26},{3,27},{4,28},{5,29},{6,30},{7,31},{8,16},{9,... | collective-permute-start | bytes 196616 | tf_op jit(solution)/shard_map/ppermute | solution.py:456
  5.9 4.2 %collective-permute-start.3 = (f32[120,128]{1,0:T(8,128)S(1)}, f32[120,128]{1,0:T(8,128)S(1)}, u32[]{:S(2)}, u32[]{:S(2)}) collective-permute-start(f32[120,128]{1,0:T(8,128)S(1)} %get-tuple-element.46), channel_id=1, source_target_pairs={{0,16},{1,17},{2,18},{3,19},{4,20},{5,21},{6,22},{7,23},{8,24},{9,... | collective-permute-start | bytes 184328 | tf_op jit(solution)/shard_map/ppermute | solution.py:456
  6.6 5.0 %collective-permute-start = (f32[88,128]{1,0:T(8,128)S(1)}, f32[88,128]{1,0:T(8,128)S(1)}, u32[]{:S(2)}, u32[]{:S(2)}) collective-permute-start(f32[88,128]{1,0:T(8,128)S(1)} %get-tuple-element.42), channel_id=1, source_target_pairs={{0,1},{1,0},{2,3},{3,2},{4,5},{5,4},{6,7},{7,6},{8,9},{9,8},{10,11... | collective-permute-start | bytes 135176 | tf_op jit(solution)/shard_map/ppermute | solution.py:456
  8.2 3.4 %collective-permute-start.1 = (f32[80,128]{1,0:T(8,128)S(1)}, f32[80,128]{1,0:T(8,128)S(1)}, u32[]{:S(2)}, u32[]{:S(2)}) collective-permute-start(f32[80,128]{1,0:T(8,128)S(1)} %get-tuple-element.43), channel_id=1, source_target_pairs={{0,4},{1,2},{2,1},{3,7},{4,0},{5,6},{6,5},{7,3},{8,12},{9,10},{10,... | collective-permute-start | bytes 122888 | tf_op jit(solution)/shard_map/ppermute | solution.py:456
  8.2 3.4 %collective-permute-start.2 = (f32[72,128]{1,0:T(8,128)S(1)}, f32[72,128]{1,0:T(8,128)S(1)}, u32[]{:S(2)}, u32[]{:S(2)}) collective-permute-start(f32[72,128]{1,0:T(8,128)S(1)} %get-tuple-element.44), channel_id=1, source_target_pairs={{0,12},{1,13},{2,14},{3,15},{4,8},{5,9},{6,10},{7,11},{8,4},{9,5},... | collective-permute-start | bytes 110600 | tf_op jit(solution)/shard_map/ppermute | solution.py:456
  10.1 1.5 %collective-permute-start.4 = (f32[68,128]{1,0:T(8,128)S(1)}, f32[68,128]{1,0:T(8,128)S(1)}, u32[]{:S(2)}, u32[]{:S(2)}) collective-permute-start(f32[68,128]{1,0:T(8,128)S(1)} %relay0.1), channel_id=1, source_target_pairs={{0,4},{1,5},{2,6},{3,7},{4,0},{5,1},{6,2},{7,3},{8,12},{9,13},{10,... | collective-permute-start | bytes 104456 | tf_op jit(solution)/shard_map/ppermute | solution.py:456
  10.1 1.5 %collective-permute-start.6 = (f32[68,128]{1,0:T(8,128)S(1)}, f32[68,128]{1,0:T(8,128)S(1)}, u32[]{:S(2)}, u32[]{:S(2)}) collective-permute-start(f32[68,128]{1,0:T(8,128)S(1)} %relay1.1), channel_id=1, source_target_pairs={{0,4},{1,5},{2,6},{3,7},{4,0},{5,1},{6,2},{7,3},{8,12},{9,13},{10,... | collective-permute-start | bytes 104456 | tf_op jit(solution)/shard_map/ppermute | solution.py:456
  12.3 6.3 %collective-permute-start.7 = (f32[88,128]{1,0:T(8,128)S(1)}, f32[88,128]{1,0:T(8,128)S(1)}, u32[]{:S(2)}, u32[]{:S(2)}) collective-permute-start(f32[88,128]{1,0:T(8,128)S(1)} %get-tuple-element.54), channel_id=1, source_target_pairs={{0,1},{1,0},{2,3},{3,2},{4,5},{5,4},{6,7},{7,6},{8,9},{9,8},{10,11... | collective-permute-start | bytes 135176 | tf_op jit(solution)/shard_map/ppermute | solution.py:456
  15.5 3.1 %collective-permute-start.8 = (f32[80,128]{1,0:T(8,128)S(1)}, f32[80,128]{1,0:T(8,128)S(1)}, u32[]{:S(2)}, u32[]{:S(2)}) collective-permute-start(f32[80,128]{1,0:T(8,128)S(1)} %get-tuple-element.55), channel_id=1, source_target_pairs={{0,4},{1,2},{2,1},{3,7},{4,0},{5,6},{6,5},{7,3},{8,12},{9,10},{10,... | collective-permute-start | bytes 122888 | tf_op jit(solution)/shard_map/ppermute | solution.py:456
  15.5 3.1 %collective-permute-start.9 = (f32[24,128]{1,0:T(8,128)S(1)}, f32[24,128]{1,0:T(8,128)S(1)}, u32[]{:S(2)}, u32[]{:S(2)}) collective-permute-start(f32[24,128]{1,0:T(8,128)S(1)} %get-tuple-element.56), channel_id=1, source_target_pairs={{0,12},{1,13},{2,14},{3,15},{4,8},{5,9},{6,10},{7,11},{8,4},{9,5},... | collective-permute-start | bytes 36872 | tf_op jit(solution)/shard_map/ppermute | solution.py:456
  16.5 1.2 %collective-permute-start.10 = (f32[16,128]{1,0:T(8,128)S(1)}, f32[16,128]{1,0:T(8,128)S(1)}, u32[]{:S(2)}, u32[]{:S(2)}) collective-permute-start(f32[16,128]{1,0:T(8,128)S(1)} %get-tuple-element.57), channel_id=1, source_target_pairs={{0,4},{1,5},{2,6},{3,7},{4,0},{5,1},{6,2},{7,3},{8,12},{9,13},{10,... | collective-permute-start | bytes 24584 | tf_op jit(solution)/shard_map/ppermute | solution.py:456
  19.0 4.7 %collective-permute-start.11 = (f32[88,128]{1,0:T(8,128)S(1)}, f32[88,128]{1,0:T(8,128)S(1)}, u32[]{:S(2)}, u32[]{:S(2)}) collective-permute-start(f32[88,128]{1,0:T(8,128)S(1)} %get-tuple-element.59), channel_id=1, source_target_pairs={{0,1},{1,0},{2,3},{3,2},{4,5},{5,4},{6,7},{7,6},{8,9},{9,8},{10,11... | collective-permute-start | bytes 135176 | tf_op jit(solution)/shard_map/ppermute | solution.py:456
  20.6 3.1 %collective-permute-start.12 = (f32[80,128]{1,0:T(8,128)S(1)}, f32[80,128]{1,0:T(8,128)S(1)}, u32[]{:S(2)}, u32[]{:S(2)}) collective-permute-start(f32[80,128]{1,0:T(8,128)S(1)} %get-tuple-element.60), channel_id=1, source_target_pairs={{0,4},{1,2},{2,1},{3,7},{4,0},{5,6},{6,5},{7,3},{8,12},{9,10},{10,... | collective-permute-start | bytes 122888 | tf_op jit(solution)/shard_map/ppermute | solution.py:456
  20.6 3.1 %collective-permute-start.13 = (f32[24,128]{1,0:T(8,128)S(1)}, f32[24,128]{1,0:T(8,128)S(1)}, u32[]{:S(2)}, u32[]{:S(2)}) collective-permute-start(f32[24,128]{1,0:T(8,128)S(1)} %get-tuple-element.61), channel_id=1, source_target_pairs={{0,12},{1,13},{2,14},{3,15},{4,8},{5,9},{6,10},{7,11},{8,4},{9,5},... | collective-permute-start | bytes 36872 | tf_op jit(solution)/shard_map/ppermute | solution.py:456
  21.6 1.2 %collective-permute-start.14 = (f32[16,128]{1,0:T(8,128)S(1)}, f32[16,128]{1,0:T(8,128)S(1)}, u32[]{:S(2)}, u32[]{:S(2)}) collective-permute-start(f32[16,128]{1,0:T(8,128)S(1)} %get-tuple-element.62), channel_id=1, source_target_pairs={{0,4},{1,5},{2,6},{3,7},{4,0},{5,1},{6,2},{7,3},{8,12},{9,13},{10,... | collective-permute-start | bytes 24584 | tf_op jit(solution)/shard_map/ppermute | solution.py:456

commit v5 on v4

--- a/solution.py
+++ b/solution.py
@@ -110,20 +110,34 @@
     packer.write(ahead_ref, back_ref, across_ref, [mate_ref.at[:SUB], mate_ref.at[SUB:]])
 
 
-def load_kernel(adjoint_ref, donors_in, couple_in, src_in, jac_in, targets_in, counts_in, weights_in, *refs):
-    lam_ref, couple_ref, src_ref, jac_ref, placed_ref, inv_ref, cols_ref, rows_ref, *tile_refs = refs[:-5]
-    donors_ref, targets_ref, counts_ref, weights_ref, sems = refs[-5:]
+def fetch_kernel(couple_ref, jac_in, targets_in, counts_in, weights_in, *refs):
+    jac_ref, placed_ref, inv_ref, cols_ref, rows_ref, targets_ref, counts_ref, weights_ref, sems = refs
+    count = jac_ref.shape[0]
+    slim = [
+        pltpu.make_async_copy(targets_in, targets_ref, sems.at[count]),
+        pltpu.make_async_copy(counts_in, counts_ref, sems.at[count + 1]),
+        pltpu.make_async_copy(weights_in, weights_ref, sems.at[count + 2]),
+    ]
+    wide = [pltpu.make_async_copy(jac_in.at[s], jac_ref.at[s], sems.at[s]) for s in range(count)]
+    for copy in slim + wide:
+        copy.start()
+    coefs_of(couple_ref, inv_ref, cols_ref, rows_ref)
+    for copy in slim:
+        copy.wait()
+    place_weights(targets_ref, counts_ref, weights_ref, placed_ref)
+    for copy in wide:
+        copy.wait()
+
+
+def load_kernel(adjoint_ref, donors_in, couple_in, src_in, *refs):
+    lam_ref, couple_ref, src_ref, *tile_refs, donors_ref, sems = refs
     nv, na, nr, _ = lam_ref.shape
     copies = [
         pltpu.make_async_copy(donors_in, donors_ref, sems.at[0]),
         pltpu.make_async_copy(adjoint_ref, lam_ref, sems.at[1]),
-        pltpu.make_async_copy(targets_in, targets_ref, sems.at[2]),
-        pltpu.make_async_copy(counts_in, counts_ref, sems.at[3]),
-        pltpu.make_async_copy(weights_in, weights_ref, sems.at[4]),
-        pltpu.make_async_copy(couple_in, couple_ref, sems.at[5]),
-        pltpu.make_async_copy(src_in, src_ref, sems.at[6]),
+        pltpu.make_async_copy(couple_in, couple_ref, sems.at[2]),
+        pltpu.make_async_copy(src_in, src_ref, sems.at[3]),
     ]
-    copies += [pltpu.make_async_copy(jac_in.at[s], jac_ref.at[s], sems.at[7 + s]) for s in range(nv)]
     for copy in copies:
         copy.start()
     copies[0].wait()
@@ -138,12 +152,7 @@
                     for a in range(2):
                         at = ((part * slots + k) * nv + v) * 2 + a
                         tile_ref[at : at + 1, :] = lam_ref[v, na - 2 + a, pl.ds(row, 1), :]
-    for copy in copies[2:5]:
-        copy.wait()
-    place_weights(targets_ref, counts_ref, weights_ref, placed_ref)
-    copies[5].wait()
-    coefs_of(couple_ref, inv_ref, cols_ref, rows_ref)
-    for copy in copies[6:]:
+    for copy in copies[2:]:
         copy.wait()
 
 
@@ -307,7 +316,7 @@
                 high_ref[s, b, half_rows(q), :] = gather.got["high", q]
 
 
-def relay_kernel(first, cols_ref, tile_ref, out_ref, *, share):
+def relay_kernel(first, cols_ref, tile_ref, _, out_ref, *, share):
     half = out_ref.shape[0] - share
     out_ref[share:, :] = tile_ref[half : 2 * half, :]
     if first < cols_ref.shape[0]:
@@ -450,6 +459,7 @@
     vmem = lambda *shape: pltpu.VMEM(shape, jnp.float32)
     inside = pl.BlockSpec(memory_space=pltpu.VMEM)
     outside = pl.BlockSpec(memory_space=pltpu.HBM)
+    unread = pl.BlockSpec(memory_space=pl.ANY)
     far = lambda x: pltpu.with_memory_space_constraint(x, pltpu.HBM)
 
     def sent(x, pairs):
@@ -462,17 +472,11 @@
         sides = 2 * nv * na
         edges = lambda across: [vmem(sides + SUB, nc), vmem(sides, nc), vmem(across, nc), vmem(nr, nc)]
         block = vmem(nv, na, nr, nc)
-        lam, cpl, rhs, jac, placed, inv, edge_coefs, row_coefs, *tiles = call(
+        lam, cpl, rhs, *tiles = call(
             load_kernel, "load",
-            [block, vmem(12, na, nr, nc), block, vmem(nv, nv, na, nr, nc), vmem(donors, slots, nr, nc),
-             vmem(na, nr, nc), vmem(2, nr, nc), vmem(4, 2 * na, nc)]
-            + [vmem(4 * slots * nv + SUB * n, nc) for n in range(count)],
-            [*map(far, (adjoint[0], donor_row[0], couple[0], source[0], jacobian[0], target_row[0],
-                        tile_count[0], weights.reshape(-1, nc)))],
-            [outside] * 8,
-            [pltpu.SMEM(donor_row.shape[1:], jnp.int32), pltpu.SMEM(target_row.shape[1:], jnp.int32),
-             pltpu.SMEM(tile_count.shape[1:], jnp.int32), pltpu.VMEM((donors * slots, nc), jnp.float32),
-             pltpu.SemaphoreType.DMA((7 + nv,))],
+            [block, vmem(12, na, nr, nc), block] + [vmem(4 * slots * nv + SUB * n, nc) for n in range(count)],
+            [*map(far, (adjoint[0], donor_row[0], couple[0], source[0]))], [outside] * 4,
+            [pltpu.SMEM(donor_row.shape[1:], jnp.int32), pltpu.SemaphoreType.DMA((4,))],
         )
         ahead, back, cross, cols = call(pack_kernel, "pack", edges(sides - SUB), [lam])
         tiles = [sent(x, pairs) for x, pairs in zip(tiles, route["faces"])]
@@ -483,9 +487,18 @@
             across = sent(cross, route["across"])
             if sweep == 0:
                 share = shares(count)
+                jac, placed, inv, edge_coefs, row_coefs = call(
+                    fetch_kernel, "fetch",
+                    [vmem(nv, nv, na, nr, nc), vmem(donors, slots, nr, nc), vmem(na, nr, nc),
+                     vmem(2, nr, nc), vmem(4, 2 * na, nc)],
+                    [cpl, *map(far, (jacobian[0], target_row[0], tile_count[0], weights.reshape(-1, nc)))],
+                    [inside] + [outside] * 4,
+                    [pltpu.SMEM(target_row.shape[1:], jnp.int32), pltpu.SMEM(tile_count.shape[1:], jnp.int32),
+                     pltpu.VMEM((donors * slots, nc), jnp.float32), pltpu.SemaphoreType.DMA((nv + 3,))],
+                )
                 relayed = [
                     call(functools.partial(relay_kernel, share * n, share=share), f"relay{n}",
-                         [vmem(share + 2 * slots * nv, nc)], [cols, x])[0]
+                         [vmem(share + 2 * slots * nv, nc)], [cols, x, inv], [inside] * 2 + [unread])[0]
                     for n, x in enumerate(tiles)
                 ]
                 relayed = [sent(x, route["mate"]) for x in relayed]

time: 25 us -> 24.5 us (0.980)
  waiting for transfers between devices: 4.61 us -> 2.61 us
  Pallas kernels: 6 us -> 6.89 us
  starting transfers between devices: 14.1 us -> 14.6 us
    ppermute x15, waiting for transfers between devices: 4.61 us -> 2.61 us  [sent(): return lax.ppermute(x, AXES, pairs)]
    pallas_call x10 -> x11, Pallas kernels: 6 us -> 6.89 us  [call(): pl.pallas_call(kernel, out_shape=outs, in_specs=[vmem] * len(args) if spe...]
    ppermute x15, starting transfers between devices: 14.1 us -> 14.6 us  [sent(): return lax.ppermute(x, AXES, pairs)]
  transfers between devices with their start and end apart: 15 -> 15, of which waited for: 6 -> 7; matrix products, arithmetic and copies ran while one was open for 0% -> 0% of each run, Pallas kernels for 8% -> 14%
where the time goes in v5:
time: 24.5 us; the launch traced here: 24.2 us
  starting transfers between devices  14.6 us (60%)
  Pallas kernels  6.89 us (28%)
  waiting for transfers between devices  2.61 us (11%)
    ppermute x15, starting transfers between devices, sent(): return lax.ppermute(x, AXES, pairs)  14.6 us
    pallas_call x11, Pallas kernels, call(): pl.pallas_call(kernel, out_shape=outs, in_specs=[vmem] * len(args) if spe...  6.89 us
    ppermute x15, waiting for transfers between devices, sent(): return lax.ppermute(x, AXES, pairs)  2.61 us
  transfers between devices with their start and end apart: 15, of which 7 were waited for; matrix products, arithmetic and copies ran while one was open for 0% of the time, Pallas kernels for 14%

profile of v5, /device:TPU:0, one launch (start us, length us, event | category | flops | bytes accessed | tf_op | source)
XLA Modules:
  0.0 24.2 jit_solution(7504116274944051738)
XLA Ops:
  0.0 1.3 %load.1 = (f32[5,8,16,128]{3,2,1,0:T(8,128)S(1)}, f32[12,8,16,128]{3,2,1,0:T(8,128)S(1)}, f32[5,8,16,128]{3,2,1,0:T(8,128)S(1)}, f32[120,128]{1,0:T(8,128)S(1)}, f32[128,128]{1,0:T(8,128)S(1)}) custom-call(f32[5,8,16,128]{3,2,1,0:T(8,128)} %bitcast.11, s32[4,4,6]{2,1,0:T(4,128)} %bitcast.14, f32[12,8,16,128]{3,2,1,0:T(8,128)} %bitcast.10, ...), custom_call_target="tpu_custom_call" | custom-call | flops 1000000 | bytes 3000000 | tf_op jit(solution)/shard_map/load/pallas_call | solution.py:443
  1.4 4.0 %collective-permute-start.5 = (f32[128,128]{1,0:T(8,128)S(1)}, f32[128,128]{1,0:T(8,128)S(1)}, u32[]{:S(2)}, u32[]{:S(2)}) collective-permute-start(f32[128,128]{1,0:T(8,128)S(1)} %get-tuple-element.47), channel_id=1, source_target_pairs={{0,24},{1,25},{2,26},{3,27},{4,28},{5,29},{6,30},{7,31},{8,16},{9,... | collective-permute-start | bytes 196616 | tf_op jit(solution)/shard_map/ppermute | solution.py:466
  5.3 0.5 %collective-permute-start.3 = (f32[120,128]{1,0:T(8,128)S(1)}, f32[120,128]{1,0:T(8,128)S(1)}, u32[]{:S(2)}, u32[]{:S(2)}) collective-permute-start(f32[120,128]{1,0:T(8,128)S(1)} %get-tuple-element.46), channel_id=1, source_target_pairs={{0,16},{1,17},{2,18},{3,19},{4,20},{5,21},{6,22},{7,23},{8,24},{9,... | collective-permute-start | bytes 184328 | tf_op jit(solution)/shard_map/ppermute | solution.py:466
  5.8 0.1 pack.1
  6.0 1.6 %collective-permute-start = (f32[88,128]{1,0:T(8,128)S(1)}, f32[88,128]{1,0:T(8,128)S(1)}, u32[]{:S(2)}, u32[]{:S(2)}) collective-permute-start(f32[88,128]{1,0:T(8,128)S(1)} %get-tuple-element.42), channel_id=1, source_target_pairs={{0,1},{1,0},{2,3},{3,2},{4,5},{5,4},{6,7},{7,6},{8,9},{9,8},{10,11... | collective-permute-start | bytes 135176 | tf_op jit(solution)/shard_map/ppermute | solution.py:466
  7.6 0.0 collective-permute-start.1
  7.6 0.6 %collective-permute-start.2 = (f32[72,128]{1,0:T(8,128)S(1)}, f32[72,128]{1,0:T(8,128)S(1)}, u32[]{:S(2)}, u32[]{:S(2)}) collective-permute-start(f32[72,128]{1,0:T(8,128)S(1)} %get-tuple-element.44), channel_id=1, source_target_pairs={{0,12},{1,13},{2,14},{3,15},{4,8},{5,9},{6,10},{7,11},{8,4},{9,5},... | collective-permute-start | bytes 110600 | tf_op jit(solution)/shard_map/ppermute | solution.py:466
  8.3 1.5 %fetch.1 = (f32[5,5,8,16,128]{4,3,2,1,0:T(8,128)S(1)}, f32[4,6,16,128]{3,2,1,0:T(8,128)S(1)}, f32[8,16,128]{2,1,0:T(8,128)S(1)}, f32[2,16,128]{2,1,0:T(8,128)S(1)}, f32[4,16,128]{2,1,0:T(8,128)S(1)}) custom-call(f32[12,8,16,128]{3,2,1,0:T(8,128)S(1)} %get-tuple-element.35.couple_ref, f32[5,5,8,16,128]{4,3,2,1,0:T(8,128)} %bitcast.9, s32[4,4,6]{2,1,0:T(4,128)} %bitcast.15, ...), custom_call_target="tpu_custom_call" | custom-call | flops 1000000 | bytes 3000000 | tf_op jit(solution)/shard_map/fetch/pallas_call | solution.py:443
  9.8 0.0 collective-permute-done.3.tile_ref.refs_12_
  9.8 0.1 collective-permute-start.4
  9.9 0.0 collective-permute-done.5.tile_ref.refs_13_
  9.9 0.5 %collective-permute-start.6 = (f32[68,128]{1,0:T(8,128)S(1)}, f32[68,128]{1,0:T(8,128)S(1)}, u32[]{:S(2)}, u32[]{:S(2)}) collective-permute-start(f32[68,128]{1,0:T(8,128)S(1)} %relay1.1), channel_id=1, source_target_pairs={{0,4},{1,5},{2,6},{3,7},{4,0},{5,1},{6,2},{7,3},{8,12},{9,13},{10,... | collective-permute-start | bytes 104456 | tf_op jit(solution)/shard_map/ppermute | solution.py:466
  10.4 0.4 %work.1.refs_0_ = f32[5,8,16,128]{3,2,1,0:T(8,128)S(1)} custom-call(f32[5,8,16,128]{3,2,1,0:T(8,128)S(1)} %get-tuple-element.34.lam_ref, f32[12,8,16,128]{3,2,1,0:T(8,128)S(1)} %get-tuple-element.35.couple_ref), custom_call_target="tpu_custom_call" | custom-call | flops 1000000 | bytes 3000000 | tf_op jit(solution)/shard_map/work/pallas_call | solution.py:443
  10.8 0.2 collective-permute-done.2.refs_9_
  11.0 0.0 collective-permute-done.1.refs_8_
  11.0 0.0 collective-permute-done.refs_7_
  11.0 0.1 collective-permute-done.4.refs_10_
  11.1 0.2 collective-permute-done.6.refs_11_
  11.2 0.7 %finish0.1 = (f32[5,8,16,128]{3,2,1,0:T(8,128)S(1)}, f32[5,8,16,128]{3,2,1,0:T(8,128)S(1)}, f32[88,128]{1,0:T(8,128)S(1)}, f32[80,128]{1,0:T(8,128)S(1)}, f32[24,128]{1,0:T(8,128)S(1)}, /*index=5*/f32[16,128]{1,0:T(8,128)S(1)}) custom-call(f32[5,8,16,128]{3,2,1,0:T(8,128)S(1)} %work.1.refs_0_, f32[5,5,8,16,128]{4,3,2,1,0:T(8,128)S(1)} %get-tuple-element.36.refs_1_.jac_ref, ...), custom_call_target="tpu_custom_call" | custom-call | flops 1000000 | bytes 3000000 | tf_op jit(solution)/shard_map/finish0/pallas_call | solution.py:443
  11.9 3.1 %collective-permute-start.7 = (f32[88,128]{1,0:T(8,128)S(1)}, f32[88,128]{1,0:T(8,128)S(1)}, u32[]{:S(2)}, u32[]{:S(2)}) collective-permute-start(f32[88,128]{1,0:T(8,128)S(1)} %get-tuple-element.54), channel_id=1, source_target_pairs={{0,1},{1,0},{2,3},{3,2},{4,5},{5,4},{6,7},{7,6},{8,9},{9,8},{10,11... | collective-permute-start | bytes 135176 | tf_op jit(solution)/shard_map/ppermute | solution.py:466
  15.0 0.0 collective-permute-start.8
  15.0 1.6 %collective-permute-start.9 = (f32[24,128]{1,0:T(8,128)S(1)}, f32[24,128]{1,0:T(8,128)S(1)}, u32[]{:S(2)}, u32[]{:S(2)}) collective-permute-start(f32[24,128]{1,0:T(8,128)S(1)} %get-tuple-element.56), channel_id=1, source_target_pairs={{0,12},{1,13},{2,14},{3,15},{4,8},{5,9},{6,10},{7,11},{8,4},{9,5},... | collective-permute-start | bytes 36872 | tf_op jit(solution)/shard_map/ppermute | solution.py:466
  16.6 0.0 collective-permute-start.10
  16.6 0.9 %local1.1 = (f32[5,8,16,128]{3,2,1,0:T(8,128)S(1)}, f32[5,5,16,128]{3,2,1,0:T(8,128)S(1)}, f32[5,5,16,128]{3,2,1,0:T(8,128)S(1)}, f32[5,5,16,128]{3,2,1,0:T(8,128)S(1)}) custom-call(f32[5,8,16,128]{3,2,1,0:T(8,128)S(1)} %get-tuple-element.48.lam_ref, f32[12,8,16,128]{3,2,1,0:T(8,128)S(1)} %get-tuple-element.35.couple_ref, ...), custom_call_target="tpu_custom_call" | custom-call | flops 1000000 | bytes 3000000 | tf_op jit(solution)/shard_map/local1/pallas_call | solution.py:443
  17.5 0.3 %collective-permute-done.10.refs_9_ = f32[16,128]{1,0:T(8,128)S(1)} collective-permute-done((f32[16,128]{1,0:T(8,128)S(1)}, f32[16,128]{1,0:T(8,128)S(1)}, u32[]{:S(2)}, u32[]{:S(2)}) %collective-permute-start.10) | collective-permute-done | bytes 8224 | tf_op jit(solution)/shard_map/ppermute | solution.py:466
  17.7 0.3 %collective-permute-done.9.refs_8_ = f32[24,128]{1,0:T(8,128)S(1)} collective-permute-done((f32[24,128]{1,0:T(8,128)S(1)}, f32[24,128]{1,0:T(8,128)S(1)}, u32[]{:S(2)}, u32[]{:S(2)}) %collective-permute-start.9) | collective-permute-done | bytes 12320 | tf_op jit(solution)/shard_map/ppermute | solution.py:466
  18.1 0.0 collective-permute-done.8.refs_7_
  18.1 0.0 collective-permute-done.7.refs_6_
  18.1 0.4 %finish1.1 = (f32[5,8,16,128]{3,2,1,0:T(8,128)S(1)}, f32[88,128]{1,0:T(8,128)S(1)}, f32[80,128]{1,0:T(8,128)S(1)}, f32[24,128]{1,0:T(8,128)S(1)}, f32[16,128]{1,0:T(8,128)S(1)}) custom-call(f32[5,8,16,128]{3,2,1,0:T(8,128)S(1)} %get-tuple-element.50.refs_0_, f32[2,16,128]{2,1,0:T(8,128)S(1)} %get-tuple-element.40.refs_5_.refs_1_, ...), custom_call_target="tpu_custom_call" | custom-call | flops 1000000 | bytes 3000000 | tf_op jit(solution)/shard_map/finish1/pallas_call | solution.py:443
  18.5 1.6 %collective-permute-start.11 = (f32[88,128]{1,0:T(8,128)S(1)}, f32[88,128]{1,0:T(8,128)S(1)}, u32[]{:S(2)}, u32[]{:S(2)}) collective-permute-start(f32[88,128]{1,0:T(8,128)S(1)} %get-tuple-element.59), channel_id=1, source_target_pairs={{0,1},{1,0},{2,3},{3,2},{4,5},{5,4},{6,7},{7,6},{8,9},{9,8},{10,11... | collective-permute-start | bytes 135176 | tf_op jit(solution)/shard_map/ppermute | solution.py:466
  20.1 0.0 collective-permute-start.12
  20.1 1.0 %collective-permute-start.13 = (f32[24,128]{1,0:T(8,128)S(1)}, f32[24,128]{1,0:T(8,128)S(1)}, u32[]{:S(2)}, u32[]{:S(2)}) collective-permute-start(f32[24,128]{1,0:T(8,128)S(1)} %get-tuple-element.61), channel_id=1, source_target_pairs={{0,12},{1,13},{2,14},{3,15},{4,8},{5,9},{6,10},{7,11},{8,4},{9,5},... | collective-permute-start | bytes 36872 | tf_op jit(solution)/shard_map/ppermute | solution.py:466
  21.1 0.0 collective-permute-start.14
  21.1 0.5 %local2.1.refs_0_ = f32[5,8,16,128]{3,2,1,0:T(8,128)S(1)} custom-call(f32[5,8,16,128]{3,2,1,0:T(8,128)S(1)} %get-tuple-element.58.lam_ref, f32[12,8,16,128]{3,2,1,0:T(8,128)S(1)} %get-tuple-element.35.couple_ref, f32[5,5,8,16,128]{4,3,2,1,0:T(8,128)S(1)} %get-tuple-element.36.refs_1_.jac_ref, f32[5,8,16,128]{3,2,1,0:T(8,128)S(1)} %get-tuple-element.49.rhs_ref, ...), custom_call_target="tpu_custom_call" | custom-call | flops 1000000 | bytes 3000000 | tf_op jit(solution)/shard_map/local2/pallas_call | solution.py:443
  21.6 0.6 %collective-permute-done.14.refs_9_ = f32[16,128]{1,0:T(8,128)S(1)} collective-permute-done((f32[16,128]{1,0:T(8,128)S(1)}, f32[16,128]{1,0:T(8,128)S(1)}, u32[]{:S(2)}, u32[]{:S(2)}) %collective-permute-start.14) | collective-permute-done | bytes 8224 | tf_op jit(solution)/shard_map/ppermute | solution.py:466
  22.3 0.9 %collective-permute-done.13.refs_8_ = f32[24,128]{1,0:T(8,128)S(1)} collective-permute-done((f32[24,128]{1,0:T(8,128)S(1)}, f32[24,128]{1,0:T(8,128)S(1)}, u32[]{:S(2)}, u32[]{:S(2)}) %collective-permute-start.13) | collective-permute-done | bytes 12320 | tf_op jit(solution)/shard_map/ppermute | solution.py:466
  23.2 0.0 collective-permute-done.12.refs_7_
  23.2 0.0 collective-permute-done.11.refs_6_
  23.2 1.0 %finish2.1 = f32[5,8,16,128]{3,2,1,0:T(8,128)} custom-call(f32[5,8,16,128]{3,2,1,0:T(8,128)S(1)} %local2.1.refs_0_, f32[2,16,128]{2,1,0:T(8,128)S(1)} %get-tuple-element.40.refs_5_.refs_1_, f32[4,16,128]{2,1,0:T(8,128)S(1)} %get-tuple-element.41.refs_6_.refs_2_, f32[5,5,16,128]{3,2,1,0:T(8,128)S(1)} %get-tuple-element.51.refs_3_, ...), custom_call_target="tpu_custom_call" | custom-call | flops 1000000 | bytes 3000000 | tf_op jit(solution)/shard_map/finish2/pallas_call | solution.py:443
  (2 shorter events, 0.0 us)
Async XLA Ops:
  1.4 8.5 %collective-permute-start.5 = (f32[128,128]{1,0:T(8,128)S(1)}, f32[128,128]{1,0:T(8,128)S(1)}, u32[]{:S(2)}, u32[]{:S(2)}) collective-permute-start(f32[128,128]{1,0:T(8,128)S(1)} %get-tuple-element.47), channel_id=1, source_target_pairs={{0,24},{1,25},{2,26},{3,27},{4,28},{5,29},{6,30},{7,31},{8,16},{9,... | collective-permute-start | bytes 196616 | tf_op jit(solution)/shard_map/ppermute | solution.py:466
  5.3 4.5 %collective-permute-start.3 = (f32[120,128]{1,0:T(8,128)S(1)}, f32[120,128]{1,0:T(8,128)S(1)}, u32[]{:S(2)}, u32[]{:S(2)}) collective-permute-start(f32[120,128]{1,0:T(8,128)S(1)} %get-tuple-element.46), channel_id=1, source_target_pairs={{0,16},{1,17},{2,18},{3,19},{4,20},{5,21},{6,22},{7,23},{8,24},{9,... | collective-permute-start | bytes 184328 | tf_op jit(solution)/shard_map/ppermute | solution.py:466
  6.0 5.0 %collective-permute-start = (f32[88,128]{1,0:T(8,128)S(1)}, f32[88,128]{1,0:T(8,128)S(1)}, u32[]{:S(2)}, u32[]{:S(2)}) collective-permute-start(f32[88,128]{1,0:T(8,128)S(1)} %get-tuple-element.42), channel_id=1, source_target_pairs={{0,1},{1,0},{2,3},{3,2},{4,5},{5,4},{6,7},{7,6},{8,9},{9,8},{10,11... | collective-permute-start | bytes 135176 | tf_op jit(solution)/shard_map/ppermute | solution.py:466
  7.6 3.4 %collective-permute-start.1 = (f32[80,128]{1,0:T(8,128)S(1)}, f32[80,128]{1,0:T(8,128)S(1)}, u32[]{:S(2)}, u32[]{:S(2)}) collective-permute-start(f32[80,128]{1,0:T(8,128)S(1)} %get-tuple-element.43), channel_id=1, source_target_pairs={{0,4},{1,2},{2,1},{3,7},{4,0},{5,6},{6,5},{7,3},{8,12},{9,10},{10,... | collective-permute-start | bytes 122888 | tf_op jit(solution)/shard_map/ppermute | solution.py:466
  7.6 3.4 %collective-permute-start.2 = (f32[72,128]{1,0:T(8,128)S(1)}, f32[72,128]{1,0:T(8,128)S(1)}, u32[]{:S(2)}, u32[]{:S(2)}) collective-permute-start(f32[72,128]{1,0:T(8,128)S(1)} %get-tuple-element.44), channel_id=1, source_target_pairs={{0,12},{1,13},{2,14},{3,15},{4,8},{5,9},{6,10},{7,11},{8,4},{9,5},... | collective-permute-start | bytes 110600 | tf_op jit(solution)/shard_map/ppermute | solution.py:466
  9.8 1.3 %collective-permute-start.4 = (f32[68,128]{1,0:T(8,128)S(1)}, f32[68,128]{1,0:T(8,128)S(1)}, u32[]{:S(2)}, u32[]{:S(2)}) collective-permute-start(f32[68,128]{1,0:T(8,128)S(1)} %relay0.1), channel_id=1, source_target_pairs={{0,4},{1,5},{2,6},{3,7},{4,0},{5,1},{6,2},{7,3},{8,12},{9,13},{10,... | collective-permute-start | bytes 104456 | tf_op jit(solution)/shard_map/ppermute | solution.py:466
  9.9 1.3 %collective-permute-start.6 = (f32[68,128]{1,0:T(8,128)S(1)}, f32[68,128]{1,0:T(8,128)S(1)}, u32[]{:S(2)}, u32[]{:S(2)}) collective-permute-start(f32[68,128]{1,0:T(8,128)S(1)} %relay1.1), channel_id=1, source_target_pairs={{0,4},{1,5},{2,6},{3,7},{4,0},{5,1},{6,2},{7,3},{8,12},{9,13},{10,... | collective-permute-start | bytes 104456 | tf_op jit(solution)/shard_map/ppermute | solution.py:466
  11.9 6.2 %collective-permute-start.7 = (f32[88,128]{1,0:T(8,128)S(1)}, f32[88,128]{1,0:T(8,128)S(1)}, u32[]{:S(2)}, u32[]{:S(2)}) collective-permute-start(f32[88,128]{1,0:T(8,128)S(1)} %get-tuple-element.54), channel_id=1, source_target_pairs={{0,1},{1,0},{2,3},{3,2},{4,5},{5,4},{6,7},{7,6},{8,9},{9,8},{10,11... | collective-permute-start | bytes 135176 | tf_op jit(solution)/shard_map/ppermute | solution.py:466
  15.0 3.1 %collective-permute-start.8 = (f32[80,128]{1,0:T(8,128)S(1)}, f32[80,128]{1,0:T(8,128)S(1)}, u32[]{:S(2)}, u32[]{:S(2)}) collective-permute-start(f32[80,128]{1,0:T(8,128)S(1)} %get-tuple-element.55), channel_id=1, source_target_pairs={{0,4},{1,2},{2,1},{3,7},{4,0},{5,6},{6,5},{7,3},{8,12},{9,10},{10,... | collective-permute-start | bytes 122888 | tf_op jit(solution)/shard_map/ppermute | solution.py:466
  15.0 3.1 %collective-permute-start.9 = (f32[24,128]{1,0:T(8,128)S(1)}, f32[24,128]{1,0:T(8,128)S(1)}, u32[]{:S(2)}, u32[]{:S(2)}) collective-permute-start(f32[24,128]{1,0:T(8,128)S(1)} %get-tuple-element.56), channel_id=1, source_target_pairs={{0,12},{1,13},{2,14},{3,15},{4,8},{5,9},{6,10},{7,11},{8,4},{9,5},... | collective-permute-start | bytes 36872 | tf_op jit(solution)/shard_map/ppermute | solution.py:466
  16.6 1.2 %collective-permute-start.10 = (f32[16,128]{1,0:T(8,128)S(1)}, f32[16,128]{1,0:T(8,128)S(1)}, u32[]{:S(2)}, u32[]{:S(2)}) collective-permute-start(f32[16,128]{1,0:T(8,128)S(1)} %get-tuple-element.57), channel_id=1, source_target_pairs={{0,4},{1,5},{2,6},{3,7},{4,0},{5,1},{6,2},{7,3},{8,12},{9,13},{10,... | collective-permute-start | bytes 24584 | tf_op jit(solution)/shard_map/ppermute | solution.py:466
  18.5 4.7 %collective-permute-start.11 = (f32[88,128]{1,0:T(8,128)S(1)}, f32[88,128]{1,0:T(8,128)S(1)}, u32[]{:S(2)}, u32[]{:S(2)}) collective-permute-start(f32[88,128]{1,0:T(8,128)S(1)} %get-tuple-element.59), channel_id=1, source_target_pairs={{0,1},{1,0},{2,3},{3,2},{4,5},{5,4},{6,7},{7,6},{8,9},{9,8},{10,11... | collective-permute-start | bytes 135176 | tf_op jit(solution)/shard_map/ppermute | solution.py:466
  20.1 3.1 %collective-permute-start.12 = (f32[80,128]{1,0:T(8,128)S(1)}, f32[80,128]{1,0:T(8,128)S(1)}, u32[]{:S(2)}, u32[]{:S(2)}) collective-permute-start(f32[80,128]{1,0:T(8,128)S(1)} %get-tuple-element.60), channel_id=1, source_target_pairs={{0,4},{1,2},{2,1},{3,7},{4,0},{5,6},{6,5},{7,3},{8,12},{9,10},{10,... | collective-permute-start | bytes 122888 | tf_op jit(solution)/shard_map/ppermute | solution.py:466
  20.1 3.1 %collective-permute-start.13 = (f32[24,128]{1,0:T(8,128)S(1)}, f32[24,128]{1,0:T(8,128)S(1)}, u32[]{:S(2)}, u32[]{:S(2)}) collective-permute-start(f32[24,128]{1,0:T(8,128)S(1)} %get-tuple-element.61), channel_id=1, source_target_pairs={{0,12},{1,13},{2,14},{3,15},{4,8},{5,9},{6,10},{7,11},{8,4},{9,5},... | collective-permute-start | bytes 36872 | tf_op jit(solution)/shard_map/ppermute | solution.py:466
  21.1 1.2 %collective-permute-start.14 = (f32[16,128]{1,0:T(8,128)S(1)}, f32[16,128]{1,0:T(8,128)S(1)}, u32[]{:S(2)}, u32[]{:S(2)}) collective-permute-start(f32[16,128]{1,0:T(8,128)S(1)} %get-tuple-element.62), channel_id=1, source_target_pairs={{0,4},{1,5},{2,6},{3,7},{4,0},{5,1},{6,2},{7,3},{8,12},{9,13},{10,... | collective-permute-start | bytes 24584 | tf_op jit(solution)/shard_map/ppermute | solution.py:466

commit v6 on v5

--- a/solution.py
+++ b/solution.py
@@ -111,7 +111,8 @@
 
 
 def fetch_kernel(couple_ref, jac_in, targets_in, counts_in, weights_in, *refs):
-    jac_ref, placed_ref, inv_ref, cols_ref, rows_ref, targets_ref, counts_ref, weights_ref, sems = refs
+    jac_ref, placed_ref, inv_ref, cols_ref, rows_ref, *edge_refs = refs[:8]
+    targets_ref, counts_ref, weights_ref, sems = refs[8:]
     count = jac_ref.shape[0]
     slim = [
         pltpu.make_async_copy(targets_in, targets_ref, sems.at[count]),
@@ -125,8 +126,26 @@
     for copy in slim:
         copy.wait()
     place_weights(targets_ref, counts_ref, weights_ref, placed_ref)
-    for copy in wide:
+    for s, copy in enumerate(wide):
         copy.wait()
+        edge_matrices(s, jac_ref, inv_ref, *edge_refs)
+
+
+def edge_matrices(s, jac_ref, inv_ref, cols_ref, low_ref, high_ref):
+    nv, na = jac_ref.shape[1:3]
+    sub, lane = iotas()
+    for b in range(nv):
+        gather = Gather(sub, lane)
+        for a in range(na):
+            for half in range(2):
+                m = jac_ref[s, b, a, half_rows(half), :] * inv_ref[a, half_rows(half), :]
+                gather.cols("cols", half, a, m)
+                gather.rows("high" if half else "low", half, a, m)
+        for half in range(2):
+            cols_ref[s, b, half_rows(half), :] = gather.got["cols", half]
+        for q in range(na // 4):
+            low_ref[s, b, half_rows(q), :] = gather.got["low", q]
+            high_ref[s, b, half_rows(q), :] = gather.got["high", q]
 
 
 def load_kernel(adjoint_ref, donors_in, couple_in, src_in, *refs):
@@ -260,17 +279,6 @@
             rows_ref[i, half_rows(q), :] = gather.got[name, q]
 
 
-def work_kernel(lam_ref, couple_ref, near_ref):
-    sub, lane = iotas()
-    for a in range(lam_ref.shape[1]):
-        coef = [
-            inner_coefs([couple_ref[i, a, half_rows(h), :] for i in range(12)], h, sub, lane) for h in range(2)
-        ]
-        for v, both in enumerate(local_sums(lam_ref, a, coef, sub)):
-            for half, x in enumerate(both):
-                near_ref[v, a, half_rows(half), :] = x
-
-
 def donor_at(at):
     return jnp.where(at < 0, at + lax.axis_size("circ"), at)
 
@@ -284,10 +292,16 @@
     return x
 
 
-def local_kernel(prepare, lam_ref, couple_ref, jac_ref, rhs_ref, inv_ref, base_ref, *edge_refs):
+def local_kernel(tiles, *refs):
+    lam_ref, couple_ref, jac_ref, rhs_ref, inv_ref = refs[:5]
     nv, na = lam_ref.shape[:2]
     sub, lane = iotas()
-    gathers = {}
+    if tiles:
+        placed_ref, *tile_refs, base_ref, sum_ref = refs[5:]
+        me = lax.axis_index("circ")
+        sources = [(ref, 0, donor_at(me - 2 * n)) for n, ref in enumerate(tile_refs)]
+    else:
+        base_ref = refs[5]
     for a in range(na):
         coef = [
             inner_coefs([couple_ref[i, a, half_rows(h), :] for i in range(12)], h, sub, lane) for h in range(2)
@@ -297,23 +311,13 @@
             inv = inv_ref[a, half_rows(half), :]
             for s in range(nv):
                 acc = rhs_ref[s, a, half_rows(half), :]
+                if tiles:
+                    if a < 2:
+                        acc = add_tiles(acc, sources, placed_ref, s, a, half, nv)
+                    sum_ref[s, a, half_rows(half), :] = acc
                 for b in range(nv):
-                    m = jac_ref[s, b, a, half_rows(half), :]
-                    acc = acc + m * near[b][half]
-                    if prepare:
-                        m = m * inv
-                        gather = gathers.setdefault((s, b), Gather(sub, lane))
-                        gather.cols("cols", half, a, m)
-                        gather.rows("high" if half else "low", half, a, m)
+                    acc = acc + jac_ref[s, b, a, half_rows(half), :] * near[b][half]
                 base_ref[s, a, half_rows(half), :] = acc * inv
-    if prepare:
-        cols_ref, low_ref, high_ref = edge_refs
-        for (s, b), gather in gathers.items():
-            for half in range(2):
-                cols_ref[s, b, half_rows(half), :] = gather.got["cols", half]
-            for q in range(na // 4):
-                low_ref[s, b, half_rows(q), :] = gather.got["low", q]
-                high_ref[s, b, half_rows(q), :] = gather.got["high", q]
 
 
 def relay_kernel(first, cols_ref, tile_ref, _, out_ref, *, share):
@@ -364,49 +368,24 @@
     return x + jnp.where(sub >= SUB - 2, down(high[a // 4], SUB - 2 - 2 * j), 0.0)
 
 
-def first_finish(routes, *refs):
-    near_ref, jac_ref, src_ref, inv_ref, placed_ref, cols_ref, rows_ref = refs[:7]
-    ahead_ref, back_ref, across_ref, *relayed = refs[7 : 10 + routes]
-    direct = refs[10 + routes : 10 + 2 * routes]
-    out_ref, rhs_ref, ahead_to, back_to, across_to, mate_to = refs[10 + 2 * routes :]
-    nv, na = near_ref.shape[:2]
-    sub, lane = iotas()
-    share = shares(routes)
-    mate_at = lambda half: relayed[SUB * half // share][SUB * half % share : SUB * half % share + SUB, :]
-    parts = halo_sums(nv, na, ahead_ref, back_ref, across_ref, mate_at, cols_ref, rows_ref)
-    me = lax.axis_index("circ")
-    sources = [(ref, 0, donor_at(me - 2 * n)) for n, ref in enumerate(direct)]
-    sources += [(ref, share, donor_at(me + 1 - 2 * (me % 2) - 2 * n)) for n, ref in enumerate(relayed)]
-    packer = Packer(na, nv)
-    for a in range(na):
-        for half in range(2):
-            rows = half_rows(half)
-            near = [spread(near_ref[v, a, rows, :], parts[v], a, half, sub, lane) for v in range(nv)]
-            inv = inv_ref[a, rows, :]
-            for s in range(nv):
-                acc = src_ref[s, a, rows, :]
-                if a < 2:
-                    acc = add_tiles(acc, sources, placed_ref, s, a, half, nv)
-                rhs_ref[s, a, rows, :] = acc
-                for b in range(nv):
-                    acc = acc + jac_ref[s, b, a, rows, :] * near[b]
-                x = acc * inv
-                out_ref[s, a, rows, :] = x
-                packer.add(s, a, half, x)
-    packer.write(ahead_to, back_to, across_to, [mate_to.at[:SUB], mate_to.at[SUB:]])
-
-
-def finish_kernel(last, *refs):
-    base_ref, cols_ref, rows_ref, edge_cols, edge_low, edge_high = refs[:6]
-    ahead_ref, back_ref, across_ref, mate_ref, out_ref, *rest = refs[6:]
+def finish_kernel(routes, last, *refs):
+    base_ref, cols_ref, rows_ref, edge_cols, edge_low, edge_high, ahead_ref, back_ref, across_ref = refs[:9]
     nv, na = base_ref.shape[:2]
     sub, lane = iotas()
+    if routes:
+        rhs_ref, inv_ref, placed_ref, *relayed = refs[9 : 12 + routes]
+        out_ref, sum_ref, *rest = refs[12 + routes :]
+        share = shares(routes)
+        mate_at = lambda half: relayed[SUB * half // share][SUB * half % share : SUB * half % share + SUB, :]
+        me = lax.axis_index("circ")
+        sources = [(ref, share, donor_at(me + 1 - 2 * (me % 2) - 2 * n)) for n, ref in enumerate(relayed)]
+    else:
+        mate_ref, out_ref, *rest = refs[9:]
+        mate_at = lambda half: mate_ref[half_rows(half), :]
     if last:
         result_ref, out_ref, sems = out_ref, *rest
         copies = []
-    sums = halo_sums(
-        nv, na, ahead_ref, back_ref, across_ref, lambda half: mate_ref[half_rows(half), :], cols_ref, rows_ref
-    )
+    sums = halo_sums(nv, na, ahead_ref, back_ref, across_ref, mate_at, cols_ref, rows_ref)
     parts = []
     for s in range(nv):
         turned = []
@@ -423,6 +402,13 @@
         for half in range(2):
             for s in range(nv):
                 x = spread(base_ref[s, a, half_rows(half), :], parts[s], a, half, sub, lane)
+                if routes:
+                    total = rhs_ref[s, a, half_rows(half), :]
+                    if a < 2:
+                        more = add_tiles(jnp.zeros_like(x), sources, placed_ref, s, a, half, nv)
+                        total = total + more
+                        x = x + more * inv_ref[a, half_rows(half), :]
+                    sum_ref[s, a, half_rows(half), :] = total
                 out_ref[s, a, half_rows(half), :] = x
                 if packer is not None:
                     packer.add(s, a, half, x)
@@ -487,10 +473,10 @@
             across = sent(cross, route["across"])
             if sweep == 0:
                 share = shares(count)
-                jac, placed, inv, edge_coefs, row_coefs = call(
+                jac, placed, inv, edge_coefs, row_coefs, *matrices = call(
                     fetch_kernel, "fetch",
                     [vmem(nv, nv, na, nr, nc), vmem(donors, slots, nr, nc), vmem(na, nr, nc),
-                     vmem(2, nr, nc), vmem(4, 2 * na, nc)],
+                     vmem(2, nr, nc), vmem(4, 2 * na, nc), vmem(nv, nv, nr, nc)] + [vmem(nv, nv, 2 * na, nc)] * 2,
                     [cpl, *map(far, (jacobian[0], target_row[0], tile_count[0], weights.reshape(-1, nc)))],
                     [inside] + [outside] * 4,
                     [pltpu.SMEM(target_row.shape[1:], jnp.int32), pltpu.SMEM(tile_count.shape[1:], jnp.int32),
@@ -502,28 +488,24 @@
                     for n, x in enumerate(tiles)
                 ]
                 relayed = [sent(x, route["mate"]) for x in relayed]
-                near, = call(work_kernel, "work", [block], [lam, cpl])
+                base, rhs = call(
+                    functools.partial(local_kernel, True), "local0", [block] * 2, [lam, cpl, jac, rhs, inv, placed, *tiles]
+                )
                 lam, rhs, ahead, back, cross, cols = call(
-                    functools.partial(first_finish, count), "finish0", [block] * 2 + edges(nr + SUB),
-                    [near, jac, rhs, inv, placed, edge_coefs, row_coefs, ahead, back, across,
-                     *relayed, *tiles],
+                    functools.partial(finish_kernel, count, False), "finish0", [block] * 2 + edges(nr + SUB),
+                    [base, edge_coefs, row_coefs, *matrices, ahead, back, across, rhs, inv, placed, *relayed],
                 )
                 continue
             mate = sent(cols, route["mate"])
-            prepare = sweep == 1
-            base, *more = call(
-                functools.partial(local_kernel, prepare), f"local{sweep}",
-                [block] + ([vmem(nv, nv, nr, nc)] + [vmem(nv, nv, 2 * na, nc)] * 2 if prepare else []),
-                [lam, cpl, jac, rhs, inv],
-            )
-            if prepare:
-                matrices = more
+            base = call(
+                functools.partial(local_kernel, False), f"local{sweep}", [block], [lam, cpl, jac, rhs, inv]
+            )[0]
             scratch, spaces, outs = [], None, [block] + edges(nr + SUB)
             if last:
                 outs, spaces = [jax.ShapeDtypeStruct((nv, na, nr, nc), jnp.float32)], [outside]
                 scratch = [pltpu.VMEM((nv, na, nr, nc), jnp.float32), pltpu.SemaphoreType.DMA((na,))]
             lam, *more = call(
-                functools.partial(finish_kernel, last), f"finish{sweep}", outs,
+                functools.partial(finish_kernel, 0, last), f"finish{sweep}", outs,
                 [base, edge_coefs, row_coefs, *matrices, ahead, back, across, mate], None, scratch, 1, spaces,
             )
             if not last:

time: 24.5 us -> 24.3 us (level)
  transfers between devices with their start and end apart: 15 -> 15, of which waited for: 7 -> 5; matrix products, arithmetic and copies ran while one was open for 0% -> 0% of each run, Pallas kernels for 14% -> 15%
where the time goes in v6:
time: 24.3 us; the launch traced here: 24 us
  starting transfers between devices  14.6 us (60%)
  Pallas kernels  6.96 us (29%)
  waiting for transfers between devices  2.4 us (10%)
    ppermute x15, starting transfers between devices, sent(): return lax.ppermute(x, AXES, pairs)  14.6 us
    pallas_call x11, Pallas kernels, call(): pl.pallas_call(kernel, out_shape=outs, in_specs=[vmem] * len(args) if spe...  6.96 us
    ppermute x15, waiting for transfers between devices, sent(): return lax.ppermute(x, AXES, pairs)  2.4 us
  transfers between devices with their start and end apart: 15, of which 5 were waited for; matrix products, arithmetic and copies ran while one was open for 0% of the time, Pallas kernels for 15%

profile of v6, /device:TPU:0, one launch (start us, length us, event | category | flops | bytes accessed | tf_op | source)
XLA Modules:
  0.0 24.0 jit_solution(3296162084266142294)
XLA Ops:
  0.0 1.3 %load.1 = (f32[5,8,16,128]{3,2,1,0:T(8,128)S(1)}, f32[12,8,16,128]{3,2,1,0:T(8,128)S(1)}, f32[5,8,16,128]{3,2,1,0:T(8,128)S(1)}, f32[120,128]{1,0:T(8,128)S(1)}, f32[128,128]{1,0:T(8,128)S(1)}) custom-call(f32[5,8,16,128]{3,2,1,0:T(8,128)} %bitcast.11, s32[4,4,6]{2,1,0:T(4,128)} %bitcast.14, f32[12,8,16,128]{3,2,1,0:T(8,128)} %bitcast.10, ...), custom_call_target="tpu_custom_call" | custom-call | flops 1000000 | bytes 3000000 | tf_op jit(solution)/shard_map/load/pallas_call | solution.py:429
  1.4 4.0 %collective-permute-start.1 = (f32[128,128]{1,0:T(8,128)S(1)}, f32[128,128]{1,0:T(8,128)S(1)}, u32[]{:S(2)}, u32[]{:S(2)}) collective-permute-start(f32[128,128]{1,0:T(8,128)S(1)} %get-tuple-element.42), channel_id=1, source_target_pairs={{0,24},{1,25},{2,26},{3,27},{4,28},{5,29},{6,30},{7,31},{8,16},{9,... | collective-permute-start | bytes 196616 | tf_op jit(solution)/shard_map/ppermute | solution.py:452
  5.3 0.5 %collective-permute-start = (f32[120,128]{1,0:T(8,128)S(1)}, f32[120,128]{1,0:T(8,128)S(1)}, u32[]{:S(2)}, u32[]{:S(2)}) collective-permute-start(f32[120,128]{1,0:T(8,128)S(1)} %get-tuple-element.41), channel_id=1, source_target_pairs={{0,16},{1,17},{2,18},{3,19},{4,20},{5,21},{6,22},{7,23},{8,24},{9,... | collective-permute-start | bytes 184328 | tf_op jit(solution)/shard_map/ppermute | solution.py:452
  5.8 0.1 pack.1
  6.0 1.6 %collective-permute-start.2 = (f32[88,128]{1,0:T(8,128)S(1)}, f32[88,128]{1,0:T(8,128)S(1)}, u32[]{:S(2)}, u32[]{:S(2)}) collective-permute-start(f32[88,128]{1,0:T(8,128)S(1)} %get-tuple-element.49), channel_id=1, source_target_pairs={{0,1},{1,0},{2,3},{3,2},{4,5},{5,4},{6,7},{7,6},{8,9},{9,8},{10,11... | collective-permute-start | bytes 135176 | tf_op jit(solution)/shard_map/ppermute | solution.py:452
  7.6 0.0 collective-permute-start.3
  7.6 0.6 %collective-permute-start.4 = (f32[72,128]{1,0:T(8,128)S(1)}, f32[72,128]{1,0:T(8,128)S(1)}, u32[]{:S(2)}, u32[]{:S(2)}) collective-permute-start(f32[72,128]{1,0:T(8,128)S(1)} %get-tuple-element.51), channel_id=1, source_target_pairs={{0,12},{1,13},{2,14},{3,15},{4,8},{5,9},{6,10},{7,11},{8,4},{9,5},... | collective-permute-start | bytes 110600 | tf_op jit(solution)/shard_map/ppermute | solution.py:452
  8.3 1.8 %fetch.1 = (f32[5,5,8,16,128]{4,3,2,1,0:T(8,128)S(1)}, f32[4,6,16,128]{3,2,1,0:T(8,128)S(1)}, f32[8,16,128]{2,1,0:T(8,128)S(1)}, f32[2,16,128]{2,1,0:T(8,128)S(1...) custom-call(f32[12,8,16,128]{3,2,1,0:T(8,128)S(1)} %get-tuple-elemen, ...), custom_call_target="tpu_custom_call" | custom-call | flops 1000000 | bytes 3000000 | tf_op jit(solution)/shard_map/fetch/pallas_call | solution.py:429
  10.1 0.0 collective-permute-done.refs_6_.tile_ref
  10.1 0.1 collective-permute-start.5
  10.2 0.0 collective-permute-done.1.refs_7_.tile_ref
  10.2 0.5 %collective-permute-start.6 = (f32[68,128]{1,0:T(8,128)S(1)}, f32[68,128]{1,0:T(8,128)S(1)}, u32[]{:S(2)}, u32[]{:S(2)}) collective-permute-start(f32[68,128]{1,0:T(8,128)S(1)} %relay1.1), channel_id=1, source_target_pairs={{0,4},{1,5},{2,6},{3,7},{4,0},{5,1},{6,2},{7,3},{8,12},{9,13},{10,... | collective-permute-start | bytes 104456 | tf_op jit(solution)/shard_map/ppermute | solution.py:452
  10.7 0.6 %local0.1 = (f32[5,8,16,128]{3,2,1,0:T(8,128)S(1)}, f32[5,8,16,128]{3,2,1,0:T(8,128)S(1)}) custom-call(f32[5,8,16,128]{3,2,1,0:T(8,128)S(1)} %get-tuple-element.35.refs_0_.lam_ref, f32[12,8,16,128]{3,2,1,0:T(8,128)S(1)} %get-tuple-element.36.couple_ref.refs_1_, f32[5,5,8,16,128]{4,3,2,1,0:T(8,128)S(1)} %get-tuple-element.37.refs_2_, ...), custom_call_target="tpu_custom_call" | custom-call | flops 1000000 | bytes 3000000 | tf_op jit(solution)/shard_map/local0/pallas_call | solution.py:429
  11.3 0.0 collective-permute-done.4.refs_8_
  11.4 0.0 collective-permute-done.3.refs_7_
  11.4 0.0 collective-permute-done.2.refs_6_
  11.4 0.0 collective-permute-done.5.refs_12_
  11.4 0.2 collective-permute-done.6.refs_13_
  11.6 0.5 %finish0.1 = (f32[5,8,16,128]{3,2,1,0:T(8,128)S(1)}, f32[5,8,16,128]{3,2,1,0:T(8,128)S(1)}, f32[88,128]{1,0:T(8,128)S(1)}, f32[80,128]{1,0:T(8,128)S(1)}, f32[24,128]{1,0:T(8,128)S(1)}, /*index=5*/f32[16,128]{1,0:T(8,128)S(1)}) custom-call(f32[5,8,16,128]{3,2,1,0:T(8,128)S(1)} %get-tuple-element.43.refs_0_, f32[2,16,128]{2,1,0:T(8,128)S(1)} %get-tuple-element.44.refs_1_, ...), custom_call_target="tpu_custom_call" | custom-call | flops 1000000 | bytes 3000000 | tf_op jit(solution)/shard_map/finish0/pallas_call | solution.py:429
  12.1 3.0 %collective-permute-start.7 = (f32[88,128]{1,0:T(8,128)S(1)}, f32[88,128]{1,0:T(8,128)S(1)}, u32[]{:S(2)}, u32[]{:S(2)}) collective-permute-start(f32[88,128]{1,0:T(8,128)S(1)} %get-tuple-element.56), channel_id=1, source_target_pairs={{0,1},{1,0},{2,3},{3,2},{4,5},{5,4},{6,7},{7,6},{8,9},{9,8},{10,11... | collective-permute-start | bytes 135176 | tf_op jit(solution)/shard_map/ppermute | solution.py:452
  15.1 0.0 collective-permute-start.8
  15.2 1.6 %collective-permute-start.9 = (f32[24,128]{1,0:T(8,128)S(1)}, f32[24,128]{1,0:T(8,128)S(1)}, u32[]{:S(2)}, u32[]{:S(2)}) collective-permute-start(f32[24,128]{1,0:T(8,128)S(1)} %get-tuple-element.58), channel_id=1, source_target_pairs={{0,12},{1,13},{2,14},{3,15},{4,8},{5,9},{6,10},{7,11},{8,4},{9,5},... | collective-permute-start | bytes 36872 | tf_op jit(solution)/shard_map/ppermute | solution.py:452
  16.8 0.0 collective-permute-start.10
  16.8 0.5 %local1.1.refs_0_ = f32[5,8,16,128]{3,2,1,0:T(8,128)S(1)} custom-call(f32[5,8,16,128]{3,2,1,0:T(8,128)S(1)} %get-tuple-element.54.refs_0_, f32[12,8,16,128]{3,2,1,0:T(8,128)S(1)} %get-tuple-element.36.couple_ref.refs_1_, f32[5,5,8,16,128]{4,3,2,1,0:T(8,128)S(1)} %get-tuple-element.37.refs_2_, f32[5,8,16,128]{3,2,1,0:T(8,128)S(1)} %get-tuple-element.55.refs_3_, ...), custom_call_target="tpu_custom_call" | custom-call | flops 1000000 | bytes 3000000 | tf_op jit(solution)/shard_map/local1/pallas_call | solution.py:429
  17.3 0.6 %collective-permute-done.10.refs_9_ = f32[16,128]{1,0:T(8,128)S(1)} collective-permute-done((f32[16,128]{1,0:T(8,128)S(1)}, f32[16,128]{1,0:T(8,128)S(1)}, u32[]{:S(2)}, u32[]{:S(2)}) %collective-permute-start.10) | collective-permute-done | bytes 8224 | tf_op jit(solution)/shard_map/ppermute | solution.py:452
  17.9 0.3 %collective-permute-done.9.refs_8_ = f32[24,128]{1,0:T(8,128)S(1)} collective-permute-done((f32[24,128]{1,0:T(8,128)S(1)}, f32[24,128]{1,0:T(8,128)S(1)}, u32[]{:S(2)}, u32[]{:S(2)}) %collective-permute-start.9) | collective-permute-done | bytes 12320 | tf_op jit(solution)/shard_map/ppermute | solution.py:452
  18.3 0.0 collective-permute-done.8.refs_7_
  18.3 0.0 collective-permute-done.7.refs_6_
  18.3 0.4 %finish1.1 = (f32[5,8,16,128]{3,2,1,0:T(8,128)S(1)}, f32[88,128]{1,0:T(8,128)S(1)}, f32[80,128]{1,0:T(8,128)S(1)}, f32[24,128]{1,0:T(8,128)S(1)}, f32[16,128]{1,0:T(8,128)S(1)}) custom-call(f32[5,8,16,128]{3,2,1,0:T(8,128)S(1)} %local1.1.refs_0_, f32[2,16,128]{2,1,0:T(8,128)S(1)} %get-tuple-element.44.refs_1_, f32[4,16,128]{2,1,0:T(8,128)S(1)} %get-tuple-element.45.refs_2_, ...), custom_call_target="tpu_custom_call" | custom-call | flops 1000000 | bytes 3000000 | tf_op jit(solution)/shard_map/finish1/pallas_call | solution.py:429
  18.7 1.2 %collective-permute-start.11 = (f32[88,128]{1,0:T(8,128)S(1)}, f32[88,128]{1,0:T(8,128)S(1)}, u32[]{:S(2)}, u32[]{:S(2)}) collective-permute-start(f32[88,128]{1,0:T(8,128)S(1)} %get-tuple-element.61), channel_id=1, source_target_pairs={{0,1},{1,0},{2,3},{3,2},{4,5},{5,4},{6,7},{7,6},{8,9},{9,8},{10,11... | collective-permute-start | bytes 135176 | tf_op jit(solution)/shard_map/ppermute | solution.py:452
  19.9 0.0 collective-permute-start.12
  19.9 1.4 %collective-permute-start.13 = (f32[24,128]{1,0:T(8,128)S(1)}, f32[24,128]{1,0:T(8,128)S(1)}, u32[]{:S(2)}, u32[]{:S(2)}) collective-permute-start(f32[24,128]{1,0:T(8,128)S(1)} %get-tuple-element.63), channel_id=1, source_target_pairs={{0,12},{1,13},{2,14},{3,15},{4,8},{5,9},{6,10},{7,11},{8,4},{9,5},... | collective-permute-start | bytes 36872 | tf_op jit(solution)/shard_map/ppermute | solution.py:452
  21.3 0.0 collective-permute-start.14
  21.3 0.5 %local2.1.refs_0_ = f32[5,8,16,128]{3,2,1,0:T(8,128)S(1)} custom-call(f32[5,8,16,128]{3,2,1,0:T(8,128)S(1)} %get-tuple-element.60.refs_0_, f32[12,8,16,128]{3,2,1,0:T(8,128)S(1)} %get-tuple-element.36.couple_ref.refs_1_, f32[5,5,8,16,128]{4,3,2,1,0:T(8,128)S(1)} %get-tuple-element.37.refs_2_, f32[5,8,16,128]{3,2,1,0:T(8,128)S(1)} %get-tuple-element.55.refs_3_, ...), custom_call_target="tpu_custom_call" | custom-call | flops 1000000 | bytes 3000000 | tf_op jit(solution)/shard_map/local2/pallas_call | solution.py:429
  21.8 0.6 %collective-permute-done.14.refs_9_ = f32[16,128]{1,0:T(8,128)S(1)} collective-permute-done((f32[16,128]{1,0:T(8,128)S(1)}, f32[16,128]{1,0:T(8,128)S(1)}, u32[]{:S(2)}, u32[]{:S(2)}) %collective-permute-start.14) | collective-permute-done | bytes 8224 | tf_op jit(solution)/shard_map/ppermute | solution.py:452
  22.5 0.6 %collective-permute-done.13.refs_8_ = f32[24,128]{1,0:T(8,128)S(1)} collective-permute-done((f32[24,128]{1,0:T(8,128)S(1)}, f32[24,128]{1,0:T(8,128)S(1)}, u32[]{:S(2)}, u32[]{:S(2)}) %collective-permute-start.13) | collective-permute-done | bytes 12320 | tf_op jit(solution)/shard_map/ppermute | solution.py:452
  23.0 0.0 collective-permute-done.12.refs_7_
  23.0 0.0 collective-permute-done.11.refs_6_
  23.0 1.0 %finish2.1 = f32[5,8,16,128]{3,2,1,0:T(8,128)} custom-call(f32[5,8,16,128]{3,2,1,0:T(8,128)S(1)} %local2.1.refs_0_, f32[2,16,128]{2,1,0:T(8,128)S(1)} %get-tuple-element.44.refs_1_, f32[4,16,128]{2,1,0:T(8,128)S(1)} %get-tuple-element.45.refs_2_, f32[5,5,16,128]{3,2,1,0:T(8,128)S(1)} %get-tuple-element.46.refs_3_, ...), custom_call_target="tpu_custom_call" | custom-call | flops 1000000 | bytes 3000000 | tf_op jit(solution)/shard_map/finish2/pallas_call | solution.py:429
  (2 shorter events, 0.0 us)
Async XLA Ops:
  1.4 8.9 %collective-permute-start.1 = (f32[128,128]{1,0:T(8,128)S(1)}, f32[128,128]{1,0:T(8,128)S(1)}, u32[]{:S(2)}, u32[]{:S(2)}) collective-permute-start(f32[128,128]{1,0:T(8,128)S(1)} %get-tuple-element.42), channel_id=1, source_target_pairs={{0,24},{1,25},{2,26},{3,27},{4,28},{5,29},{6,30},{7,31},{8,16},{9,... | collective-permute-start | bytes 196616 | tf_op jit(solution)/shard_map/ppermute | solution.py:452
  5.3 4.8 %collective-permute-start = (f32[120,128]{1,0:T(8,128)S(1)}, f32[120,128]{1,0:T(8,128)S(1)}, u32[]{:S(2)}, u32[]{:S(2)}) collective-permute-start(f32[120,128]{1,0:T(8,128)S(1)} %get-tuple-element.41), channel_id=1, source_target_pairs={{0,16},{1,17},{2,18},{3,19},{4,20},{5,21},{6,22},{7,23},{8,24},{9,... | collective-permute-start | bytes 184328 | tf_op jit(solution)/shard_map/ppermute | solution.py:452
  6.0 5.4 %collective-permute-start.2 = (f32[88,128]{1,0:T(8,128)S(1)}, f32[88,128]{1,0:T(8,128)S(1)}, u32[]{:S(2)}, u32[]{:S(2)}) collective-permute-start(f32[88,128]{1,0:T(8,128)S(1)} %get-tuple-element.49), channel_id=1, source_target_pairs={{0,1},{1,0},{2,3},{3,2},{4,5},{5,4},{6,7},{7,6},{8,9},{9,8},{10,11... | collective-permute-start | bytes 135176 | tf_op jit(solution)/shard_map/ppermute | solution.py:452
  7.6 3.7 %collective-permute-start.3 = (f32[80,128]{1,0:T(8,128)S(1)}, f32[80,128]{1,0:T(8,128)S(1)}, u32[]{:S(2)}, u32[]{:S(2)}) collective-permute-start(f32[80,128]{1,0:T(8,128)S(1)} %get-tuple-element.50), channel_id=1, source_target_pairs={{0,4},{1,2},{2,1},{3,7},{4,0},{5,6},{6,5},{7,3},{8,12},{9,10},{10,... | collective-permute-start | bytes 122888 | tf_op jit(solution)/shard_map/ppermute | solution.py:452
  7.6 3.7 %collective-permute-start.4 = (f32[72,128]{1,0:T(8,128)S(1)}, f32[72,128]{1,0:T(8,128)S(1)}, u32[]{:S(2)}, u32[]{:S(2)}) collective-permute-start(f32[72,128]{1,0:T(8,128)S(1)} %get-tuple-element.51), channel_id=1, source_target_pairs={{0,12},{1,13},{2,14},{3,15},{4,8},{5,9},{6,10},{7,11},{8,4},{9,5},... | collective-permute-start | bytes 110600 | tf_op jit(solution)/shard_map/ppermute | solution.py:452
  10.1 1.3 %collective-permute-start.5 = (f32[68,128]{1,0:T(8,128)S(1)}, f32[68,128]{1,0:T(8,128)S(1)}, u32[]{:S(2)}, u32[]{:S(2)}) collective-permute-start(f32[68,128]{1,0:T(8,128)S(1)} %relay0.1), channel_id=1, source_target_pairs={{0,4},{1,5},{2,6},{3,7},{4,0},{5,1},{6,2},{7,3},{8,12},{9,13},{10,... | collective-permute-start | bytes 104456 | tf_op jit(solution)/shard_map/ppermute | solution.py:452
  10.2 1.3 %collective-permute-start.6 = (f32[68,128]{1,0:T(8,128)S(1)}, f32[68,128]{1,0:T(8,128)S(1)}, u32[]{:S(2)}, u32[]{:S(2)}) collective-permute-start(f32[68,128]{1,0:T(8,128)S(1)} %relay1.1), channel_id=1, source_target_pairs={{0,4},{1,5},{2,6},{3,7},{4,0},{5,1},{6,2},{7,3},{8,12},{9,13},{10,... | collective-permute-start | bytes 104456 | tf_op jit(solution)/shard_map/ppermute | solution.py:452
  12.1 6.2 %collective-permute-start.7 = (f32[88,128]{1,0:T(8,128)S(1)}, f32[88,128]{1,0:T(8,128)S(1)}, u32[]{:S(2)}, u32[]{:S(2)}) collective-permute-start(f32[88,128]{1,0:T(8,128)S(1)} %get-tuple-element.56), channel_id=1, source_target_pairs={{0,1},{1,0},{2,3},{3,2},{4,5},{5,4},{6,7},{7,6},{8,9},{9,8},{10,11... | collective-permute-start | bytes 135176 | tf_op jit(solution)/shard_map/ppermute | solution.py:452
  15.1 3.1 %collective-permute-start.8 = (f32[80,128]{1,0:T(8,128)S(1)}, f32[80,128]{1,0:T(8,128)S(1)}, u32[]{:S(2)}, u32[]{:S(2)}) collective-permute-start(f32[80,128]{1,0:T(8,128)S(1)} %get-tuple-element.57), channel_id=1, source_target_pairs={{0,4},{1,2},{2,1},{3,7},{4,0},{5,6},{6,5},{7,3},{8,12},{9,10},{10,... | collective-permute-start | bytes 122888 | tf_op jit(solution)/shard_map/ppermute | solution.py:452
  15.2 3.1 %collective-permute-start.9 = (f32[24,128]{1,0:T(8,128)S(1)}, f32[24,128]{1,0:T(8,128)S(1)}, u32[]{:S(2)}, u32[]{:S(2)}) collective-permute-start(f32[24,128]{1,0:T(8,128)S(1)} %get-tuple-element.58), channel_id=1, source_target_pairs={{0,12},{1,13},{2,14},{3,15},{4,8},{5,9},{6,10},{7,11},{8,4},{9,5},... | collective-permute-start | bytes 36872 | tf_op jit(solution)/shard_map/ppermute | solution.py:452
  16.8 1.2 %collective-permute-start.10 = (f32[16,128]{1,0:T(8,128)S(1)}, f32[16,128]{1,0:T(8,128)S(1)}, u32[]{:S(2)}, u32[]{:S(2)}) collective-permute-start(f32[16,128]{1,0:T(8,128)S(1)} %get-tuple-element.59), channel_id=1, source_target_pairs={{0,4},{1,5},{2,6},{3,7},{4,0},{5,1},{6,2},{7,3},{8,12},{9,13},{10,... | collective-permute-start | bytes 24584 | tf_op jit(solution)/shard_map/ppermute | solution.py:452
  18.7 4.3 %collective-permute-start.11 = (f32[88,128]{1,0:T(8,128)S(1)}, f32[88,128]{1,0:T(8,128)S(1)}, u32[]{:S(2)}, u32[]{:S(2)}) collective-permute-start(f32[88,128]{1,0:T(8,128)S(1)} %get-tuple-element.61), channel_id=1, source_target_pairs={{0,1},{1,0},{2,3},{3,2},{4,5},{5,4},{6,7},{7,6},{8,9},{9,8},{10,11... | collective-permute-start | bytes 135176 | tf_op jit(solution)/shard_map/ppermute | solution.py:452
  19.9 3.1 %collective-permute-start.12 = (f32[80,128]{1,0:T(8,128)S(1)}, f32[80,128]{1,0:T(8,128)S(1)}, u32[]{:S(2)}, u32[]{:S(2)}) collective-permute-start(f32[80,128]{1,0:T(8,128)S(1)} %get-tuple-element.62), channel_id=1, source_target_pairs={{0,4},{1,2},{2,1},{3,7},{4,0},{5,6},{6,5},{7,3},{8,12},{9,10},{10,... | collective-permute-start | bytes 122888 | tf_op jit(solution)/shard_map/ppermute | solution.py:452
  19.9 3.1 %collective-permute-start.13 = (f32[24,128]{1,0:T(8,128)S(1)}, f32[24,128]{1,0:T(8,128)S(1)}, u32[]{:S(2)}, u32[]{:S(2)}) collective-permute-start(f32[24,128]{1,0:T(8,128)S(1)} %get-tuple-element.63), channel_id=1, source_target_pairs={{0,12},{1,13},{2,14},{3,15},{4,8},{5,9},{6,10},{7,11},{8,4},{9,5},... | collective-permute-start | bytes 36872 | tf_op jit(solution)/shard_map/ppermute | solution.py:452
  21.3 1.2 %collective-permute-start.14 = (f32[16,128]{1,0:T(8,128)S(1)}, f32[16,128]{1,0:T(8,128)S(1)}, u32[]{:S(2)}, u32[]{:S(2)}) collective-permute-start(f32[16,128]{1,0:T(8,128)S(1)} %get-tuple-element.64), channel_id=1, source_target_pairs={{0,4},{1,5},{2,6},{3,7},{4,0},{5,1},{6,2},{7,3},{8,12},{9,13},{10,... | collective-permute-start | bytes 24584 | tf_op jit(solution)/shard_map/ppermute | solution.py:452

commit v7 on v6

--- a/solution.py
+++ b/solution.py
@@ -386,7 +386,7 @@
         result_ref, out_ref, sems = out_ref, *rest
         copies = []
     sums = halo_sums(nv, na, ahead_ref, back_ref, across_ref, mate_at, cols_ref, rows_ref)
-    parts = []
+    packer = None if last else Packer(na, nv)
     for s in range(nv):
         turned = []
         for kind, edge_ref in enumerate((edge_cols, edge_low, edge_high)):
@@ -396,12 +396,9 @@
                 for b in range(1, nv):
                     total = total + edge_ref[s, b, half_rows(q), :] * sums[b][kind][q]
                 turned[-1].append(total)
-        parts.append(turned)
-    packer = None if last else Packer(na, nv)
-    for a in range(na):
-        for half in range(2):
-            for s in range(nv):
-                x = spread(base_ref[s, a, half_rows(half), :], parts[s], a, half, sub, lane)
+        for a in range(na):
+            for half in range(2):
+                x = spread(base_ref[s, a, half_rows(half), :], turned, a, half, sub, lane)
                 if routes:
                     total = rhs_ref[s, a, half_rows(half), :]
                     if a < 2:
@@ -413,7 +410,7 @@
                 if packer is not None:
                     packer.add(s, a, half, x)
         if last:
-            copy = pltpu.make_async_copy(out_ref.at[:, a], result_ref.at[:, a], sems.at[a])
+            copy = pltpu.make_async_copy(out_ref.at[s], result_ref.at[s], sems.at[s])
             copy.start()
             copies.append(copy)
     if last:
@@ -503,7 +500,7 @@
             scratch, spaces, outs = [], None, [block] + edges(nr + SUB)
             if last:
                 outs, spaces = [jax.ShapeDtypeStruct((nv, na, nr, nc), jnp.float32)], [outside]
-                scratch = [pltpu.VMEM((nv, na, nr, nc), jnp.float32), pltpu.SemaphoreType.DMA((na,))]
+                scratch = [pltpu.VMEM((nv, na, nr, nc), jnp.float32), pltpu.SemaphoreType.DMA((nv,))]
             lam, *more = call(
                 functools.partial(finish_kernel, 0, last), f"finish{sweep}", outs,
                 [base, edge_coefs, row_coefs, *matrices, ahead, back, across, mate], None, scratch, 1, spaces,

time: 24.3 us -> 24.3 us (level)
  no operation moved by 1% of the time
where the time goes in v7:
time: 24.3 us; the launch traced here: 24 us
  starting transfers between devices  14.6 us (60%)
  Pallas kernels  6.91 us (28%)
  waiting for transfers between devices  2.4 us (10%)
    ppermute x15, starting transfers between devices, sent(): return lax.ppermute(x, AXES, pairs)  14.6 us
    pallas_call x11, Pallas kernels, call(): pl.pallas_call(kernel, out_shape=outs, in_specs=[vmem] * len(args) if spe...  6.91 us
    ppermute x15, waiting for transfers between devices, sent(): return lax.ppermute(x, AXES, pairs)  2.4 us
  transfers between devices with their start and end apart: 15, of which 5 were waited for; matrix products, arithmetic and copies ran while one was open for 0% of the time, Pallas kernels for 15%

profile of v7, /device:TPU:0, one launch (start us, length us, event | category | flops | bytes accessed | tf_op | source)
XLA Modules:
  0.0 24.0 jit_solution(6767154256024599019)
XLA Ops:
  0.0 1.3 %load.1 = (f32[5,8,16,128]{3,2,1,0:T(8,128)S(1)}, f32[12,8,16,128]{3,2,1,0:T(8,128)S(1)}, f32[5,8,16,128]{3,2,1,0:T(8,128)S(1)}, f32[120,128]{1,0:T(8,128)S(1)}, f32[128,128]{1,0:T(8,128)S(1)}) custom-call(f32[5,8,16,128]{3,2,1,0:T(8,128)} %bitcast.11, s32[4,4,6]{2,1,0:T(4,128)} %bitcast.14, f32[12,8,16,128]{3,2,1,0:T(8,128)} %bitcast.10, ...), custom_call_target="tpu_custom_call" | custom-call | flops 1000000 | bytes 3000000 | tf_op jit(solution)/shard_map/load/pallas_call | solution.py:426
  1.4 4.0 %collective-permute-start.1 = (f32[128,128]{1,0:T(8,128)S(1)}, f32[128,128]{1,0:T(8,128)S(1)}, u32[]{:S(2)}, u32[]{:S(2)}) collective-permute-start(f32[128,128]{1,0:T(8,128)S(1)} %get-tuple-element.42), channel_id=1, source_target_pairs={{0,24},{1,25},{2,26},{3,27},{4,28},{5,29},{6,30},{7,31},{8,16},{9,... | collective-permute-start | bytes 196616 | tf_op jit(solution)/shard_map/ppermute | solution.py:449
  5.3 0.5 %collective-permute-start = (f32[120,128]{1,0:T(8,128)S(1)}, f32[120,128]{1,0:T(8,128)S(1)}, u32[]{:S(2)}, u32[]{:S(2)}) collective-permute-start(f32[120,128]{1,0:T(8,128)S(1)} %get-tuple-element.41), channel_id=1, source_target_pairs={{0,16},{1,17},{2,18},{3,19},{4,20},{5,21},{6,22},{7,23},{8,24},{9,... | collective-permute-start | bytes 184328 | tf_op jit(solution)/shard_map/ppermute | solution.py:449
  5.8 0.1 pack.1
  6.0 1.6 %collective-permute-start.2 = (f32[88,128]{1,0:T(8,128)S(1)}, f32[88,128]{1,0:T(8,128)S(1)}, u32[]{:S(2)}, u32[]{:S(2)}) collective-permute-start(f32[88,128]{1,0:T(8,128)S(1)} %get-tuple-element.49), channel_id=1, source_target_pairs={{0,1},{1,0},{2,3},{3,2},{4,5},{5,4},{6,7},{7,6},{8,9},{9,8},{10,11... | collective-permute-start | bytes 135176 | tf_op jit(solution)/shard_map/ppermute | solution.py:449
  7.6 0.0 collective-permute-start.3
  7.6 0.6 %collective-permute-start.4 = (f32[72,128]{1,0:T(8,128)S(1)}, f32[72,128]{1,0:T(8,128)S(1)}, u32[]{:S(2)}, u32[]{:S(2)}) collective-permute-start(f32[72,128]{1,0:T(8,128)S(1)} %get-tuple-element.51), channel_id=1, source_target_pairs={{0,12},{1,13},{2,14},{3,15},{4,8},{5,9},{6,10},{7,11},{8,4},{9,5},... | collective-permute-start | bytes 110600 | tf_op jit(solution)/shard_map/ppermute | solution.py:449
  8.3 1.8 %fetch.1 = (f32[5,5,8,16,128]{4,3,2,1,0:T(8,128)S(1)}, f32[4,6,16,128]{3,2,1,0:T(8,128)S(1)}, f32[8,16,128]{2,1,0:T(8,128)S(1)}, f32[2,16,128]{2,1,0:T(8,128)S(1...) custom-call(f32[12,8,16,128]{3,2,1,0:T(8,128)S(1)} %get-tuple-elemen, ...), custom_call_target="tpu_custom_call" | custom-call | flops 1000000 | bytes 3000000 | tf_op jit(solution)/shard_map/fetch/pallas_call | solution.py:426
  10.1 0.0 collective-permute-done.refs_6_.tile_ref
  10.1 0.1 collective-permute-start.5
  10.2 0.0 collective-permute-done.1.refs_7_.tile_ref
  10.2 0.5 %collective-permute-start.6 = (f32[68,128]{1,0:T(8,128)S(1)}, f32[68,128]{1,0:T(8,128)S(1)}, u32[]{:S(2)}, u32[]{:S(2)}) collective-permute-start(f32[68,128]{1,0:T(8,128)S(1)} %relay1.1), channel_id=1, source_target_pairs={{0,4},{1,5},{2,6},{3,7},{4,0},{5,1},{6,2},{7,3},{8,12},{9,13},{10,... | collective-permute-start | bytes 104456 | tf_op jit(solution)/shard_map/ppermute | solution.py:449
  10.7 0.6 %local0.1 = (f32[5,8,16,128]{3,2,1,0:T(8,128)S(1)}, f32[5,8,16,128]{3,2,1,0:T(8,128)S(1)}) custom-call(f32[5,8,16,128]{3,2,1,0:T(8,128)S(1)} %get-tuple-element.35.refs_0_.lam_ref, f32[12,8,16,128]{3,2,1,0:T(8,128)S(1)} %get-tuple-element.36.couple_ref.refs_1_, f32[5,5,8,16,128]{4,3,2,1,0:T(8,128)S(1)} %get-tuple-element.37.refs_2_, ...), custom_call_target="tpu_custom_call" | custom-call | flops 1000000 | bytes 3000000 | tf_op jit(solution)/shard_map/local0/pallas_call | solution.py:426
  11.3 0.0 collective-permute-done.4.refs_8_
  11.4 0.0 collective-permute-done.3.refs_7_
  11.4 0.0 collective-permute-done.2.refs_6_
  11.4 0.0 collective-permute-done.5.refs_12_
  11.4 0.2 collective-permute-done.6.refs_13_
  11.6 0.5 %finish0.1 = (f32[5,8,16,128]{3,2,1,0:T(8,128)S(1)}, f32[5,8,16,128]{3,2,1,0:T(8,128)S(1)}, f32[88,128]{1,0:T(8,128)S(1)}, f32[80,128]{1,0:T(8,128)S(1)}, f32[24,128]{1,0:T(8,128)S(1)}, /*index=5*/f32[16,128]{1,0:T(8,128)S(1)}) custom-call(f32[5,8,16,128]{3,2,1,0:T(8,128)S(1)} %get-tuple-element.43.refs_0_, f32[2,16,128]{2,1,0:T(8,128)S(1)} %get-tuple-element.44.refs_1_, ...), custom_call_target="tpu_custom_call" | custom-call | flops 1000000 | bytes 3000000 | tf_op jit(solution)/shard_map/finish0/pallas_call | solution.py:426
  12.1 3.0 %collective-permute-start.7 = (f32[88,128]{1,0:T(8,128)S(1)}, f32[88,128]{1,0:T(8,128)S(1)}, u32[]{:S(2)}, u32[]{:S(2)}) collective-permute-start(f32[88,128]{1,0:T(8,128)S(1)} %get-tuple-element.56), channel_id=1, source_target_pairs={{0,1},{1,0},{2,3},{3,2},{4,5},{5,4},{6,7},{7,6},{8,9},{9,8},{10,11... | collective-permute-start | bytes 135176 | tf_op jit(solution)/shard_map/ppermute | solution.py:449
  15.1 0.0 collective-permute-start.8
  15.1 1.6 %collective-permute-start.9 = (f32[24,128]{1,0:T(8,128)S(1)}, f32[24,128]{1,0:T(8,128)S(1)}, u32[]{:S(2)}, u32[]{:S(2)}) collective-permute-start(f32[24,128]{1,0:T(8,128)S(1)} %get-tuple-element.58), channel_id=1, source_target_pairs={{0,12},{1,13},{2,14},{3,15},{4,8},{5,9},{6,10},{7,11},{8,4},{9,5},... | collective-permute-start | bytes 36872 | tf_op jit(solution)/shard_map/ppermute | solution.py:449
  16.7 0.0 collective-permute-start.10
  16.7 0.5 %local1.1.refs_0_ = f32[5,8,16,128]{3,2,1,0:T(8,128)S(1)} custom-call(f32[5,8,16,128]{3,2,1,0:T(8,128)S(1)} %get-tuple-element.54.refs_0_, f32[12,8,16,128]{3,2,1,0:T(8,128)S(1)} %get-tuple-element.36.couple_ref.refs_1_, f32[5,5,8,16,128]{4,3,2,1,0:T(8,128)S(1)} %get-tuple-element.37.refs_2_, f32[5,8,16,128]{3,2,1,0:T(8,128)S(1)} %get-tuple-element.55.refs_3_, ...), custom_call_target="tpu_custom_call" | custom-call | flops 1000000 | bytes 3000000 | tf_op jit(solution)/shard_map/local1/pallas_call | solution.py:426
  17.3 0.6 %collective-permute-done.10.refs_9_ = f32[16,128]{1,0:T(8,128)S(1)} collective-permute-done((f32[16,128]{1,0:T(8,128)S(1)}, f32[16,128]{1,0:T(8,128)S(1)}, u32[]{:S(2)}, u32[]{:S(2)}) %collective-permute-start.10) | collective-permute-done | bytes 8224 | tf_op jit(solution)/shard_map/ppermute | solution.py:449
  17.9 0.3 %collective-permute-done.9.refs_8_ = f32[24,128]{1,0:T(8,128)S(1)} collective-permute-done((f32[24,128]{1,0:T(8,128)S(1)}, f32[24,128]{1,0:T(8,128)S(1)}, u32[]{:S(2)}, u32[]{:S(2)}) %collective-permute-start.9) | collective-permute-done | bytes 12320 | tf_op jit(solution)/shard_map/ppermute | solution.py:449
  18.2 0.0 collective-permute-done.8.refs_7_
  18.3 0.0 collective-permute-done.7.refs_6_
  18.3 0.4 %finish1.1 = (f32[5,8,16,128]{3,2,1,0:T(8,128)S(1)}, f32[88,128]{1,0:T(8,128)S(1)}, f32[80,128]{1,0:T(8,128)S(1)}, f32[24,128]{1,0:T(8,128)S(1)}, f32[16,128]{1,0:T(8,128)S(1)}) custom-call(f32[5,8,16,128]{3,2,1,0:T(8,128)S(1)} %local1.1.refs_0_, f32[2,16,128]{2,1,0:T(8,128)S(1)} %get-tuple-element.44.refs_1_, f32[4,16,128]{2,1,0:T(8,128)S(1)} %get-tuple-element.45.refs_2_, ...), custom_call_target="tpu_custom_call" | custom-call | flops 1000000 | bytes 3000000 | tf_op jit(solution)/shard_map/finish1/pallas_call | solution.py:426
  18.7 1.2 %collective-permute-start.11 = (f32[88,128]{1,0:T(8,128)S(1)}, f32[88,128]{1,0:T(8,128)S(1)}, u32[]{:S(2)}, u32[]{:S(2)}) collective-permute-start(f32[88,128]{1,0:T(8,128)S(1)} %get-tuple-element.61), channel_id=1, source_target_pairs={{0,1},{1,0},{2,3},{3,2},{4,5},{5,4},{6,7},{7,6},{8,9},{9,8},{10,11... | collective-permute-start | bytes 135176 | tf_op jit(solution)/shard_map/ppermute | solution.py:449
  19.9 0.0 collective-permute-start.12
  19.9 1.4 %collective-permute-start.13 = (f32[24,128]{1,0:T(8,128)S(1)}, f32[24,128]{1,0:T(8,128)S(1)}, u32[]{:S(2)}, u32[]{:S(2)}) collective-permute-start(f32[24,128]{1,0:T(8,128)S(1)} %get-tuple-element.63), channel_id=1, source_target_pairs={{0,12},{1,13},{2,14},{3,15},{4,8},{5,9},{6,10},{7,11},{8,4},{9,5},... | collective-permute-start | bytes 36872 | tf_op jit(solution)/shard_map/ppermute | solution.py:449
  21.3 0.0 collective-permute-start.14
  21.3 0.5 %local2.1.refs_0_ = f32[5,8,16,128]{3,2,1,0:T(8,128)S(1)} custom-call(f32[5,8,16,128]{3,2,1,0:T(8,128)S(1)} %get-tuple-element.60.refs_0_, f32[12,8,16,128]{3,2,1,0:T(8,128)S(1)} %get-tuple-element.36.couple_ref.refs_1_, f32[5,5,8,16,128]{4,3,2,1,0:T(8,128)S(1)} %get-tuple-element.37.refs_2_, f32[5,8,16,128]{3,2,1,0:T(8,128)S(1)} %get-tuple-element.55.refs_3_, ...), custom_call_target="tpu_custom_call" | custom-call | flops 1000000 | bytes 3000000 | tf_op jit(solution)/shard_map/local2/pallas_call | solution.py:426
  21.8 0.6 %collective-permute-done.14.refs_9_ = f32[16,128]{1,0:T(8,128)S(1)} collective-permute-done((f32[16,128]{1,0:T(8,128)S(1)}, f32[16,128]{1,0:T(8,128)S(1)}, u32[]{:S(2)}, u32[]{:S(2)}) %collective-permute-start.14) | collective-permute-done | bytes 8224 | tf_op jit(solution)/shard_map/ppermute | solution.py:449
  22.5 0.6 %collective-permute-done.13.refs_8_ = f32[24,128]{1,0:T(8,128)S(1)} collective-permute-done((f32[24,128]{1,0:T(8,128)S(1)}, f32[24,128]{1,0:T(8,128)S(1)}, u32[]{:S(2)}, u32[]{:S(2)}) %collective-permute-start.13) | collective-permute-done | bytes 12320 | tf_op jit(solution)/shard_map/ppermute | solution.py:449
  23.0 0.0 collective-permute-done.12.refs_7_
  23.0 0.0 collective-permute-done.11.refs_6_
  23.0 1.0 %finish2.1 = f32[5,8,16,128]{3,2,1,0:T(8,128)} custom-call(f32[5,8,16,128]{3,2,1,0:T(8,128)S(1)} %local2.1.refs_0_, f32[2,16,128]{2,1,0:T(8,128)S(1)} %get-tuple-element.44.refs_1_, f32[4,16,128]{2,1,0:T(8,128)S(1)} %get-tuple-element.45.refs_2_, f32[5,5,16,128]{3,2,1,0:T(8,128)S(1)} %get-tuple-element.46.refs_3_, ...), custom_call_target="tpu_custom_call" | custom-call | flops 1000000 | bytes 3000000 | tf_op jit(solution)/shard_map/finish2/pallas_call | solution.py:426
  (2 shorter events, 0.0 us)
Async XLA Ops:
  1.4 8.9 %collective-permute-start.1 = (f32[128,128]{1,0:T(8,128)S(1)}, f32[128,128]{1,0:T(8,128)S(1)}, u32[]{:S(2)}, u32[]{:S(2)}) collective-permute-start(f32[128,128]{1,0:T(8,128)S(1)} %get-tuple-element.42), channel_id=1, source_target_pairs={{0,24},{1,25},{2,26},{3,27},{4,28},{5,29},{6,30},{7,31},{8,16},{9,... | collective-permute-start | bytes 196616 | tf_op jit(solution)/shard_map/ppermute | solution.py:449
  5.3 4.8 %collective-permute-start = (f32[120,128]{1,0:T(8,128)S(1)}, f32[120,128]{1,0:T(8,128)S(1)}, u32[]{:S(2)}, u32[]{:S(2)}) collective-permute-start(f32[120,128]{1,0:T(8,128)S(1)} %get-tuple-element.41), channel_id=1, source_target_pairs={{0,16},{1,17},{2,18},{3,19},{4,20},{5,21},{6,22},{7,23},{8,24},{9,... | collective-permute-start | bytes 184328 | tf_op jit(solution)/shard_map/ppermute | solution.py:449
  6.0 5.4 %collective-permute-start.2 = (f32[88,128]{1,0:T(8,128)S(1)}, f32[88,128]{1,0:T(8,128)S(1)}, u32[]{:S(2)}, u32[]{:S(2)}) collective-permute-start(f32[88,128]{1,0:T(8,128)S(1)} %get-tuple-element.49), channel_id=1, source_target_pairs={{0,1},{1,0},{2,3},{3,2},{4,5},{5,4},{6,7},{7,6},{8,9},{9,8},{10,11... | collective-permute-start | bytes 135176 | tf_op jit(solution)/shard_map/ppermute | solution.py:449
  7.6 3.7 %collective-permute-start.3 = (f32[80,128]{1,0:T(8,128)S(1)}, f32[80,128]{1,0:T(8,128)S(1)}, u32[]{:S(2)}, u32[]{:S(2)}) collective-permute-start(f32[80,128]{1,0:T(8,128)S(1)} %get-tuple-element.50), channel_id=1, source_target_pairs={{0,4},{1,2},{2,1},{3,7},{4,0},{5,6},{6,5},{7,3},{8,12},{9,10},{10,... | collective-permute-start | bytes 122888 | tf_op jit(solution)/shard_map/ppermute | solution.py:449
  7.6 3.7 %collective-permute-start.4 = (f32[72,128]{1,0:T(8,128)S(1)}, f32[72,128]{1,0:T(8,128)S(1)}, u32[]{:S(2)}, u32[]{:S(2)}) collective-permute-start(f32[72,128]{1,0:T(8,128)S(1)} %get-tuple-element.51), channel_id=1, source_target_pairs={{0,12},{1,13},{2,14},{3,15},{4,8},{5,9},{6,10},{7,11},{8,4},{9,5},... | collective-permute-start | bytes 110600 | tf_op jit(solution)/shard_map/ppermute | solution.py:449
  10.1 1.3 %collective-permute-start.5 = (f32[68,128]{1,0:T(8,128)S(1)}, f32[68,128]{1,0:T(8,128)S(1)}, u32[]{:S(2)}, u32[]{:S(2)}) collective-permute-start(f32[68,128]{1,0:T(8,128)S(1)} %relay0.1), channel_id=1, source_target_pairs={{0,4},{1,5},{2,6},{3,7},{4,0},{5,1},{6,2},{7,3},{8,12},{9,13},{10,... | collective-permute-start | bytes 104456 | tf_op jit(solution)/shard_map/ppermute | solution.py:449
  10.2 1.3 %collective-permute-start.6 = (f32[68,128]{1,0:T(8,128)S(1)}, f32[68,128]{1,0:T(8,128)S(1)}, u32[]{:S(2)}, u32[]{:S(2)}) collective-permute-start(f32[68,128]{1,0:T(8,128)S(1)} %relay1.1), channel_id=1, source_target_pairs={{0,4},{1,5},{2,6},{3,7},{4,0},{5,1},{6,2},{7,3},{8,12},{9,13},{10,... | collective-permute-start | bytes 104456 | tf_op jit(solution)/shard_map/ppermute | solution.py:449
  12.1 6.2 %collective-permute-start.7 = (f32[88,128]{1,0:T(8,128)S(1)}, f32[88,128]{1,0:T(8,128)S(1)}, u32[]{:S(2)}, u32[]{:S(2)}) collective-permute-start(f32[88,128]{1,0:T(8,128)S(1)} %get-tuple-element.56), channel_id=1, source_target_pairs={{0,1},{1,0},{2,3},{3,2},{4,5},{5,4},{6,7},{7,6},{8,9},{9,8},{10,11... | collective-permute-start | bytes 135176 | tf_op jit(solution)/shard_map/ppermute | solution.py:449
  15.1 3.1 %collective-permute-start.8 = (f32[80,128]{1,0:T(8,128)S(1)}, f32[80,128]{1,0:T(8,128)S(1)}, u32[]{:S(2)}, u32[]{:S(2)}) collective-permute-start(f32[80,128]{1,0:T(8,128)S(1)} %get-tuple-element.57), channel_id=1, source_target_pairs={{0,4},{1,2},{2,1},{3,7},{4,0},{5,6},{6,5},{7,3},{8,12},{9,10},{10,... | collective-permute-start | bytes 122888 | tf_op jit(solution)/shard_map/ppermute | solution.py:449
  15.1 3.1 %collective-permute-start.9 = (f32[24,128]{1,0:T(8,128)S(1)}, f32[24,128]{1,0:T(8,128)S(1)}, u32[]{:S(2)}, u32[]{:S(2)}) collective-permute-start(f32[24,128]{1,0:T(8,128)S(1)} %get-tuple-element.58), channel_id=1, source_target_pairs={{0,12},{1,13},{2,14},{3,15},{4,8},{5,9},{6,10},{7,11},{8,4},{9,5},... | collective-permute-start | bytes 36872 | tf_op jit(solution)/shard_map/ppermute | solution.py:449
  16.7 1.2 %collective-permute-start.10 = (f32[16,128]{1,0:T(8,128)S(1)}, f32[16,128]{1,0:T(8,128)S(1)}, u32[]{:S(2)}, u32[]{:S(2)}) collective-permute-start(f32[16,128]{1,0:T(8,128)S(1)} %get-tuple-element.59), channel_id=1, source_target_pairs={{0,4},{1,5},{2,6},{3,7},{4,0},{5,1},{6,2},{7,3},{8,12},{9,13},{10,... | collective-permute-start | bytes 24584 | tf_op jit(solution)/shard_map/ppermute | solution.py:449
  18.7 4.3 %collective-permute-start.11 = (f32[88,128]{1,0:T(8,128)S(1)}, f32[88,128]{1,0:T(8,128)S(1)}, u32[]{:S(2)}, u32[]{:S(2)}) collective-permute-start(f32[88,128]{1,0:T(8,128)S(1)} %get-tuple-element.61), channel_id=1, source_target_pairs={{0,1},{1,0},{2,3},{3,2},{4,5},{5,4},{6,7},{7,6},{8,9},{9,8},{10,11... | collective-permute-start | bytes 135176 | tf_op jit(solution)/shard_map/ppermute | solution.py:449
  19.9 3.1 %collective-permute-start.12 = (f32[80,128]{1,0:T(8,128)S(1)}, f32[80,128]{1,0:T(8,128)S(1)}, u32[]{:S(2)}, u32[]{:S(2)}) collective-permute-start(f32[80,128]{1,0:T(8,128)S(1)} %get-tuple-element.62), channel_id=1, source_target_pairs={{0,4},{1,2},{2,1},{3,7},{4,0},{5,6},{6,5},{7,3},{8,12},{9,10},{10,... | collective-permute-start | bytes 122888 | tf_op jit(solution)/shard_map/ppermute | solution.py:449
  19.9 3.1 %collective-permute-start.13 = (f32[24,128]{1,0:T(8,128)S(1)}, f32[24,128]{1,0:T(8,128)S(1)}, u32[]{:S(2)}, u32[]{:S(2)}) collective-permute-start(f32[24,128]{1,0:T(8,128)S(1)} %get-tuple-element.63), channel_id=1, source_target_pairs={{0,12},{1,13},{2,14},{3,15},{4,8},{5,9},{6,10},{7,11},{8,4},{9,5},... | collective-permute-start | bytes 36872 | tf_op jit(solution)/shard_map/ppermute | solution.py:449
  21.3 1.2 %collective-permute-start.14 = (f32[16,128]{1,0:T(8,128)S(1)}, f32[16,128]{1,0:T(8,128)S(1)}, u32[]{:S(2)}, u32[]{:S(2)}) collective-permute-start(f32[16,128]{1,0:T(8,128)S(1)} %get-tuple-element.64), channel_id=1, source_target_pairs={{0,4},{1,5},{2,6},{3,7},{4,0},{5,1},{6,2},{7,3},{8,12},{9,13},{10,... | collective-permute-start | bytes 24584 | tf_op jit(solution)/shard_map/ppermute | solution.py:449

commit v8 on v7

--- a/solution.py
+++ b/solution.py
@@ -128,10 +128,11 @@
     place_weights(targets_ref, counts_ref, weights_ref, placed_ref)
     for s, copy in enumerate(wide):
         copy.wait()
-        edge_matrices(s, jac_ref, inv_ref, *edge_refs)
-
-
-def edge_matrices(s, jac_ref, inv_ref, cols_ref, low_ref, high_ref):
+        if s < edge_refs[0].shape[0]:
+            edge_matrices(s, s, jac_ref, inv_ref, *edge_refs)
+
+
+def edge_matrices(s, at, jac_ref, inv_ref, cols_ref, low_ref, high_ref):
     nv, na = jac_ref.shape[1:3]
     sub, lane = iotas()
     for b in range(nv):
@@ -142,10 +143,10 @@
                 gather.cols("cols", half, a, m)
                 gather.rows("high" if half else "low", half, a, m)
         for half in range(2):
-            cols_ref[s, b, half_rows(half), :] = gather.got["cols", half]
+            cols_ref[at, b, half_rows(half), :] = gather.got["cols", half]
         for q in range(na // 4):
-            low_ref[s, b, half_rows(q), :] = gather.got["low", q]
-            high_ref[s, b, half_rows(q), :] = gather.got["high", q]
+            low_ref[at, b, half_rows(q), :] = gather.got["low", q]
+            high_ref[at, b, half_rows(q), :] = gather.got["high", q]
 
 
 def load_kernel(adjoint_ref, donors_in, couple_in, src_in, *refs):
@@ -297,7 +298,10 @@
     nv, na = lam_ref.shape[:2]
     sub, lane = iotas()
     if tiles:
-        placed_ref, *tile_refs, base_ref, sum_ref = refs[5:]
+        placed_ref, *tile_refs, base_ref, sum_ref = refs[5:-3]
+        rest = refs[-3:]
+        for s in range(nv - rest[0].shape[0], nv):
+            edge_matrices(s, s - nv + rest[0].shape[0], jac_ref, inv_ref, *rest)
         me = lax.axis_index("circ")
         sources = [(ref, 0, donor_at(me - 2 * n)) for n, ref in enumerate(tile_refs)]
     else:
@@ -369,18 +373,20 @@
 
 
 def finish_kernel(routes, last, *refs):
-    base_ref, cols_ref, rows_ref, edge_cols, edge_low, edge_high, ahead_ref, back_ref, across_ref = refs[:9]
+    base_ref, cols_ref, rows_ref, *edges = refs[:9]
+    ahead_ref, back_ref, across_ref, *refs = refs[9:]
+    pick = lambda s: (edges[:3], s) if s < edges[0].shape[0] else (edges[3:], s - edges[0].shape[0])
     nv, na = base_ref.shape[:2]
     sub, lane = iotas()
     if routes:
-        rhs_ref, inv_ref, placed_ref, *relayed = refs[9 : 12 + routes]
-        out_ref, sum_ref, *rest = refs[12 + routes :]
+        rhs_ref, inv_ref, placed_ref, *relayed = refs[: 3 + routes]
+        out_ref, sum_ref, *rest = refs[3 + routes :]
         share = shares(routes)
         mate_at = lambda half: relayed[SUB * half // share][SUB * half % share : SUB * half % share + SUB, :]
         me = lax.axis_index("circ")
         sources = [(ref, share, donor_at(me + 1 - 2 * (me % 2) - 2 * n)) for n, ref in enumerate(relayed)]
     else:
-        mate_ref, out_ref, *rest = refs[9:]
+        mate_ref, out_ref, *rest = refs
         mate_at = lambda half: mate_ref[half_rows(half), :]
     if last:
         result_ref, out_ref, sems = out_ref, *rest
@@ -389,12 +395,12 @@
     packer = None if last else Packer(na, nv)
     for s in range(nv):
         turned = []
-        for kind, edge_ref in enumerate((edge_cols, edge_low, edge_high)):
+        for kind, edge_ref in enumerate(pick(s)[0]):
             turned.append([])
             for q in range(2 if kind == 0 else na // 4):
-                total = edge_ref[s, 0, half_rows(q), :] * sums[0][kind][q]
+                total = edge_ref[pick(s)[1], 0, half_rows(q), :] * sums[0][kind][q]
                 for b in range(1, nv):
-                    total = total + edge_ref[s, b, half_rows(q), :] * sums[b][kind][q]
+                    total = total + edge_ref[pick(s)[1], b, half_rows(q), :] * sums[b][kind][q]
                 turned[-1].append(total)
         for a in range(na):
             for half in range(2):
@@ -455,9 +461,10 @@
         sides = 2 * nv * na
         edges = lambda across: [vmem(sides + SUB, nc), vmem(sides, nc), vmem(across, nc), vmem(nr, nc)]
         block = vmem(nv, na, nr, nc)
+        edge_forms = lambda n: [vmem(n, nv, nr, nc)] + [vmem(n, nv, 2 * na, nc)] * 2
         lam, cpl, rhs, *tiles = call(
             load_kernel, "load",
-            [block, vmem(12, na, nr, nc), block] + [vmem(4 * slots * nv + SUB * n, nc) for n in range(count)],
+            [block, vmem(12, na, nr, nc), block] + [vmem(4 * slots * nv + SUB * (count - 1 - n), nc) for n in range(count)],
             [*map(far, (adjoint[0], donor_row[0], couple[0], source[0]))], [outside] * 4,
             [pltpu.SMEM(donor_row.shape[1:], jnp.int32), pltpu.SemaphoreType.DMA((4,))],
         )
@@ -473,7 +480,7 @@
                 jac, placed, inv, edge_coefs, row_coefs, *matrices = call(
                     fetch_kernel, "fetch",
                     [vmem(nv, nv, na, nr, nc), vmem(donors, slots, nr, nc), vmem(na, nr, nc),
-                     vmem(2, nr, nc), vmem(4, 2 * na, nc), vmem(nv, nv, nr, nc)] + [vmem(nv, nv, 2 * na, nc)] * 2,
+                     vmem(2, nr, nc), vmem(4, 2 * na, nc), *edge_forms(nv // 2)],
                     [cpl, *map(far, (jacobian[0], target_row[0], tile_count[0], weights.reshape(-1, nc)))],
                     [inside] + [outside] * 4,
                     [pltpu.SMEM(target_row.shape[1:], jnp.int32), pltpu.SMEM(tile_count.shape[1:], jnp.int32),
@@ -485,11 +492,12 @@
                     for n, x in enumerate(tiles)
                 ]
                 relayed = [sent(x, route["mate"]) for x in relayed]
-                base, rhs = call(
-                    functools.partial(local_kernel, True), "local0", [block] * 2, [lam, cpl, jac, rhs, inv, placed, *tiles]
+                base, rhs, *more = call(
+                    functools.partial(local_kernel, True), "local0", [block] * 2 + edge_forms(nv - nv // 2), [lam, cpl, jac, rhs, inv, placed, *tiles]
                 )
+                matrices += more
                 lam, rhs, ahead, back, cross, cols = call(
-                    functools.partial(finish_kernel, count, False), "finish0", [block] * 2 + edges(nr + SUB),
+                    functools.partial(finish_kernel, count, False), "finish0", [block] * 2 + edges(nr),
                     [base, edge_coefs, row_coefs, *matrices, ahead, back, across, rhs, inv, placed, *relayed],
                 )
                 continue
@@ -497,7 +505,7 @@
             base = call(
                 functools.partial(local_kernel, False), f"local{sweep}", [block], [lam, cpl, jac, rhs, inv]
             )[0]
-            scratch, spaces, outs = [], None, [block] + edges(nr + SUB)
+            scratch, spaces, outs = [], None, [block] + edges(nr)
             if last:
                 outs, spaces = [jax.ShapeDtypeStruct((nv, na, nr, nc), jnp.float32)], [outside]
                 scratch = [pltpu.VMEM((nv, na, nr, nc), jnp.float32), pltpu.SemaphoreType.DMA((nv,))]

time: 24.3 us -> 24.4 us (level)
    ppermute x15, starting transfers between devices: 14.6 us -> 14.8 us  [sent(): return lax.ppermute(x, AXES, pairs)]
  transfers between devices with their start and end apart: 15 -> 15, of which waited for: 5 -> 2; matrix products, arithmetic and copies ran while one was open for 0% -> 0% of each run, Pallas kernels for 15% -> 15%
where the time goes in v8:
time: 24.4 us; the launch traced here: 24.1 us
  starting transfers between devices  14.8 us (61%)
  Pallas kernels  6.81 us (28%)
  waiting for transfers between devices  2.3 us (9%)
    ppermute x15, starting transfers between devices, sent(): return lax.ppermute(x, AXES, pairs)  14.8 us
    pallas_call x11, Pallas kernels, call(): pl.pallas_call(kernel, out_shape=outs, in_specs=[vmem] * len(args) if spe...  6.81 us
    ppermute x15, waiting for transfers between devices, sent(): return lax.ppermute(x, AXES, pairs)  2.3 us
  transfers between devices with their start and end apart: 15, of which 2 were waited for; matrix products, arithmetic and copies ran while one was open for 0% of the time, Pallas kernels for 15%

profile of v8, /device:TPU:0, one launch (start us, length us, event | category | flops | bytes accessed | tf_op | source)
XLA Modules:
  0.0 24.1 jit_solution(17956604923315966262)
XLA Ops:
  0.0 1.3 %load.1 = (f32[5,8,16,128]{3,2,1,0:T(8,128)S(1)}, f32[12,8,16,128]{3,2,1,0:T(8,128)S(1)}, f32[5,8,16,128]{3,2,1,0:T(8,128)S(1)}, f32[128,128]{1,0:T(8,128)S(1)}, f32[120,128]{1,0:T(8,128)S(1)}) custom-call(f32[5,8,16,128]{3,2,1,0:T(8,128)} %bitcast.11, s32[4,4,6]{2,1,0:T(4,128)} %bitcast.14, f32[12,8,16,128]{3,2,1,0:T(8,128)} %bitcast.10, ...), custom_call_target="tpu_custom_call" | custom-call | flops 1000000 | bytes 3000000 | tf_op jit(solution)/shard_map/load/pallas_call | solution.py:432
  1.4 3.0 %collective-permute-start = (f32[128,128]{1,0:T(8,128)S(1)}, f32[128,128]{1,0:T(8,128)S(1)}, u32[]{:S(2)}, u32[]{:S(2)}) collective-permute-start(f32[128,128]{1,0:T(8,128)S(1)} %get-tuple-element.44), channel_id=1, source_target_pairs={{0,16},{1,17},{2,18},{3,19},{4,20},{5,21},{6,22},{7,23},{8,24},{9,... | collective-permute-start | bytes 196616 | tf_op jit(solution)/shard_map/ppermute | solution.py:455
  4.4 1.4 %collective-permute-start.1 = (f32[120,128]{1,0:T(8,128)S(1)}, f32[120,128]{1,0:T(8,128)S(1)}, u32[]{:S(2)}, u32[]{:S(2)}) collective-permute-start(f32[120,128]{1,0:T(8,128)S(1)} %get-tuple-element.45), channel_id=1, source_target_pairs={{0,24},{1,25},{2,26},{3,27},{4,28},{5,29},{6,30},{7,31},{8,16},{9,... | collective-permute-start | bytes 184328 | tf_op jit(solution)/shard_map/ppermute | solution.py:455
  5.8 0.1 pack.1
  6.0 1.6 %collective-permute-start.2 = (f32[88,128]{1,0:T(8,128)S(1)}, f32[88,128]{1,0:T(8,128)S(1)}, u32[]{:S(2)}, u32[]{:S(2)}) collective-permute-start(f32[88,128]{1,0:T(8,128)S(1)} %get-tuple-element.55), channel_id=1, source_target_pairs={{0,1},{1,0},{2,3},{3,2},{4,5},{5,4},{6,7},{7,6},{8,9},{9,8},{10,11... | collective-permute-start | bytes 135176 | tf_op jit(solution)/shard_map/ppermute | solution.py:455
  7.6 0.0 collective-permute-start.3
  7.6 0.6 %collective-permute-start.4 = (f32[72,128]{1,0:T(8,128)S(1)}, f32[72,128]{1,0:T(8,128)S(1)}, u32[]{:S(2)}, u32[]{:S(2)}) collective-permute-start(f32[72,128]{1,0:T(8,128)S(1)} %get-tuple-element.57), channel_id=1, source_target_pairs={{0,12},{1,13},{2,14},{3,15},{4,8},{5,9},{6,10},{7,11},{8,4},{9,5},... | collective-permute-start | bytes 110600 | tf_op jit(solution)/shard_map/ppermute | solution.py:455
  8.3 1.5 %fetch.1 = (f32[5,5,8,16,128]{4,3,2,1,0:T(8,128)S(1)}, f32[4,6,16,128]{3,2,1,0:T(8,128)S(1)}, f32[8,16,128]{2,1,0:T(8,128)S(1)}, f32[2,16,128]{2,1,0:T(8,128)S(1...) custom-call(f32[12,8,16,128]{3,2,1,0:T(8,128)S(1)} %get-tuple-elemen, ...), custom_call_target="tpu_custom_call" | custom-call | flops 1000000 | bytes 3000000 | tf_op jit(solution)/shard_map/fetch/pallas_call | solution.py:432
  9.7 0.0 collective-permute-done.1.refs_7_.tile_ref
  9.8 0.1 collective-permute-start.6
  9.8 0.0 collective-permute-done.refs_6_.tile_ref
  9.9 0.5 %collective-permute-start.5 = (f32[68,128]{1,0:T(8,128)S(1)}, f32[68,128]{1,0:T(8,128)S(1)}, u32[]{:S(2)}, u32[]{:S(2)}) collective-permute-start(f32[68,128]{1,0:T(8,128)S(1)} %relay0.1), channel_id=1, source_target_pairs={{0,4},{1,5},{2,6},{3,7},{4,0},{5,1},{6,2},{7,3},{8,12},{9,13},{10,... | collective-permute-start | bytes 104456 | tf_op jit(solution)/shard_map/ppermute | solution.py:455
  10.3 0.9 %local0.1 = (f32[5,8,16,128]{3,2,1,0:T(8,128)S(1)}, f32[5,8,16,128]{3,2,1,0:T(8,128)S(1)}, f32[3,5,16,128]{3,2,1,0:T(8,128)S(1)}, f32[3,5,16,128]{3,2,1,0:T(8,128)S(1)}, f32[3,5,16,128]{3,2,1,0:T(8,128)S(1)}) custom-call(f32[5,8,16,128]{3,2,1,0:T(8,128)S(1)} %get-tuple-element.38.refs_0_.lam_ref, ...), custom_call_target="tpu_custom_call" | custom-call | flops 1000000 | bytes 3000000 | tf_op jit(solution)/shard_map/local0/pallas_call | solution.py:432
  11.2 0.0 collective-permute-done.4.refs_11_
  11.2 0.0 collective-permute-done.3.refs_10_
  11.2 0.0 collective-permute-done.2.refs_9_
  11.2 0.0 collective-permute-done.6.refs_16_
  11.3 0.0 collective-permute-done.5.refs_15_
  11.3 0.5 %finish0.1 = (f32[5,8,16,128]{3,2,1,0:T(8,128)S(1)}, f32[5,8,16,128]{3,2,1,0:T(8,128)S(1)}, f32[88,128]{1,0:T(8,128)S(1)}, f32[80,128]{1,0:T(8,128)S(1)}, f32[16,128]{1,0:T(8,128)S(1)}, /*index=5*/f32[16,128]{1,0:T(8,128)S(1)}) custom-call(f32[5,8,16,128]{3,2,1,0:T(8,128)S(1)} %get-tuple-element.46.refs_0_, f32[2,16,128]{2,1,0:T(8,128)S(1)} %get-tuple-element.47.refs_1_, ...), custom_call_target="tpu_custom_call" | custom-call | flops 1000000 | bytes 3000000 | tf_op jit(solution)/shard_map/finish0/pallas_call | solution.py:432
  11.8 3.0 %collective-permute-start.7 = (f32[88,128]{1,0:T(8,128)S(1)}, f32[88,128]{1,0:T(8,128)S(1)}, u32[]{:S(2)}, u32[]{:S(2)}) collective-permute-start(f32[88,128]{1,0:T(8,128)S(1)} %get-tuple-element.62), channel_id=1, source_target_pairs={{0,1},{1,0},{2,3},{3,2},{4,5},{5,4},{6,7},{7,6},{8,9},{9,8},{10,11... | collective-permute-start | bytes 135176 | tf_op jit(solution)/shard_map/ppermute | solution.py:455
  14.7 0.0 collective-permute-start.8
  14.7 0.5 %collective-permute-start.10 = (f32[16,128]{1,0:T(8,128)S(1)}, f32[16,128]{1,0:T(8,128)S(1)}, u32[]{:S(2)}, u32[]{:S(2)}) collective-permute-start(f32[16,128]{1,0:T(8,128)S(1)} %get-tuple-element.65), channel_id=1, source_target_pairs={{0,4},{1,5},{2,6},{3,7},{4,0},{5,1},{6,2},{7,3},{8,12},{9,13},{10,... | collective-permute-start | bytes 24584 | tf_op jit(solution)/shard_map/ppermute | solution.py:455
  15.2 1.1 %collective-permute-start.9 = (f32[16,128]{1,0:T(8,128)S(1)}, f32[16,128]{1,0:T(8,128)S(1)}, u32[]{:S(2)}, u32[]{:S(2)}) collective-permute-start(f32[16,128]{1,0:T(8,128)S(1)} %get-tuple-element.64), channel_id=1, source_target_pairs={{0,12},{1,13},{2,14},{3,15},{4,8},{5,9},{6,10},{7,11},{8,4},{9,5},... | collective-permute-start | bytes 24584 | tf_op jit(solution)/shard_map/ppermute | solution.py:455
  16.3 0.5 %local1.1.refs_0_ = f32[5,8,16,128]{3,2,1,0:T(8,128)S(1)} custom-call(f32[5,8,16,128]{3,2,1,0:T(8,128)S(1)} %get-tuple-element.60.refs_0_, f32[12,8,16,128]{3,2,1,0:T(8,128)S(1)} %get-tuple-element.39.couple_ref.refs_1_, f32[5,5,8,16,128]{4,3,2,1,0:T(8,128)S(1)} %get-tuple-element.40.refs_2_, f32[5,8,16,128]{3,2,1,0:T(8,128)S(1)} %get-tuple-element.61.refs_3_, ...), custom_call_target="tpu_custom_call" | custom-call | flops 1000000 | bytes 3000000 | tf_op jit(solution)/shard_map/local1/pallas_call | solution.py:432
  16.9 0.0 collective-permute-done.10.refs_12_
  16.9 1.4 %collective-permute-done.9.refs_11_ = f32[16,128]{1,0:T(8,128)S(1)} collective-permute-done((f32[16,128]{1,0:T(8,128)S(1)}, f32[16,128]{1,0:T(8,128)S(1)}, u32[]{:S(2)}, u32[]{:S(2)}) %collective-permute-start.9) | collective-permute-done | bytes 8224 | tf_op jit(solution)/shard_map/ppermute | solution.py:455
  18.3 0.0 collective-permute-done.8.refs_10_
  18.3 0.0 collective-permute-done.7.refs_9_
  18.3 0.4 %finish1.1 = (f32[5,8,16,128]{3,2,1,0:T(8,128)S(1)}, f32[88,128]{1,0:T(8,128)S(1)}, f32[80,128]{1,0:T(8,128)S(1)}, f32[16,128]{1,0:T(8,128)S(1)}, f32[16,128]{1,0:T(8,128)S(1)}) custom-call(f32[5,8,16,128]{3,2,1,0:T(8,128)S(1)} %local1.1.refs_0_, f32[2,16,128]{2,1,0:T(8,128)S(1)} %get-tuple-element.47.refs_1_, f32[4,16,128]{2,1,0:T(8,128)S(1)} %get-tuple-element.48.refs_2_, ...), custom_call_target="tpu_custom_call" | custom-call | flops 1000000 | bytes 3000000 | tf_op jit(solution)/shard_map/finish1/pallas_call | solution.py:432
  18.8 1.0 %collective-permute-start.11 = (f32[88,128]{1,0:T(8,128)S(1)}, f32[88,128]{1,0:T(8,128)S(1)}, u32[]{:S(2)}, u32[]{:S(2)}) collective-permute-start(f32[88,128]{1,0:T(8,128)S(1)} %get-tuple-element.67), channel_id=1, source_target_pairs={{0,1},{1,0},{2,3},{3,2},{4,5},{5,4},{6,7},{7,6},{8,9},{9,8},{10,11... | collective-permute-start | bytes 135176 | tf_op jit(solution)/shard_map/ppermute | solution.py:455
  19.8 0.2 collective-permute-start.12
  20.0 1.5 %collective-permute-start.13 = (f32[16,128]{1,0:T(8,128)S(1)}, f32[16,128]{1,0:T(8,128)S(1)}, u32[]{:S(2)}, u32[]{:S(2)}) collective-permute-start(f32[16,128]{1,0:T(8,128)S(1)} %get-tuple-element.69), channel_id=1, source_target_pairs={{0,12},{1,13},{2,14},{3,15},{4,8},{5,9},{6,10},{7,11},{8,4},{9,5},... | collective-permute-start | bytes 24584 | tf_op jit(solution)/shard_map/ppermute | solution.py:455
  21.5 0.2 collective-permute-start.14
  21.7 0.5 %local2.1.refs_0_ = f32[5,8,16,128]{3,2,1,0:T(8,128)S(1)} custom-call(f32[5,8,16,128]{3,2,1,0:T(8,128)S(1)} %get-tuple-element.66.refs_0_, f32[12,8,16,128]{3,2,1,0:T(8,128)S(1)} %get-tuple-element.39.couple_ref.refs_1_, f32[5,5,8,16,128]{4,3,2,1,0:T(8,128)S(1)} %get-tuple-element.40.refs_2_, f32[5,8,16,128]{3,2,1,0:T(8,128)S(1)} %get-tuple-element.61.refs_3_, ...), custom_call_target="tpu_custom_call" | custom-call | flops 1000000 | bytes 3000000 | tf_op jit(solution)/shard_map/local2/pallas_call | solution.py:432
  22.2 0.8 %collective-permute-done.13.refs_11_ = f32[16,128]{1,0:T(8,128)S(1)} collective-permute-done((f32[16,128]{1,0:T(8,128)S(1)}, f32[16,128]{1,0:T(8,128)S(1)}, u32[]{:S(2)}, u32[]{:S(2)}) %collective-permute-start.13) | collective-permute-done | bytes 8224 | tf_op jit(solution)/shard_map/ppermute | solution.py:455
  23.1 0.0 collective-permute-done.14.refs_12_
  23.1 0.0 collective-permute-done.12.refs_10_
  23.1 0.0 collective-permute-done.11.refs_9_
  23.1 1.0 %finish2.1 = f32[5,8,16,128]{3,2,1,0:T(8,128)} custom-call(f32[5,8,16,128]{3,2,1,0:T(8,128)S(1)} %local2.1.refs_0_, f32[2,16,128]{2,1,0:T(8,128)S(1)} %get-tuple-element.47.refs_1_, f32[4,16,128]{2,1,0:T(8,128)S(1)} %get-tuple-element.48.refs_2_, f32[2,5,16,128]{3,2,1,0:T(8,128)S(1)} %get-tuple-element.49.refs_3_, ...), custom_call_target="tpu_custom_call" | custom-call | flops 1000000 | bytes 3000000 | tf_op jit(solution)/shard_map/finish2/pallas_call | solution.py:432
  (2 shorter events, 0.0 us)
Async XLA Ops:
  1.4 8.5 %collective-permute-start = (f32[128,128]{1,0:T(8,128)S(1)}, f32[128,128]{1,0:T(8,128)S(1)}, u32[]{:S(2)}, u32[]{:S(2)}) collective-permute-start(f32[128,128]{1,0:T(8,128)S(1)} %get-tuple-element.44), channel_id=1, source_target_pairs={{0,16},{1,17},{2,18},{3,19},{4,20},{5,21},{6,22},{7,23},{8,24},{9,... | collective-permute-start | bytes 196616 | tf_op jit(solution)/shard_map/ppermute | solution.py:455
  4.4 5.4 %collective-permute-start.1 = (f32[120,128]{1,0:T(8,128)S(1)}, f32[120,128]{1,0:T(8,128)S(1)}, u32[]{:S(2)}, u32[]{:S(2)}) collective-permute-start(f32[120,128]{1,0:T(8,128)S(1)} %get-tuple-element.45), channel_id=1, source_target_pairs={{0,24},{1,25},{2,26},{3,27},{4,28},{5,29},{6,30},{7,31},{8,16},{9,... | collective-permute-start | bytes 184328 | tf_op jit(solution)/shard_map/ppermute | solution.py:455
  6.0 5.3 %collective-permute-start.2 = (f32[88,128]{1,0:T(8,128)S(1)}, f32[88,128]{1,0:T(8,128)S(1)}, u32[]{:S(2)}, u32[]{:S(2)}) collective-permute-start(f32[88,128]{1,0:T(8,128)S(1)} %get-tuple-element.55), channel_id=1, source_target_pairs={{0,1},{1,0},{2,3},{3,2},{4,5},{5,4},{6,7},{7,6},{8,9},{9,8},{10,11... | collective-permute-start | bytes 135176 | tf_op jit(solution)/shard_map/ppermute | solution.py:455
  7.6 3.6 %collective-permute-start.3 = (f32[80,128]{1,0:T(8,128)S(1)}, f32[80,128]{1,0:T(8,128)S(1)}, u32[]{:S(2)}, u32[]{:S(2)}) collective-permute-start(f32[80,128]{1,0:T(8,128)S(1)} %get-tuple-element.56), channel_id=1, source_target_pairs={{0,4},{1,2},{2,1},{3,7},{4,0},{5,6},{6,5},{7,3},{8,12},{9,10},{10,... | collective-permute-start | bytes 122888 | tf_op jit(solution)/shard_map/ppermute | solution.py:455
  7.6 3.6 %collective-permute-start.4 = (f32[72,128]{1,0:T(8,128)S(1)}, f32[72,128]{1,0:T(8,128)S(1)}, u32[]{:S(2)}, u32[]{:S(2)}) collective-permute-start(f32[72,128]{1,0:T(8,128)S(1)} %get-tuple-element.57), channel_id=1, source_target_pairs={{0,12},{1,13},{2,14},{3,15},{4,8},{5,9},{6,10},{7,11},{8,4},{9,5},... | collective-permute-start | bytes 110600 | tf_op jit(solution)/shard_map/ppermute | solution.py:455
  9.8 1.5 %collective-permute-start.6 = (f32[68,128]{1,0:T(8,128)S(1)}, f32[68,128]{1,0:T(8,128)S(1)}, u32[]{:S(2)}, u32[]{:S(2)}) collective-permute-start(f32[68,128]{1,0:T(8,128)S(1)} %relay1.1), channel_id=1, source_target_pairs={{0,4},{1,5},{2,6},{3,7},{4,0},{5,1},{6,2},{7,3},{8,12},{9,13},{10,... | collective-permute-start | bytes 104456 | tf_op jit(solution)/shard_map/ppermute | solution.py:455
  9.9 1.4 %collective-permute-start.5 = (f32[68,128]{1,0:T(8,128)S(1)}, f32[68,128]{1,0:T(8,128)S(1)}, u32[]{:S(2)}, u32[]{:S(2)}) collective-permute-start(f32[68,128]{1,0:T(8,128)S(1)} %relay0.1), channel_id=1, source_target_pairs={{0,4},{1,5},{2,6},{3,7},{4,0},{5,1},{6,2},{7,3},{8,12},{9,13},{10,... | collective-permute-start | bytes 104456 | tf_op jit(solution)/shard_map/ppermute | solution.py:455
  11.8 6.6 %collective-permute-start.7 = (f32[88,128]{1,0:T(8,128)S(1)}, f32[88,128]{1,0:T(8,128)S(1)}, u32[]{:S(2)}, u32[]{:S(2)}) collective-permute-start(f32[88,128]{1,0:T(8,128)S(1)} %get-tuple-element.62), channel_id=1, source_target_pairs={{0,1},{1,0},{2,3},{3,2},{4,5},{5,4},{6,7},{7,6},{8,9},{9,8},{10,11... | collective-permute-start | bytes 135176 | tf_op jit(solution)/shard_map/ppermute | solution.py:455
  14.7 3.6 %collective-permute-start.8 = (f32[80,128]{1,0:T(8,128)S(1)}, f32[80,128]{1,0:T(8,128)S(1)}, u32[]{:S(2)}, u32[]{:S(2)}) collective-permute-start(f32[80,128]{1,0:T(8,128)S(1)} %get-tuple-element.63), channel_id=1, source_target_pairs={{0,4},{1,2},{2,1},{3,7},{4,0},{5,6},{6,5},{7,3},{8,12},{9,10},{10,... | collective-permute-start | bytes 122888 | tf_op jit(solution)/shard_map/ppermute | solution.py:455
  14.7 2.2 %collective-permute-start.10 = (f32[16,128]{1,0:T(8,128)S(1)}, f32[16,128]{1,0:T(8,128)S(1)}, u32[]{:S(2)}, u32[]{:S(2)}) collective-permute-start(f32[16,128]{1,0:T(8,128)S(1)} %get-tuple-element.65), channel_id=1, source_target_pairs={{0,4},{1,5},{2,6},{3,7},{4,0},{5,1},{6,2},{7,3},{8,12},{9,13},{10,... | collective-permute-start | bytes 24584 | tf_op jit(solution)/shard_map/ppermute | solution.py:455
  15.2 3.1 %collective-permute-start.9 = (f32[16,128]{1,0:T(8,128)S(1)}, f32[16,128]{1,0:T(8,128)S(1)}, u32[]{:S(2)}, u32[]{:S(2)}) collective-permute-start(f32[16,128]{1,0:T(8,128)S(1)} %get-tuple-element.64), channel_id=1, source_target_pairs={{0,12},{1,13},{2,14},{3,15},{4,8},{5,9},{6,10},{7,11},{8,4},{9,5},... | collective-permute-start | bytes 24584 | tf_op jit(solution)/shard_map/ppermute | solution.py:455
  18.8 4.3 %collective-permute-start.11 = (f32[88,128]{1,0:T(8,128)S(1)}, f32[88,128]{1,0:T(8,128)S(1)}, u32[]{:S(2)}, u32[]{:S(2)}) collective-permute-start(f32[88,128]{1,0:T(8,128)S(1)} %get-tuple-element.67), channel_id=1, source_target_pairs={{0,1},{1,0},{2,3},{3,2},{4,5},{5,4},{6,7},{7,6},{8,9},{9,8},{10,11... | collective-permute-start | bytes 135176 | tf_op jit(solution)/shard_map/ppermute | solution.py:455
  19.8 3.3 %collective-permute-start.12 = (f32[80,128]{1,0:T(8,128)S(1)}, f32[80,128]{1,0:T(8,128)S(1)}, u32[]{:S(2)}, u32[]{:S(2)}) collective-permute-start(f32[80,128]{1,0:T(8,128)S(1)} %get-tuple-element.68), channel_id=1, source_target_pairs={{0,4},{1,2},{2,1},{3,7},{4,0},{5,6},{6,5},{7,3},{8,12},{9,10},{10,... | collective-permute-start | bytes 122888 | tf_op jit(solution)/shard_map/ppermute | solution.py:455
  20.0 3.1 %collective-permute-start.13 = (f32[16,128]{1,0:T(8,128)S(1)}, f32[16,128]{1,0:T(8,128)S(1)}, u32[]{:S(2)}, u32[]{:S(2)}) collective-permute-start(f32[16,128]{1,0:T(8,128)S(1)} %get-tuple-element.69), channel_id=1, source_target_pairs={{0,12},{1,13},{2,14},{3,15},{4,8},{5,9},{6,10},{7,11},{8,4},{9,5},... | collective-permute-start | bytes 24584 | tf_op jit(solution)/shard_map/ppermute | solution.py:455
  21.5 1.6 %collective-permute-start.14 = (f32[16,128]{1,0:T(8,128)S(1)}, f32[16,128]{1,0:T(8,128)S(1)}, u32[]{:S(2)}, u32[]{:S(2)}) collective-permute-start(f32[16,128]{1,0:T(8,128)S(1)} %get-tuple-element.70), channel_id=1, source_target_pairs={{0,4},{1,5},{2,6},{3,7},{4,0},{5,1},{6,2},{7,3},{8,12},{9,13},{10,... | collective-permute-start | bytes 24584 | tf_op jit(solution)/shard_map/ppermute | solution.py:455
